TPU v7x, 32 devices: a whole 2x2x4 slice. The times are simulated.
32 devices in a mesh: section: 2 (over core), dp: 16 (over z, y, x).
Axes of the slice: x: 2, y: 2, z: 4, core: 2. Of those that a mesh axis runs over, the one named last changes fastest.
Arguments:
- features: bfloat16 [50176, 1024], P('dp')
- image_group: int32 [256], replicated, may hold values from 0 to 511, as said below
- token_ids: int32 [8192], P('dp'), may hold values from 0 to 31999
- text_lengths: int32 [16, 32], P('dp'), may hold values from 1 to 32, 512 in all within a row
- cotangent: float32 [8192, 768], P('dp'), may hold values from -6 to 6
- table_master: float32 [32000, 768], P(('section', 'dp')), may hold values from -6 to 6
- table_momentum: float32 [32000, 768], P(('section', 'dp')), may hold values from -1.5 to 1.5
- table_average: float32 [32000, 768], P(('section', 'dp')), may hold values from -6 to 6
- block_master: float32 [768, 9216], P(('section', 'dp'))
- block_momentum: float32 [768, 9216], P(('section', 'dp')), may hold values from -28 to 28
- block_average: float32 [768, 9216], P(('section', 'dp')), may hold values from -0.21875 to 0.21875
- project_master: float32 [4096, 768], P(('section', 'dp')), may hold values from -0.109375 to 0.109375
- project_momentum: float32 [4096, 768], P(('section', 'dp')), may hold values from -28 to 28
- project_average: float32 [4096, 768], P(('section', 'dp')), may hold values from -0.109375 to 0.109375
- vector_master: float32 [11264], P(('section', 'dp'))
- vector_momentum: float32 [11264], P(('section', 'dp')), may hold values from -28 to 28
- vector_average: float32 [11264], P(('section', 'dp')), may hold values from 0.5 to 1.5
Outputs:
- block_out: bfloat16 [8192, 768], P('dp', 'section')
- feature_grad: float32 [50176, 1024], P('dp', 'section')
- table_grad: float32 [32000, 768], P(('section', 'dp'))
- table_momentum_new: float32 [32000, 768], P(('section', 'dp'))
- table_average_new: float32 [32000, 768], P(('section', 'dp'))
- table_master_new: float32 [32000, 768], P(('section', 'dp'))
- table_copy: bfloat16 [32000, 768], P(('section', 'dp'))
- block_grad: float32 [768, 9216], P(('section', 'dp'))
- block_momentum_new: float32 [768, 9216], P(('section', 'dp'))
- block_average_new: float32 [768, 9216], P(('section', 'dp'))
- block_master_new: float32 [768, 9216], P(('section', 'dp'))
- block_copy: bfloat16 [768, 9216], P(('section', 'dp'))
- project_grad: float32 [4096, 768], P(('section', 'dp'))
- project_momentum_new: float32 [4096, 768], P(('section', 'dp'))
- project_average_new: float32 [4096, 768], P(('section', 'dp'))
- project_master_new: float32 [4096, 768], P(('section', 'dp'))
- project_copy: bfloat16 [4096, 768], P(('section', 'dp'))
- vector_grad: float32 [11264], P(('section', 'dp'))
- vector_momentum_new: float32 [11264], P(('section', 'dp'))
- vector_average_new: float32 [11264], P(('section', 'dp'))
- vector_master_new: float32 [11264], P(('section', 'dp'))
- vector_copy: bfloat16 [11264], P(('section', 'dp'))
Inputs may be any that keep to these rules, and one draw needn't show every extreme that they name: `image_group`: no group is named twice, so some groups are named by no image. Of the 16 images of one stem device at most 2 name groups of one text device, and exactly 2 do for some pair; some text device has all its 32 groups named. `text_lengths`: each row sums to 512, and its largest entry is 32.
All inputs are finite; a program needn't handle non-finite values.
Results may differ from a plain program's by a relative error of at most 0.015.
Values may be sent and summed in bfloat16 or wider, within the bound.
No kernel may reach another device: no remote copies, remote signals or barrier semaphores. Data moves between devices by JAX's collectives and lax.ppermute only.
A program may use at most 448 MiB of HBM per device.

v0:
```python
import math

import jax
import jax.numpy as jnp
from jax import lax
from jax.sharding import PartitionSpec as P

D = 768
HEADS = 12
HEAD_DIM = 64
FF = 3072
CH = 1024
PATCH = 196
IMG_DEV = 16
GROUPS_DEV = 32
LONGEST = 32


def partner(block, axis, stride):
    count = lax.axis_size(axis)
    route = []
    for low in range(count):
        high = low | 1 << stride
        if high != low and high < count:
            route += [(low, high), (high, low)]
    return lax.ppermute(block, axis, route)


def gelu_tanh(values):
    return jax.nn.gelu(values, approximate=True)


def matmul(left, right):
    return jnp.dot(left, right, preferred_element_type=jnp.float32)


def matmul_right_t(left, right):
    return lax.dot_general(
        left, right, (((1,), (1,)), ((), ())), preferred_element_type=jnp.float32
    )


def matmul_left_t(left, right):
    return lax.dot_general(
        left, right, (((0,), (0,)), ((), ())), preferred_element_type=jnp.float32
    )


def split_vector(vector):
    offset = 2 * CH + D
    return (
        vector[:CH],
        vector[CH : 2 * CH],
        vector[2 * CH : offset],
        vector[offset : offset + D],
        vector[offset + D : offset + 2 * D],
        vector[offset + 2 * D : offset + 3 * D],
        vector[offset + 3 * D : offset + 4 * D],
        vector[offset + 4 * D : offset + 5 * D],
        vector[offset + 5 * D : offset + 6 * D],
        vector[offset + 6 * D : offset + 6 * D + FF],
        vector[offset + 6 * D + FF :],
    )


def norm_forward(values, gain_vec, bias_vec):
    center = jnp.mean(values, axis=-1, keepdims=True)
    shifted = values - center
    spread = jnp.mean(shifted * shifted, axis=-1, keepdims=True)
    factor = lax.rsqrt(spread + 1e-05)
    normed = shifted * factor
    return (normed * gain_vec + bias_vec, normed, factor)


def norm_backward(grad_out, normed, factor, gain_vec):
    grad_normed = grad_out * gain_vec
    mean_grad = jnp.mean(grad_normed, axis=-1, keepdims=True)
    mean_cross = jnp.mean(grad_normed * normed, axis=-1, keepdims=True)
    grad_in = factor * (grad_normed - mean_grad - normed * mean_cross)
    return (grad_in, jnp.sum(grad_out * normed, axis=0), jnp.sum(grad_out, axis=0))


def split_heads(matrix):
    return matrix.reshape(matrix.shape[0], HEADS, HEAD_DIM)


def masked_scores(queries, key_rows, allowed):
    scores = jnp.einsum(
        "thc,shc->hts",
        split_heads(queries),
        split_heads(key_rows),
        preferred_element_type=jnp.float32,
    ) * HEAD_DIM ** (-0.5)
    return jnp.where(allowed[None], scores, -1e30)


def attend_forward(queries, key_rows, value_rows, allowed):
    scores = masked_scores(queries, key_rows, allowed)
    highest = jnp.max(scores, axis=-1, keepdims=True)
    weights = jnp.exp(scores - highest)
    weight_sum = jnp.sum(weights, axis=-1, keepdims=True)
    shares = (weights / weight_sum).astype(jnp.bfloat16)
    mixed_rows = jnp.einsum(
        "hts,shc->thc", shares, split_heads(value_rows), preferred_element_type=jnp.float32
    )
    return (mixed_rows.reshape(queries.shape[0], HEADS * HEAD_DIM), highest + jnp.log(weight_sum))


def attend_backward(grad_mixed, queries, key_rows, value_rows, allowed, summary):
    shares = jnp.exp(masked_scores(queries, key_rows, allowed) - summary)
    heads_grad = split_heads(grad_mixed)
    grad_shares = jnp.einsum(
        "thc,shc->hts", heads_grad, split_heads(value_rows), preferred_element_type=jnp.float32
    )
    row_inner = jnp.sum(grad_shares * shares, axis=-1, keepdims=True)
    grad_scores = (shares * (grad_shares - row_inner)).astype(jnp.bfloat16)
    grad_queries = jnp.einsum(
        "hts,shc->thc", grad_scores, split_heads(key_rows), preferred_element_type=jnp.float32
    ) * HEAD_DIM ** (-0.5)
    grad_keys = jnp.einsum(
        "hts,thc->shc", grad_scores, split_heads(queries), preferred_element_type=jnp.float32
    ) * HEAD_DIM ** (-0.5)
    grad_values = jnp.einsum(
        "hts,thc->shc", shares.astype(jnp.bfloat16), heads_grad, preferred_element_type=jnp.float32
    )
    return (
        grad_queries.reshape(queries.shape[0], D).astype(jnp.bfloat16),
        grad_keys.reshape(key_rows.shape[0], D).astype(jnp.bfloat16),
        grad_values.reshape(value_rows.shape[0], D).astype(jnp.bfloat16),
    )


def window_heads(matrix, rows):
    return matrix[rows].reshape(rows.shape[0], rows.shape[1], HEADS, HEAD_DIM)


def group_heads(group_kv, first):
    return group_kv[:, :, first : first + D].reshape(
        group_kv.shape[0], group_kv.shape[1], HEADS, HEAD_DIM
    )


def cross_scores(query_win, key_heads):
    return jnp.einsum(
        "gwhc,gphc->ghwp", query_win, key_heads, preferred_element_type=jnp.float32
    ) * HEAD_DIM ** (-0.5)


def cross_forward(cross_q, group_kv, rows, valid):
    query_win = window_heads(cross_q, rows)
    key_heads = group_heads(group_kv, 0)
    value_heads = group_heads(group_kv, D)
    scores = cross_scores(query_win, key_heads)
    highest = jnp.max(scores, axis=-1, keepdims=True)
    weights = jnp.exp(scores - highest)
    total = jnp.sum(weights, axis=-1, keepdims=True)
    shares = (weights / total).astype(jnp.bfloat16)
    mixed = jnp.einsum("ghwp,gphc->gwhc", shares, value_heads, preferred_element_type=jnp.float32)
    mixed = mixed.reshape(rows.shape[0], rows.shape[1], D) * valid[:, :, None].astype(jnp.float32)
    placed = (
        jnp.zeros((cross_q.shape[0], D), jnp.float32).at[rows.reshape(-1)].add(mixed.reshape(-1, D))
    )
    return (placed, highest + jnp.log(total))


def cross_backward(grad_mix, cross_q, group_kv, rows, valid, summary):
    count, window = rows.shape
    patch_count = group_kv.shape[1]
    query_win = window_heads(cross_q, rows)
    key_heads = group_heads(group_kv, 0)
    value_heads = group_heads(group_kv, D)
    grad_win = (grad_mix[rows] * valid[:, :, None].astype(jnp.bfloat16)).reshape(
        count, window, HEADS, HEAD_DIM
    )
    shares = jnp.exp(cross_scores(query_win, key_heads) - summary)
    grad_shares = jnp.einsum(
        "gwhc,gphc->ghwp", grad_win, value_heads, preferred_element_type=jnp.float32
    )
    row_inner = jnp.sum(grad_shares * shares, axis=-1, keepdims=True)
    grad_scores = (shares * (grad_shares - row_inner)).astype(jnp.bfloat16)
    grad_query_win = jnp.einsum(
        "ghwp,gphc->gwhc", grad_scores, key_heads, preferred_element_type=jnp.float32
    ) * HEAD_DIM ** (-0.5)
    grad_keys = jnp.einsum(
        "ghwp,gwhc->gphc", grad_scores, query_win, preferred_element_type=jnp.float32
    ) * HEAD_DIM ** (-0.5)
    grad_values = jnp.einsum(
        "ghwp,gwhc->gphc", shares.astype(jnp.bfloat16), grad_win, preferred_element_type=jnp.float32
    )
    grad_query = (
        jnp.zeros((cross_q.shape[0], D), jnp.float32)
        .at[rows.reshape(-1)]
        .add(grad_query_win.reshape(-1, D))
        .astype(jnp.bfloat16)
    )
    grad_kv = jnp.concatenate(
        [grad_keys.reshape(count, patch_count, D), grad_values.reshape(count, patch_count, D)],
        axis=2,
    ).astype(jnp.bfloat16)
    return (grad_query, grad_kv)


def sgd_update(gradient, momentum, master, average, step_rate):
    new_momentum = 0.9 * momentum + gradient
    new_master = master - step_rate * (gradient + 0.9 * new_momentum)
    new_average = 0.8 * average + 0.2 * new_master
    return (gradient, new_momentum, new_average, new_master, new_master.astype(jnp.bfloat16))


def per_device(
    features,
    image_group,
    token_ids,
    text_lengths,
    cotangent,
    table_master,
    table_momentum,
    table_average,
    block_master,
    block_momentum,
    block_average,
    project_master,
    project_momentum,
    project_average,
    vector_master,
    vector_momentum,
    vector_average,
):
    dp_count = lax.axis_size("dp")
    section_count = lax.axis_size("section")
    group_size = lax.axis_size(("section", "dp"))
    dp_index = lax.axis_index("dp")
    is_stem = lax.axis_index("section") == 0
    block_full, project_full, vector_low = (
        lax.all_gather(block_master.astype(jnp.bfloat16), ("section", "dp"), axis=0, tiled=True),
        lax.all_gather(project_master.astype(jnp.bfloat16), ("section", "dp"), axis=0, tiled=True),
        lax.all_gather(vector_master.astype(jnp.bfloat16), ("section", "dp"), axis=0, tiled=True),
    )
    (
        bn_gain,
        bn_bias,
        patch_bias,
        gain_one,
        bias_one,
        gain_two,
        bias_two,
        gain_three,
        bias_three,
        up_bias,
        down_bias,
    ) = split_vector(vector_low.astype(jnp.float32))
    w_qkv = block_full[:, : 3 * D]
    w_out = block_full[:, 3 * D : 4 * D]
    w_cross_q = block_full[:, 4 * D : 5 * D]
    w_cross_kv = block_full[:, 5 * D : 7 * D]
    w_cross_out = block_full[:, 7 * D : 8 * D]
    w_up = block_full[:, 8 * D :]
    w_patch = project_full[:CH]
    w_down = project_full[CH:]
    image_rows = features.shape[0]
    every_patch = image_rows * dp_count
    capacity = (2 * IMG_DEV + dp_count - 1) // dp_count
    images_all = image_group.shape[0]
    destination = image_group // GROUPS_DEV
    by_source = destination.reshape(dp_count, IMG_DEV)
    local_order = jnp.arange(IMG_DEV, dtype=jnp.int32)
    earlier = local_order[None, :] < local_order[:, None]
    rank_all = jnp.sum(
        ((by_source[:, :, None] == by_source[:, None, :]) & earlier[None]).astype(jnp.int32), axis=2
    ).reshape(images_all)
    my_dest = lax.dynamic_slice_in_dim(destination, dp_index * IMG_DEV, IMG_DEV)
    my_rank = lax.dynamic_slice_in_dim(rank_all, dp_index * IMG_DEV, IMG_DEV)
    slot_total = group_size * capacity
    send_slot = (dp_count + my_dest) * capacity + my_rank
    read_slot = (dp_count + my_dest) * capacity + my_rank
    zero_channels = jnp.zeros((CH,), jnp.float32)
    local_sum = lax.cond(
        is_stem, lambda: jnp.sum(features.astype(jnp.float32), axis=0), lambda: zero_channels
    )
    center = lax.psum(local_sum, "dp") / every_patch
    local_square = lax.cond(
        is_stem,
        lambda: jnp.sum(jnp.square(features.astype(jnp.float32) - center), axis=0),
        lambda: zero_channels,
    )
    spread = lax.psum(local_square, "dp") / every_patch
    factor = lax.rsqrt(spread + 1e-05)

    def stem_state():
        stem_normed = (features.astype(jnp.float32) - center) * factor
        return (stem_normed, stem_normed * bn_gain + bn_bias)

    def stem_send():
        stem_normed, stem_pre = stem_state()
        stem_hidden = gelu_tanh(stem_pre).astype(jnp.bfloat16)
        patches = (matmul(stem_hidden, w_patch) + patch_bias).astype(jnp.bfloat16)
        return (
            jnp.zeros((slot_total, PATCH, D), jnp.bfloat16)
            .at[send_slot]
            .set(patches.reshape(IMG_DEV, PATCH, D))
        )

    outgoing = lax.cond(is_stem, stem_send, lambda: jnp.zeros((slot_total, PATCH, D), jnp.bfloat16))
    arrived = lax.all_to_all(outgoing, ("section", "dp"), split_axis=0, concat_axis=0, tiled=True)
    token_rows = token_ids.shape[0]
    running = jnp.zeros((token_rows, D), jnp.float32)
    shard_rows = lax.all_gather(
        table_master.astype(jnp.bfloat16), ("section", "dp"), axis=0, tiled=True
    )

    def add_rows():
        inside = (token_ids >= 0) & (token_ids < shard_rows.shape[0])
        picked = jnp.take(shard_rows, jnp.clip(token_ids, 0, shard_rows.shape[0] - 1), axis=0)
        return jnp.where(inside[:, None], picked.astype(jnp.float32), 0.0)

    resid_zero = lax.cond(is_stem, lambda: running, add_rows)

    def text_work():
        groups = dp_index * GROUPS_DEV + jnp.arange(GROUPS_DEV, dtype=jnp.int32)
        match = image_group[None, :] == groups[:, None]
        has_image = jnp.any(match, axis=1)
        image_of = jnp.sum(
            jnp.where(match, jnp.arange(images_all, dtype=jnp.int32)[None, :], 0), axis=1
        )
        slot_of = image_of // IMG_DEV * capacity + rank_all[image_of]
        flat_images = arrived[slot_of].reshape(GROUPS_DEV * PATCH, D)
        group_kv = (
            matmul(flat_images, w_cross_kv).astype(jnp.bfloat16).reshape(GROUPS_DEV, PATCH, 2 * D)
        )
        lengths = text_lengths[0]
        group_ends = jnp.cumsum(lengths)
        group_starts = group_ends - lengths
        window_start = jnp.minimum(group_starts, token_rows - LONGEST)
        window_rows = window_start[:, None] + jnp.arange(LONGEST, dtype=jnp.int32)[None, :]
        valid = (
            (window_rows >= group_starts[:, None])
            & (window_rows < group_ends[:, None])
            & has_image[:, None]
        )
        places = jnp.arange(token_rows, dtype=jnp.int32)
        segment = jnp.sum((places[:, None] >= group_ends[None, :]).astype(jnp.int32), axis=1)
        causal = (segment[:, None] == segment[None, :]) & (places[:, None] >= places[None, :])
        normed_one_f, unit_one, factor_one = norm_forward(resid_zero, gain_one, bias_one)
        normed_one = normed_one_f.astype(jnp.bfloat16)
        qkv_rows = matmul(normed_one, w_qkv).astype(jnp.bfloat16)
        self_queries = qkv_rows[:, :D]
        self_keys = qkv_rows[:, D : 2 * D]
        self_values = qkv_rows[:, 2 * D :]
        self_mix_f, self_summary = attend_forward(self_queries, self_keys, self_values, causal)
        self_mix = self_mix_f.astype(jnp.bfloat16)
        resid_one = resid_zero + matmul(self_mix, w_out)
        normed_two_f, unit_two, factor_two = norm_forward(resid_one, gain_two, bias_two)
        normed_two = normed_two_f.astype(jnp.bfloat16)
        cross_q = matmul(normed_two, w_cross_q).astype(jnp.bfloat16)
        cross_mix_f, cross_summary = cross_forward(cross_q, group_kv, window_rows, valid)
        cross_mix = cross_mix_f.astype(jnp.bfloat16)
        resid_two = resid_one + matmul(cross_mix, w_cross_out)
        normed_three_f, unit_three, factor_three = norm_forward(resid_two, gain_three, bias_three)
        normed_three = normed_three_f.astype(jnp.bfloat16)
        up_rows = matmul(normed_three, w_up) + up_bias
        up_act_f, up_gelu_back = jax.vjp(gelu_tanh, up_rows)
        up_act = up_act_f.astype(jnp.bfloat16)
        text_out = (resid_two + matmul(up_act, w_down) + down_bias).astype(jnp.bfloat16)
        grad_down_in = cotangent.astype(jnp.bfloat16)
        grad_w_down = matmul_left_t(up_act, grad_down_in)
        grad_down_bias = jnp.sum(cotangent, axis=0)
        grad_act = matmul_right_t(grad_down_in, w_down)
        grad_up = up_gelu_back(grad_act)[0].astype(jnp.bfloat16)
        grad_up_bias = jnp.sum(grad_up.astype(jnp.float32), axis=0)
        grad_w_up = matmul_left_t(normed_three, grad_up)
        back_three, grad_gain_three, grad_bias_three = norm_backward(
            matmul_right_t(grad_up, w_up), unit_three, factor_three, gain_three
        )
        grad_two = cotangent + back_three
        grad_cross_in = grad_two.astype(jnp.bfloat16)
        grad_w_cross_out = matmul_left_t(cross_mix, grad_cross_in)
        grad_cross_mix = matmul_right_t(grad_cross_in, w_cross_out).astype(jnp.bfloat16)
        grad_cross_q, grad_group_kv = cross_backward(
            grad_cross_mix, cross_q, group_kv, window_rows, valid, cross_summary
        )
        grad_w_cross_q = matmul_left_t(normed_two, grad_cross_q)
        back_two, grad_gain_two, grad_bias_two = norm_backward(
            matmul_right_t(grad_cross_q, w_cross_q), unit_two, factor_two, gain_two
        )
        grad_one = grad_two + back_two
        grad_self_in = grad_one.astype(jnp.bfloat16)
        grad_w_out = matmul_left_t(self_mix, grad_self_in)
        grad_self_mix = matmul_right_t(grad_self_in, w_out).astype(jnp.bfloat16)
        grad_self_q, grad_self_k, grad_self_v = attend_backward(
            grad_self_mix, self_queries, self_keys, self_values, causal, self_summary
        )
        grad_qkv = jnp.concatenate([grad_self_q, grad_self_k, grad_self_v], axis=1)
        grad_w_qkv = matmul_left_t(normed_one, grad_qkv)
        back_one, grad_gain_one, grad_bias_one = norm_backward(
            matmul_right_t(grad_qkv, w_qkv), unit_one, factor_one, gain_one
        )
        text_grad_embed = (grad_one + back_one).astype(jnp.bfloat16)
        flat_grad_kv = grad_group_kv.reshape(GROUPS_DEV * PATCH, 2 * D)
        grad_w_cross_kv = matmul_left_t(flat_images, flat_grad_kv)
        grad_group = (
            matmul_right_t(flat_grad_kv, w_cross_kv)
            .astype(jnp.bfloat16)
            .reshape(GROUPS_DEV, PATCH, D)
        )
        text_back = jnp.zeros((slot_total, PATCH, D), jnp.bfloat16).at[slot_of].add(grad_group)
        text_block = jnp.concatenate(
            [grad_w_qkv, grad_w_out, grad_w_cross_q, grad_w_cross_kv, grad_w_cross_out, grad_w_up],
            axis=1,
        )
        text_vector = jnp.concatenate(
            [
                grad_gain_one,
                grad_bias_one,
                grad_gain_two,
                grad_bias_two,
                grad_gain_three,
                grad_bias_three,
                grad_up_bias,
                grad_down_bias,
            ]
        )
        return (text_out, text_grad_embed, text_block, grad_w_down, text_vector, text_back)

    def text_blank():
        return (
            jnp.zeros((token_rows, D), jnp.bfloat16),
            jnp.zeros((token_rows, D), jnp.bfloat16),
            jnp.zeros((D, 8 * D + FF), jnp.float32),
            jnp.zeros((FF, D), jnp.float32),
            jnp.zeros((7 * D + FF,), jnp.float32),
            jnp.zeros((slot_total, PATCH, D), jnp.bfloat16),
        )

    block_out, grad_embed, block_term, grad_w_down, text_vector, back_buffer = lax.cond(
        is_stem, text_blank, text_work
    )
    returned = lax.all_to_all(
        back_buffer, ("section", "dp"), split_axis=0, concat_axis=0, tiled=True
    )

    def stem_back():
        grad_patches = returned[read_slot].reshape(image_rows, D)
        stem_normed, stem_pre = stem_state()
        stem_act, gelu_back = jax.vjp(gelu_tanh, stem_pre)
        stem_hidden = stem_act.astype(jnp.bfloat16)
        grad_patch_bias = jnp.sum(grad_patches.astype(jnp.float32), axis=0)
        grad_w_patch = matmul_left_t(stem_hidden, grad_patches)
        grad_pre = gelu_back(matmul_right_t(grad_patches, w_patch))[0]
        return (grad_pre, stem_normed, grad_w_patch, grad_patch_bias)

    def stem_blank():
        return (
            jnp.zeros((image_rows, CH), jnp.float32),
            jnp.zeros((image_rows, CH), jnp.float32),
            jnp.zeros((CH, D), jnp.float32),
            jnp.zeros((D,), jnp.float32),
        )

    grad_pre, stem_normed, grad_w_patch, grad_patch_bias = lax.cond(is_stem, stem_back, stem_blank)
    local_bias = jnp.sum(grad_pre, axis=0)
    local_gain = jnp.sum(grad_pre * stem_normed, axis=0)
    totals = lax.psum(jnp.stack([local_bias, local_gain]), "dp")
    feature_grad = factor * (
        grad_pre * bn_gain
        - bn_gain * totals[0] / every_patch
        - stem_normed * (bn_gain * totals[1] / every_patch)
    )
    project_term = jnp.concatenate([grad_w_patch, grad_w_down], axis=0)
    vector_term = jnp.concatenate([local_gain, local_bias, grad_patch_bias, text_vector])
    block_grad, project_grad, vector_grad = (
        lax.psum_scatter(block_term, ("section", "dp"), scatter_dimension=0, tiled=True),
        lax.psum_scatter(project_term, ("section", "dp"), scatter_dimension=0, tiled=True),
        lax.psum_scatter(vector_term, ("section", "dp"), scatter_dimension=0, tiled=True),
    )
    table_rows = table_master.shape[0]
    row_count = table_rows * lax.axis_size(("section", "dp"))

    def scatter_rows():
        inside = (token_ids >= 0) & (token_ids < row_count)
        spot = jnp.clip(token_ids, 0, row_count - 1)
        values = jnp.where(inside[:, None], grad_embed.astype(jnp.float32), 0.0)
        return jnp.zeros((row_count, D), jnp.float32).at[spot].add(values)

    table_grad = lax.psum_scatter(
        lax.cond(is_stem, lambda: jnp.zeros((row_count, D), jnp.float32), scatter_rows),
        ("section", "dp"),
        scatter_dimension=0,
        tiled=True,
    )
    root_tokens = math.sqrt(token_rows * dp_count)
    table_new = sgd_update(table_grad, table_momentum, table_master, table_average, 0.05)
    block_new = sgd_update(
        block_grad, block_momentum, block_master, block_average, 0.5 * D ** (-0.5) / root_tokens
    )
    project_new = sgd_update(
        project_grad,
        project_momentum,
        project_master,
        project_average,
        0.5 * FF ** (-0.5) / root_tokens,
    )
    vector_new = sgd_update(
        vector_grad, vector_momentum, vector_master, vector_average, 0.1 / root_tokens
    )
    half_channels = CH // section_count
    half_width = D // section_count
    got_grad, got_out = (
        partner(feature_grad[:, half_channels:].astype(jnp.bfloat16), "section", 0).astype(
            jnp.float32
        ),
        partner(block_out[:, :half_width], "section", 0),
    )
    feature_piece = jnp.where(is_stem, feature_grad[:, :half_channels], got_grad)
    block_piece = jnp.where(is_stem, got_out, block_out[:, half_width:])
    return (
        block_piece,
        feature_piece,
        table_new[0],
        table_new[1],
        table_new[2],
        table_new[3],
        table_new[4],
        block_new[0],
        block_new[1],
        block_new[2],
        block_new[3],
        block_new[4],
        project_new[0],
        project_new[1],
        project_new[2],
        project_new[3],
        project_new[4],
        vector_new[0],
        vector_new[1],
        vector_new[2],
        vector_new[3],
        vector_new[4],
    )


def solution(mesh):
    placed = (
        P("dp", None),
        P(),
        P("dp"),
        P("dp", None),
        P("dp", None),
        P(("section", "dp"), None),
        P(("section", "dp"), None),
        P(("section", "dp"), None),
        P(("section", "dp"), None),
        P(("section", "dp"), None),
        P(("section", "dp"), None),
        P(("section", "dp"), None),
        P(("section", "dp"), None),
        P(("section", "dp"), None),
        P(("section", "dp")),
        P(("section", "dp")),
        P(("section", "dp")),
    )
    return jax.shard_map(
        per_device,
        mesh=mesh,
        in_specs=placed,
        out_specs=(
            P("dp", "section"),
            P("dp", "section"),
            P(("section", "dp"), None),
            P(("section", "dp"), None),
            P(("section", "dp"), None),
            P(("section", "dp"), None),
            P(("section", "dp"), None),
            P(("section", "dp"), None),
            P(("section", "dp"), None),
            P(("section", "dp"), None),
            P(("section", "dp"), None),
            P(("section", "dp"), None),
            P(("section", "dp"), None),
            P(("section", "dp"), None),
            P(("section", "dp"), None),
            P(("section", "dp"), None),
            P(("section", "dp"), None),
            P(("section", "dp")),
            P(("section", "dp")),
            P(("section", "dp")),
            P(("section", "dp")),
            P(("section", "dp")),
        ),
        check_vma=False,
    )
```

profile of v0, /device:TPU:0, one launch (start us, length us, event | category | flops | bytes accessed | tf_op | source)
XLA Modules:
  0.0 3079.5 jit_solution(4144853299398783841)
XLA Ops:
  16.1 43.6 %psum.21 = f32[1024]{0:T(1024)S(1)} all-reduce(f32[1024]{0:T(1024)S(1)} %get-tuple-element.286), channel_id=1, replica_groups=mesh['section'=2,'dp'=16] {'dp'}, use_global_device_ids=true, to_apply=%region_4.5 | all-reduce | flops 1024 | bytes 8192 | tf_op jit(solution)/shard_map/psum | solution.py:280
  60.5 38.0 %all-reduce = bf16[11264]{0:T(1024)(128)(2,1)S(1)} all-reduce(bf16[11264]{0:T(1024)(128)(2,1)S(1)} %dynamic-update-slice), channel_id=1, replica_groups=mesh['section'=2,'dp'=16] {'section','dp'}, use_global_device_ids=true, to_apply=%add | all-reduce | flops 11264 | bytes 45056
  103.1 41.6 %psum.22 = f32[1024]{0:T(1024)S(1)} all-reduce(f32[1024]{0:T(1024)S(1)} %get-tuple-element.287), channel_id=1, replica_groups=mesh['section'=2,'dp'=16] {'dp'}, use_global_device_ids=true, to_apply=%region_8.9 | all-reduce | flops 1024 | bytes 8192 | tf_op jit(solution)/shard_map/psum | solution.py:286
  147.5 39.2 %conditional.10 = (bf16[64,196,768]{2,1,0:T(8,128)(2,1)}) conditional(s32[]{:T(128)} %convert_element_type.206, () %tuple.56, (s32[16]{0:T(128)S(1)}, bf16[3136,1024]{1,0:T(8,128)(2,1)}, f32[1024]{0:T(1024)S(1)}, f32[1024]{0:T(1024)S(1)}, f32[1024]{0:T(1024)S(1)}, /*index=5*/f32[1024]{0:T(1024)S(1)}, bf16[1024,768]{1,0:T(8,128)(2,1)S(1)}, ...), branch_computations={%region_9.10_spmd, %region_10.12_spmd} | conditional | flops 4982276096 | bytes 56190152 | solution.py:303
  147.5 13.4 add_convert_fusion
  160.9 7.2 reshape.656
  168.1 6.8 broadcast.516
  174.9 11.8 scatter_fusion.1
  191.8 419.8 %all-gather.4.cloned.1.call-done = bf16[32000,768]{1,0:T(8,128)(2,1)} async-done(((bf16[1000,768]{1,0:T(8,128)(2,1)}), bf16[32000,768]{1,0:T(8,128)(2,1)}) %all-gather.4.cloned.1.call-update) | async-done | bytes 49152016 | tf_op jit(solution)/shard_map/all_gather | solution.py:307
  611.8 191.9 %all-gather.6.cloned.1.call-done = bf16[768,9216]{1,0:T(8,128)(2,1)} async-done(((bf16[24,9216]{1,0:T(8,128)(2,1)}), bf16[768,9216]{1,0:T(8,128)(2,1)}) %all-gather.6.cloned.1.call-update) | async-done | bytes 14155792 | tf_op jit(solution)/shard_map/all_gather | solution.py:235
  803.8 33.9 %all-to-all-done = bf16[64,196,768]{2,1,0:T(8,128)(2,1)} async-done(((bf16[64,196,768]{2,1,0:T(8,128)(2,1)}), bf16[64,196,768]{2,1,0:T(8,128)(2,1)}, u32[]{:S(2)}, u32[]{:S(2)}) %all-to-all-start) | async-done | bytes 19267616 | tf_op jit(solution)/shard_map/all_to_all | solution.py:304
  837.6 30.4 conditional.11
  848.4 6.8 broadcast.553
  855.2 12.9 broadcast.550
  868.7 593.4 %all-to-all-start.1 = ((bf16[64,196,768]{2,1,0:T(8,128)(2,1)}), bf16[64,196,768]{2,1,0:T(8,128)(2,1)}, u32[]{:S(2)}, u32[]{:S(2)}) async-start(bf16[64,196,768]{2,1,0:T(8,128)(2,1)} %get-tuple-element.172), calls=%async_computation.1 | async-start | bytes 39321600 | tf_op jit(solution)/shard_map/all_to_all | solution.py:437
  1462.6 565.6 %all-to-all-done.1 = bf16[64,196,768]{2,1,0:T(8,128)(2,1)} async-done(((bf16[64,196,768]{2,1,0:T(8,128)(2,1)}), bf16[64,196,768]{2,1,0:T(8,128)(2,1)}, u32[]{:S(2)}, u32[]{:S(2)}) %all-to-all-start.1) | async-done | bytes 19267616 | tf_op jit(solution)/shard_map/all_to_all | solution.py:437
  2028.3 58.0 %conditional.12 = (f32[3136,1024]{1,0:T(8,128)}, f32[3136,1024]{1,0:T(8,128)}, f32[1024,768]{1,0:T(8,128)S(1)}, f32[768]{0:T(1024)S(1)}, f32[1024]{0:T(1024)S(1)}, /*index=5*/f32[1024]{0:T(1024)S(1)}) conditional(s32[]{:T(128)} %convert_element_type.206, () %tuple.63, (s32[16]{0:T(128)S(1)}, bf16[64,196,768]{2,1,0:T(8,128)(2,1)}, ...), branch_computations={%region_49.50_spmd, %region_50.52_spmd} | conditional | flops 9991845888 | bytes 121838952 | solution.py:459
  2028.6 9.7 gather_fusion.5
  2041.4 7.2 reshape.600
  2048.6 9.5 subtract_multiply_fusion
  2058.1 10.3 fusion.6
  2068.5 17.9 multiply_reduce_fusion.1
  2086.4 9.1 pad_maximum_fusion.3
  2096.6 35.6 %conditional.13 = (f32[32000,768]{1,0:T(8,128)}) conditional(s32[]{:T(128)} %convert_element_type.206, (s32[512]{0:T(512)S(1)}, bf16[512,768]{1,0:T(8,128)(2,1)S(1)}) %tuple.150, () %tuple.66), branch_computations={%region_55.57_spmd, %region_57.58_spmd} | conditional | flops 1183232 | bytes 105391112 | solution.py:485
  2096.6 35.6 %broadcast.566 = f32[32000,768]{1,0:T(8,128)} broadcast(f32[]{:T(128)} %constant.179.clone), dimensions={} | broadcast | bytes 98304000 | tf_op jit(solution)/shard_map/broadcast.112
  2133.4 16.6 collective-permute-start
  2152.2 39.6 %psum.23 = f32[2,1024]{1,0:T(2,128)S(1)} all-reduce(f32[2,1024]{1,0:T(2,128)S(1)} %pad_maximum_fusion.5), channel_id=1, replica_groups=mesh['section'=2,'dp'=16] {'dp'}, use_global_device_ids=true, to_apply=%region_54.55 | all-reduce | flops 2048 | bytes 16384 | tf_op jit(solution)/shard_map/psum | solution.py:462
  2192.5 10.0 subtract_multiply_fusion.4
  2209.6 38.7 %all-reduce.2 = f32[11264]{0:T(1024)S(1)} all-reduce(f32[11264]{0:T(1024)S(1)} %pad_maximum_fusion.4), channel_id=5, replica_groups=mesh['section'=2,'dp'=16] {'section','dp'}, use_global_device_ids=true, to_apply=%region_61.62.clone | all-reduce | flops 11264 | bytes 90112
  2254.0 8.1 slice_select_fusion
  2266.9 796.8 %reduce-scatter.10.cloned.1.call-done = f32[1000,768]{1,0:T(8,128)} async-done(((f32[32000,768]{1,0:T(8,128)}), f32[1000,768]{1,0:T(8,128)}) %reduce-scatter.10.cloned.1.call-update) | async-done | bytes 3072016
  3063.7 6.0 fusion.128
  (141 shorter events, 66.4 us)
Async XLA Ops:
  7.2 137.6 %all-gather.8.cloned.1.call-start = ((), (), s32[]{:S(2)}) async-start(), calls=%async_computation.7 | async-start | bytes 6488064 | tf_op jit(solution)/shard_map/all_gather | solution.py:236
  9.0 50.6 %copy-start.78 = (s32[256]{0:T(256)S(1)}, s32[256]{0:T(256)}, u32[]{:S(2)}) copy-start(s32[256]{0:T(256)} %param.32) | copy-start | bytes 3076
  9.0 602.5 %all-gather.4.cloned.1.call-start = ((), (), s32[]{:S(2)}) async-start(), calls=%async_computation.5 | async-start | bytes 50688000 | tf_op jit(solution)/shard_map/all_gather | solution.py:307
  59.6 86.8 %copy-start.50 = (f32[1024]{0:T(1024)}, f32[1024]{0:T(1024)S(1)}, u32[]{:S(2)}) copy-start(f32[1024]{0:T(1024)S(1)} %broadcast_multiply_fusion.10) | copy-start | bytes 12292
  98.5 739.1 %copy-start.47 = (f32[11264]{0:T(1024)}, f32[11264]{0:T(1024)S(1)}, u32[]{:S(2)}) copy-start(f32[11264]{0:T(1024)S(1)} %convert_element_type.209) | copy-start | bytes 135172
  186.7 424.8 %copy-start.60 = (s32[512]{0:T(512)S(1)}, s32[512]{0:T(512)}, u32[]{:S(2)}) copy-start(s32[512]{0:T(512)} %param.33) | copy-start | bytes 6148
  186.7 650.9 %all-to-all-start = ((bf16[64,196,768]{2,1,0:T(8,128)(2,1)}), bf16[64,196,768]{2,1,0:T(8,128)(2,1)}, u32[]{:S(2)}, u32[]{:S(2)}) async-start(bf16[64,196,768]{2,1,0:T(8,128)(2,1)} %get-tuple-element.288), calls=%async_computation | async-start | bytes 39321600 | tf_op jit(solution)/shard_map/all_to_all | solution.py:304
  190.9 646.8 %copy-start.95 = (s32[1,32]{1,0:T(1,128)S(1)}, s32[1,32]{1,0:T(1,128)}, u32[]{:S(2)}) copy-start(s32[1,32]{1,0:T(1,128)} %param.34) | copy-start | bytes 388
  190.9 612.9 %all-gather.6.cloned.1.call-start = ((), (), s32[]{:S(2)}) async-start(), calls=%async_computation.6 | async-start | bytes 14598144 | tf_op jit(solution)/shard_map/all_gather | solution.py:235
  868.7 1159.6 %all-to-all-start.1 = ((bf16[64,196,768]{2,1,0:T(8,128)(2,1)}), bf16[64,196,768]{2,1,0:T(8,128)(2,1)}, u32[]{:S(2)}, u32[]{:S(2)}) async-start(bf16[64,196,768]{2,1,0:T(8,128)(2,1)} %get-tuple-element.172), calls=%async_computation.1 | async-start | bytes 39321600 | tf_op jit(solution)/shard_map/all_to_all | solution.py:437
  1462.0 787.5 %reduce-scatter.6.cloned.1.call-start = ((), (), s32[]{:S(2)}) async-start(), calls=%async_computation.8 | async-start | bytes 29196288 | tf_op jit(solution)/shard_map/reduce_scatter | solution.py:471
  1462.1 566.2 %copy-start.49 = (f32[1024]{0:T(1024)S(1)}, f32[1024]{0:T(1024)}, u32[]{:S(2)}) copy-start(f32[1024]{0:T(1024)} %copy-done.48) | copy-start | bytes 12292
  1462.1 566.2 %copy-start.51 = (f32[1024]{0:T(1024)S(1)}, f32[1024]{0:T(1024)}, u32[]{:S(2)}) copy-start(f32[1024]{0:T(1024)} %copy-done.50) | copy-start | bytes 12292
  1462.1 566.2 %copy-start.75 = (f32[1024]{0:T(1024)S(1)}, f32[1024]{0:T(1024)}, u32[]{:S(2)}) copy-start(f32[1024]{0:T(1024)} %copy-done.74) | copy-start | bytes 12292
  1462.1 566.2 %copy-start.92 = (f32[1024]{0:T(1024)S(1)}, f32[1024]{0:T(1024)}, u32[]{:S(2)}) copy-start(f32[1024]{0:T(1024)} %copy-done.91) | copy-start | bytes 12292
  1462.1 566.2 %copy-start.99 = (s32[16]{0:T(128)S(1)}, s32[16]{0:T(128)}, u32[]{:S(2)}) copy-start(s32[16]{0:T(128)} %copy-done.98) | copy-start | bytes 196
  1462.6 799.5 %reduce-scatter.8.cloned.1.call-start = ((), (), s32[]{:S(2)}) async-start(), calls=%async_computation.9 | async-start | bytes 12976128 | tf_op jit(solution)/shard_map/reduce_scatter | solution.py:472
  2048.6 9.5 copy-start.25
  2058.1 10.3 copy-start.37
  2095.5 968.3 %reduce-scatter.10.cloned.1.call-start = ((), (), s32[]{:S(2)}) async-start(), calls=%async_computation.10 | async-start | bytes 101376000
  2133.4 18.0 collective-permute-start
  2207.3 41.0 %copy-start.85 = (f32[352]{0:T(512)S(1)}, f32[352]{0:T(512)}, u32[]{:S(2)}) copy-start(f32[352]{0:T(512)} %param.45) | copy-start | bytes 4228
  2207.3 41.0 %copy-start.93 = (f32[352]{0:T(512)S(1)}, f32[352]{0:T(512)}, u32[]{:S(2)}) copy-start(f32[352]{0:T(512)} %param.46) | copy-start | bytes 4228
  2207.3 41.7 %copy-start.94 = (f32[352]{0:T(512)S(1)}, f32[352]{0:T(512)}, u32[]{:S(2)}) copy-start(f32[352]{0:T(512)} %param.47) | copy-start | bytes 4228
  2207.3 42.2 %copy-start.27 = (f32[24,9216]{1,0:T(8,128)S(1)}, f32[24,9216]{1,0:T(8,128)}, u32[]{:S(2)}) copy-start(f32[24,9216]{1,0:T(8,128)} %param.39) | copy-start | bytes 2654212
  2207.3 42.2 %copy-start.42 = (f32[24,9216]{1,0:T(8,128)S(1)}, f32[24,9216]{1,0:T(8,128)}, u32[]{:S(2)}) copy-start(f32[24,9216]{1,0:T(8,128)} %param.40) | copy-start | bytes 2654212
  2207.4 45.6 %copy-start.43 = (f32[24,9216]{1,0:T(8,128)S(1)}, f32[24,9216]{1,0:T(8,128)}, u32[]{:S(2)}) copy-start(f32[24,9216]{1,0:T(8,128)} %param.41) | copy-start | bytes 2654212
  2209.6 44.4 %collective-permute-start.1 = (bf16[3136,512]{1,0:T(8,128)(2,1)}, bf16[3136,512]{1,0:T(8,128)(2,1)}, u32[]{:S(2)}, u32[]{:S(2)}) collective-permute-start(bf16[3136,512]{1,0:T(8,128)(2,1)} %slice.180), channel_id=1, source_target_pairs={{0,16},{16,0},{1,17},{17,1},{2,18},{18,2},{3,19},{19,3},{4,20},{20... | collective-permute-start | bytes 9633800 | tf_op jit(solution)/shard_map/ppermute | solution.py:26
  2249.0 13.1 copy-start.83
  2254.0 8.1 copy-start.40
  2254.0 809.7 %copy-start.16 = (f32[1000,768]{1,0:T(8,128)S(1)}, f32[1000,768]{1,0:T(8,128)}, u32[]{:S(2)}) copy-start(f32[1000,768]{1,0:T(8,128)} %param.36) | copy-start | bytes 9216004
  3063.7 6.0 copy-start.34
  (16 other events, 32.3 us)
Sparse Core Ops, SparseCore 0:
  11.5 73.6 all-gather.7
  88.6 522.8 all-gather.3
  615.0 188.7 all-gather.5
  1469.5 518.6 reduce-scatter.5
  2095.6 152.2 reduce-scatter.7
  2255.9 807.7 reduce-scatter.9
where the time goes:
time: 3100 us; the launch traced here: 3080 us
  waiting for transfers between devices  2010 us (65%)
  starting transfers between devices  614 us (20%)
  blocking collectives  201 us (6%)
  local copies, waits for them, and re-layouts  119 us (4%)
  other arithmetic  73.2 us (2%)
  matrix products  41.6 us (1%)
    unnamed x7, waiting for transfers between devices  797 us
    all_to_all x1, starting transfers between devices, per_device(): lax.all_to_all(back_buffer, ('section', 'dp'), split_axis=0, concat_axis=...  593 us
    all_to_all x1, waiting for transfers between devices, per_device(): lax.all_to_all(back_buffer, ('section', 'dp'), split_axis=0, concat_axis=...  566 us
    all_gather x1, waiting for transfers between devices, per_device(): lax.all_gather(table_master.astype(jnp.bfloat16), ('section', 'dp'), axis...  420 us
    all_gather x1, waiting for transfers between devices, per_device(): lax.all_gather(block_master.astype(jnp.bfloat16), ('section', 'dp'), axis...  192 us
    unnamed x2, blocking collectives  76.7 us
    another operation x9, local copies, waits for them, and re-layouts  68.2 us
  transfers between devices with their start and end apart: 10, of which 6 were waited for; matrix products, arithmetic and copies ran while one was open for 6% of the time, Pallas kernels for 0%

commit v1 on v0

v1 whole, which is shorter than its diff:
```python
import functools
import math

import jax
import jax.numpy as jnp
from jax import lax
from jax.experimental import pallas as pl
from jax.experimental.pallas import tpu as pltpu
from jax.sharding import PartitionSpec as P

D = 768
HEADS = 12
HEAD_DIM = 64
QUAD = 4 * HEAD_DIM
QUADS = HEADS // 4
FF = 3072
CH = 1024
PATCH = 196
WINDOW = 208
IMG_DEV = 16
GROUPS_DEV = 32
LONGEST = 32
HALF_ROWS = LONGEST // 2
BLOCK = 128
SPAN = BLOCK + LONGEST
SCALE = HEAD_DIM ** (-0.5)
EPS = 1e-05
NEG = -1e30
BOTH = ("section", "dp")
VMEM_BYTES = 58 * 1024 * 1024
bf16 = jnp.bfloat16
f32 = jnp.float32
i32 = jnp.int32


def mm(left, right):
    return jnp.dot(left, right, preferred_element_type=f32)


def mm_rt(left, right):
    return lax.dot_general(left, right, (((1,), (1,)), ((), ())), preferred_element_type=f32)


def mm_lt(left, right):
    return lax.dot_general(left, right, (((0,), (0,)), ((), ())), preferred_element_type=f32)


def normalise(values):
    shifted = values - jnp.mean(values, axis=-1, keepdims=True)
    factor = lax.rsqrt(jnp.mean(shifted * shifted, axis=-1, keepdims=True) + EPS)
    return shifted * factor, factor


def norm_back(incoming, unit, factor, gain):
    scaled = incoming * gain
    mean_grad = jnp.mean(scaled, axis=-1, keepdims=True)
    mean_cross = jnp.mean(scaled * unit, axis=-1, keepdims=True)
    return factor * (scaled - mean_grad - unit * mean_cross)


GELU_C = math.sqrt(2.0 / math.pi)


def gelu_parts(values):
    square = values * values
    bend = jnp.tanh(GELU_C * values * (1.0 + 0.044715 * square))
    half = 0.5 * (1.0 + bend)
    slope = half + 0.5 * values * (1.0 - bend * bend) * (GELU_C * (1.0 + 3 * 0.044715 * square))
    return values * half, slope


def gelu_only(values):
    bend = jnp.tanh(GELU_C * values * (1.0 + 0.044715 * (values * values)))
    return 0.5 * values * (1.0 + bend)


def head_masks(dtype):
    lanes = lax.broadcasted_iota(i32, (1, QUAD), 1) // HEAD_DIM
    return [jnp.where(lanes == h, 1.0, 0.0).astype(dtype) for h in range(4)]


def spread_heads(rows, masks):
    return jnp.concatenate([rows * m for m in masks], axis=0)


def join_heads(stacked, masks):
    count = stacked.shape[0] // 4
    total = stacked[:count] * masks[0]
    for h in range(1, 4):
        total = total + stacked[h * count : (h + 1) * count] * masks[h]
    return total


def softmax(scores, allowed):
    scores = jnp.where(allowed, scores * SCALE, NEG)
    weights = jnp.exp(scores - jnp.max(scores, axis=-1, keepdims=True))
    return weights * (1.0 / jnp.sum(weights, axis=-1, keepdims=True))


def one_hot_cols(index_col, width):
    places = lax.broadcasted_iota(i32, (index_col.shape[0], width), 1)
    return jnp.where(places == index_col, 1.0, 0.0).astype(bf16)


def one_hot_rows(index_row, height, offset=0):
    places = lax.broadcasted_iota(i32, (height, index_row.shape[1]), 0) + offset
    return jnp.where(places == index_row, 1.0, 0.0).astype(bf16)


def join_halves(target, low_ref, high_ref):
    count = low_ref.shape[0]
    target[:count, :] = low_ref[...]
    target[count : 2 * count, :] = high_ref[...]


def self_allowed(start_rows, first):
    rows = lax.broadcasted_iota(i32, (BLOCK, SPAN), 0) + first
    keys = lax.broadcasted_iota(i32, (BLOCK, SPAN), 1) + (first - LONGEST)
    allowed = (keys <= rows) & (keys >= start_rows)
    return jnp.concatenate([jnp.where(allowed, 1, 0)] * 4, axis=0) > 0


def text_first(
    embed, start, pack_a, pack_b, vecs,
    qkv_lo, qkv_hi, out_lo, out_hi, cq_lo, cq_hi,
    qkv_rows, mix_rows, resid_one, slots_a, slots_b,
    w_qkv, w_out, w_cq, padded,
):
    tokens = embed.shape[0]
    join_halves(w_qkv, qkv_lo, qkv_hi)
    join_halves(w_out, out_lo, out_hi)
    join_halves(w_cq, cq_lo, cq_hi)
    values = embed[...].astype(f32)
    unit, _ = normalise(values)
    normed = (unit * vecs[0:1, :] + vecs[1:2, :]).astype(bf16)
    for third in range(3):
        columns = slice(third * D, (third + 1) * D)
        qkv_rows[:, columns] = mm(normed, w_qkv[:, columns]).astype(bf16)
    padded[:LONGEST, :] = jnp.zeros((LONGEST, 2 * D), bf16)
    padded[LONGEST : LONGEST + tokens, :] = qkv_rows[:, D:]
    masks = head_masks(bf16)
    masks_f = head_masks(f32)

    def block(index, carry):
        first = pl.multiple_of(index * BLOCK, BLOCK)
        allowed = self_allowed(start[pl.ds(first, BLOCK), :], first)
        for quad in range(QUADS):
            lanes = slice(quad * QUAD, (quad + 1) * QUAD)
            later = slice(D + quad * QUAD, D + (quad + 1) * QUAD)
            queries = spread_heads(qkv_rows[pl.ds(first, BLOCK), lanes], masks)
            shares = softmax(mm_rt(queries, padded[pl.ds(first, SPAN), lanes]), allowed)
            mixed = mm(shares.astype(bf16), padded[pl.ds(first, SPAN), later])
            mix_rows[pl.ds(first, BLOCK), lanes] = join_heads(mixed, masks_f).astype(bf16)
        return carry

    lax.fori_loop(0, tokens // BLOCK, block, 0)
    resid = values + mm(mix_rows[...], w_out[...])
    resid_one[...] = resid
    unit, _ = normalise(resid)
    normed = (unit * vecs[2:3, :] + vecs[3:4, :]).astype(bf16)
    queries = mm(normed, w_cq[...]).astype(bf16)
    slots_a[...] = mm(one_hot_cols(pack_a[...], tokens), queries).astype(bf16)
    slots_b[...] = mm(one_hot_cols(pack_b[...], tokens), queries).astype(bf16)


def text_middle(
    mix_a, mix_b, take_a, take_b, pack_a, pack_b, resid_one, cotangent, vecs, up_bias,
    cout_lo, cout_hi, up_lo, up_hi, w_down,
    block_out, grad_two, grad_up_w, grad_down_w, grad_cout_w, slots_a, slots_b,
    vec_grad, up_bias_grad,
    w_cout, w_up, mixed, normed, normed_t, unit_s, factor_s, total, back, grad_down,
):
    step = pl.program_id(0)
    tokens = resid_one.shape[0]

    @pl.when(step == 0)
    def _():
        join_halves(w_cout, cout_lo, cout_hi)
        rows = mm(one_hot_rows(take_a[...], tokens), mix_a[...])
        rows = rows + mm(one_hot_rows(take_b[...], tokens), mix_b[...])
        mixed[...] = rows.astype(bf16)
        resid_two = resid_one[...] + mm(mixed[...], w_cout[...])
        unit, factor = normalise(resid_two)
        unit_s[...] = unit
        factor_s[...] = factor
        rows = unit * vecs[0:1, :] + vecs[1:2, :]
        normed[...] = rows.astype(bf16)
        normed_t[...] = rows.astype(bf16).T
        total[...] = resid_two + vecs[2:3, :]
        back[...] = jnp.zeros_like(back)
        grad_down[...] = cotangent[...].astype(bf16)
        vec_grad[2:3, :] = jnp.sum(cotangent[...], axis=0, keepdims=True)

    join_halves(w_up, up_lo, up_hi)
    up = mm(normed[...], w_up[...]) + up_bias[...]
    act, slope = gelu_parts(up)
    act = act.astype(bf16)
    total[...] += mm(act, w_down[...])
    grad_up_f = mm_rt(grad_down[...], w_down[...]) * slope
    grad_up = grad_up_f.astype(bf16)
    up_bias_grad[...] = jnp.sum(grad_up.astype(f32), axis=0, keepdims=True)
    grad_down_w[...] = mm_lt(act, grad_down[...]).astype(bf16)
    grad_up_w[...] = mm(normed_t[...], grad_up).astype(bf16)
    back[...] += mm_rt(grad_up, w_up[...])

    @pl.when(step == pl.num_programs(0) - 1)
    def _():
        block_out[...] = total[...].astype(bf16)
        incoming, unit = back[...], unit_s[...]
        vec_grad[0:1, :] = jnp.sum(incoming * unit, axis=0, keepdims=True)
        vec_grad[1:2, :] = jnp.sum(incoming, axis=0, keepdims=True)
        grad = cotangent[...] + norm_back(incoming, unit, factor_s[...], vecs[0:1, :])
        grad_two[...] = grad
        grad = grad.astype(bf16)
        grad_cout_w[...] = mm_lt(mixed[...], grad).astype(bf16)
        grad = mm_rt(grad, w_cout[...]).astype(bf16)
        slots_a[...] = mm(one_hot_cols(pack_a[...], tokens), grad).astype(bf16)
        slots_b[...] = mm(one_hot_cols(pack_b[...], tokens), grad).astype(bf16)


def text_last(
    grad_a, grad_b, take_a, take_b, place, grad_two, resid_one, embed, qkv_rows, mix_rows, start, vecs,
    qkv_lo, qkv_hi, out_lo, out_hi, cq_lo, cq_hi,
    grad_embed, rows_a, rows_b, grad_w, vec_grad,
    w_qkv, w_out, w_cq, padded, grad_mix, grad_qkv, total,
):
    tokens = embed.shape[0]
    join_halves(w_qkv, qkv_lo, qkv_hi)
    join_halves(w_out, out_lo, out_hi)
    join_halves(w_cq, cq_lo, cq_hi)
    grad_q = mm(one_hot_rows(take_a[...], tokens), grad_a[...])
    grad_q = (grad_q + mm(one_hot_rows(take_b[...], tokens), grad_b[...])).astype(bf16)
    unit, factor = normalise(resid_one[...])
    normed = (unit * vecs[2:3, :] + vecs[3:4, :]).astype(bf16)
    grad_w[:, 4 * D : 5 * D] = mm_lt(normed, grad_q).astype(bf16)
    incoming = mm_rt(grad_q, w_cq[...])
    vec_grad[2:3, :] = jnp.sum(incoming * unit, axis=0, keepdims=True)
    vec_grad[3:4, :] = jnp.sum(incoming, axis=0, keepdims=True)
    grad_one = grad_two[...] + norm_back(incoming, unit, factor, vecs[2:3, :])
    grad_low = grad_one.astype(bf16)
    grad_w[:, 3 * D : 4 * D] = mm_lt(mix_rows[...], grad_low).astype(bf16)
    grad_mix[...] = mm_rt(grad_low, w_out[...]).astype(bf16)
    padded[:LONGEST, :] = jnp.zeros((LONGEST, 2 * D), bf16)
    padded[LONGEST : LONGEST + tokens, :] = qkv_rows[:, D:]
    total[...] = jnp.zeros_like(total)
    masks = head_masks(bf16)
    masks_f = head_masks(f32)

    def block(index, carry):
        first = pl.multiple_of(index * BLOCK, BLOCK)
        allowed = self_allowed(start[pl.ds(first, BLOCK), :], first)
        for quad in range(QUADS):
            lanes = slice(quad * QUAD, (quad + 1) * QUAD)
            later = slice(D + quad * QUAD, D + (quad + 1) * QUAD)
            queries = spread_heads(qkv_rows[pl.ds(first, BLOCK), lanes], masks)
            grads = spread_heads(grad_mix[pl.ds(first, BLOCK), lanes], masks)
            keys = padded[pl.ds(first, SPAN), lanes]
            shares = softmax(mm_rt(queries, keys), allowed)
            grad_shares = mm_rt(grads, padded[pl.ds(first, SPAN), later])
            inner = jnp.sum(grad_shares * shares, axis=-1, keepdims=True)
            grad_scores = (shares * (grad_shares - inner)).astype(bf16)
            grad_queries = join_heads(mm(grad_scores, keys), masks_f) * SCALE
            grad_qkv[pl.ds(first, BLOCK), lanes] = grad_queries.astype(bf16)
            total[pl.ds(first, SPAN), lanes] += mm_lt(grad_scores, queries) * SCALE
            total[pl.ds(first, SPAN), later] += mm_lt(shares.astype(bf16), grads)
        return carry

    lax.fori_loop(0, tokens // BLOCK, block, 0)
    grad_qkv[:, D:] = total[LONGEST : LONGEST + tokens, :].astype(bf16)
    unit, factor = normalise(embed[...].astype(f32))
    normed = (unit * vecs[0:1, :] + vecs[1:2, :]).astype(bf16)
    for third in range(3):
        columns = slice(third * D, (third + 1) * D)
        grad_w[:, columns] = mm_lt(normed, grad_qkv[:, columns]).astype(bf16)
    incoming = mm_rt(grad_qkv[...], w_qkv[...])
    vec_grad[0:1, :] = jnp.sum(incoming * unit, axis=0, keepdims=True)
    vec_grad[1:2, :] = jnp.sum(incoming, axis=0, keepdims=True)
    grad_low = (grad_one + norm_back(incoming, unit, factor, vecs[0:1, :])).astype(bf16)
    grad_embed[...] = grad_low
    count = rows_a.shape[0]
    rows_a[...] = mm(one_hot_rows(place[...], count), grad_low).astype(bf16)
    rows_b[...] = mm(one_hot_rows(place[...], count, count), grad_low).astype(bf16)


def unpack_rows(rows_a, rows_b, place, embed):
    count = rows_a.shape[0]
    total = mm(one_hot_cols(place[...], count), rows_a[...])
    total = total + mm(one_hot_cols(place[...] - count, count), rows_b[...])
    embed[...] = total.astype(bf16)


def stem_forward(
    features, bn, w_patch, patch_bias, kv_lo0, kv_hi0, kv_lo1, kv_hi1, patches, kv, w_kv
):
    @pl.when(pl.program_id(0) == 0)
    def _():
        join_halves(w_kv.at[:, :D], kv_lo0, kv_hi0)
        join_halves(w_kv.at[:, D:], kv_lo1, kv_hi1)

    normed = (features[...].astype(f32) - bn[0:1, :]) * bn[1:2, :]
    hidden = gelu_only(normed * bn[2:3, :] + bn[3:4, :]).astype(bf16)
    rows = (mm(hidden, w_patch[...]) + patch_bias[...]).astype(bf16)
    patches[...] = rows
    kv[...] = mm(rows, w_kv[...]).astype(bf16)


def image_window(image):
    first = image * PATCH
    aligned = pl.multiple_of(first // 16 * 16, 16)
    lanes = lax.broadcasted_iota(i32, (1, WINDOW), 1) + (aligned - first)
    return aligned, (lanes >= 0) & (lanes < PATCH)


def cross_forward(slot, q_a, q_b, kv, mix_a, mix_b):
    mix_a[...] = jnp.zeros_like(mix_a)
    mix_b[...] = jnp.zeros_like(mix_b)
    masks = head_masks(bf16)
    masks_f = head_masks(f32)

    def image(index, carry):
        aligned, allowed = image_window(index)
        place = pl.ds(pl.multiple_of(slot[index] * HALF_ROWS, HALF_ROWS), HALF_ROWS)
        for quad in range(QUADS):
            lanes = slice(quad * QUAD, (quad + 1) * QUAD)
            later = slice(D + quad * QUAD, D + (quad + 1) * QUAD)
            rows = jnp.concatenate([q_a[place, lanes], q_b[place, lanes]], axis=0)
            scores = mm_rt(spread_heads(rows, masks), kv[pl.ds(aligned, WINDOW), lanes])
            shares = softmax(scores, allowed).astype(bf16)
            mixed = join_heads(mm(shares, kv[pl.ds(aligned, WINDOW), later]), masks_f).astype(bf16)
            mix_a[place, lanes] = mixed[:HALF_ROWS]
            mix_b[place, lanes] = mixed[HALF_ROWS:]
        return carry

    lax.fori_loop(0, IMG_DEV, image, 0)


def cross_backward(slot, q_a, q_b, g_a, g_b, kv, grad_a, grad_b, grad_kv):
    grad_a[...] = jnp.zeros_like(grad_a)
    grad_b[...] = jnp.zeros_like(grad_b)
    grad_kv[...] = jnp.zeros_like(grad_kv)
    masks = head_masks(bf16)
    masks_f = head_masks(f32)

    def image(index, carry):
        aligned, allowed = image_window(index)
        place = pl.ds(pl.multiple_of(slot[index] * HALF_ROWS, HALF_ROWS), HALF_ROWS)
        window = pl.ds(aligned, WINDOW)
        for quad in range(QUADS):
            lanes = slice(quad * QUAD, (quad + 1) * QUAD)
            later = slice(D + quad * QUAD, D + (quad + 1) * QUAD)
            rows = jnp.concatenate([q_a[place, lanes], q_b[place, lanes]], axis=0)
            queries = spread_heads(rows, masks)
            rows = jnp.concatenate([g_a[place, lanes], g_b[place, lanes]], axis=0)
            grads = spread_heads(rows, masks)
            keys = kv[window, lanes]
            shares = softmax(mm_rt(queries, keys), allowed)
            grad_shares = mm_rt(grads, kv[window, later])
            inner = jnp.sum(grad_shares * shares, axis=-1, keepdims=True)
            grad_scores = (shares * (grad_shares - inner)).astype(bf16)
            back = (join_heads(mm(grad_scores, keys), masks_f) * SCALE).astype(bf16)
            grad_a[place, lanes] = back[:HALF_ROWS]
            grad_b[place, lanes] = back[HALF_ROWS:]
            grad_kv[window, lanes] += (mm_lt(grad_scores, queries) * SCALE).astype(bf16)
            grad_kv[window, later] += mm_lt(shares.astype(bf16), grads).astype(bf16)
        return carry

    lax.fori_loop(0, IMG_DEV, image, 0)


def stem_backward(
    features, bn, w_patch, kv_lo0, kv_hi0, kv_lo1, kv_hi1, patches, grad_kv,
    grad_lo, grad_hi, grad_kv_w, grad_patch_w, sums, bias_sum,
    w_kv, kv_acc, patch_acc,
):
    step = pl.program_id(0)

    @pl.when(step == 0)
    def _():
        join_halves(w_kv.at[:, :D], kv_lo0, kv_hi0)
        join_halves(w_kv.at[:, D:], kv_lo1, kv_hi1)
        kv_acc[...] = jnp.zeros_like(kv_acc)
        patch_acc[...] = jnp.zeros_like(patch_acc)
        sums[...] = jnp.zeros_like(sums)
        bias_sum[...] = jnp.zeros_like(bias_sum)

    normed = (features[...].astype(f32) - bn[0:1, :]) * bn[1:2, :]
    hidden, slope = gelu_parts(normed * bn[2:3, :] + bn[3:4, :])
    grad_rows = mm_rt(grad_kv[...], w_kv[...]).astype(bf16)
    bias_sum[...] += jnp.sum(grad_rows.astype(f32), axis=0, keepdims=True)
    kv_acc[...] += mm_lt(patches[...], grad_kv[...])
    patch_acc[...] += mm_lt(hidden.astype(bf16), grad_rows)
    grad_pre = mm_rt(grad_rows, w_patch[...]) * slope
    sums[0:1, :] += jnp.sum(grad_pre * normed, axis=0, keepdims=True)
    sums[1:2, :] += jnp.sum(grad_pre, axis=0, keepdims=True)
    grad_low = grad_pre.astype(bf16)
    grad_lo[...] = grad_low[:, : CH // 2]
    grad_hi[...] = grad_low[:, CH // 2 :]

    @pl.when(step == pl.num_programs(0) - 1)
    def _():
        grad_kv_w[...] = kv_acc[...].astype(bf16)
        grad_patch_w[...] = patch_acc[...].astype(bf16)


def shape(dims, dtype):
    return jax.ShapeDtypeStruct(dims, dtype)


def whole(array):
    zeros = (0,) * array.ndim
    return pl.BlockSpec(array.shape, lambda *_: zeros)


def at(dims, *index):
    return pl.BlockSpec(dims, lambda *_: index)


def call(kernel, steps, in_specs, out_specs, outs, scratch, flops):
    return pl.pallas_call(
        kernel,
        grid=(steps,),
        in_specs=in_specs,
        out_specs=out_specs,
        out_shape=outs,
        scratch_shapes=scratch,
        compiler_params=pltpu.CompilerParams(vmem_limit_bytes=VMEM_BYTES),
        cost_estimate=pl.CostEstimate(flops=flops, bytes_accessed=flops // 500, transcendentals=0),
    )


def simple(kernel, inputs, outs, scratch, flops):
    return call(
        kernel,
        1,
        [whole(a) for a in inputs],
        [at(o.shape, *(0,) * len(o.shape)) for o in outs],
        outs,
        scratch,
        flops,
    )(*inputs)


def blank(outs):
    return pl.pallas_call(
        lambda *refs: None,
        out_shape=outs,
        out_specs=[pl.BlockSpec(memory_space=pl.ANY) for _ in outs],
    )()


def doubled(state, axis, count, merge):
    step = 1
    while step < count:
        other = lax.ppermute(state, axis, [(i, i ^ step) for i in range(count)])
        state = merge(state, other, step)
        step *= 2
    return state


def sgd_update(gradient, momentum, master, average, step_rate):
    new_momentum = 0.9 * momentum + gradient
    new_master = master - step_rate * (gradient + 0.9 * new_momentum)
    new_average = 0.8 * average + 0.2 * new_master
    return (gradient, new_momentum, new_average, new_master, new_master.astype(bf16))


def per_device(
    features,
    image_group,
    token_ids,
    text_lengths,
    cotangent,
    table_master,
    table_momentum,
    table_average,
    block_master,
    block_momentum,
    block_average,
    project_master,
    project_momentum,
    project_average,
    vector_master,
    vector_momentum,
    vector_average,
):
    dp = lax.axis_size("dp")
    group = lax.axis_size(BOTH)
    dp_index = lax.axis_index("dp")
    section = lax.axis_index("section")
    is_stem = section == 0
    me = section * dp + dp_index
    tokens = token_ids.shape[0]
    image_rows = features.shape[0]
    every_patch = image_rows * dp
    table_rows = table_master.shape[0]
    images = image_group.shape[0]

    block_full = lax.all_gather(block_master.astype(bf16), BOTH, axis=0, tiled=True)
    project_full = lax.all_gather(project_master.astype(bf16), BOTH, axis=0, tiled=True)

    capacity = (2 * IMG_DEV + dp - 1) // dp
    slots = dp * capacity
    half_slots = slots * HALF_ROWS
    destination = image_group // GROUPS_DEV
    by_source = destination.reshape(dp, IMG_DEV)
    order = jnp.arange(IMG_DEV, dtype=i32)
    earlier = order[None, :] < order[:, None]
    rank_all = jnp.sum(
        ((by_source[:, :, None] == by_source[:, None, :]) & earlier[None]).astype(i32), axis=2
    ).reshape(images)
    my_dest = lax.dynamic_slice_in_dim(destination, dp_index * IMG_DEV, IMG_DEV)
    my_rank = lax.dynamic_slice_in_dim(rank_all, dp_index * IMG_DEV, IMG_DEV)
    stem_slot = my_dest * capacity + my_rank
    slot_of_image = jnp.where(
        destination == dp_index,
        jnp.arange(images, dtype=i32) // IMG_DEV * capacity + rank_all,
        -1,
    )
    lengths = text_lengths[0]
    group_ends = jnp.cumsum(lengths)
    group_starts = group_ends - lengths
    places = jnp.arange(tokens, dtype=i32)
    start = jnp.max(
        jnp.where(group_starts[None, :] <= places[:, None], group_starts[None, :], 0), axis=1
    )
    match = slot_of_image[None, :] == jnp.arange(slots, dtype=i32)[:, None]
    slot_group = jnp.max(jnp.where(match, (image_group % GROUPS_DEV)[None, :], -1), axis=1)
    group_hit = slot_group[:, None] == jnp.arange(GROUPS_DEV, dtype=i32)[None, :]
    slot_start = jnp.sum(jnp.where(group_hit, group_starts[None, :], 0), axis=1)
    slot_length = jnp.sum(jnp.where(group_hit, lengths[None, :], 0), axis=1)
    within = jnp.arange(LONGEST, dtype=i32)
    slot_rows = jnp.where(
        within[None, :] < slot_length[:, None], slot_start[:, None] + within[None, :], -1
    )
    rows_a = slot_rows[:, :HALF_ROWS].reshape(half_slots)
    rows_b = slot_rows[:, HALF_ROWS:].reshape(half_slots)
    pack_a, pack_b = rows_a[:, None], rows_b[:, None]
    take_a, take_b = rows_a[None, :], rows_b[None, :]
    start = start[:, None]

    room = max(16, 2 * tokens // group)
    owner = token_ids // table_rows
    before = places[None, :] < places[:, None]
    same = token_ids[:, None] == token_ids[None, :]
    is_first = ~jnp.any(same & before, axis=1)
    rank = jnp.sum(
        ((owner[:, None] == owner[None, :]) & before & is_first[None, :]).astype(i32), axis=1
    )
    crowded = jnp.any(is_first & (rank >= room))
    first_place = jnp.where(is_first, owner * room + rank, -1)
    place = jnp.max(jnp.where(same, first_place[None, :], -1), axis=1)
    half_room = dp * room
    asked = lax.dynamic_slice_in_dim(
        jnp.max(
            jnp.where(
                first_place[None, :] == jnp.arange(group * room, dtype=i32)[:, None],
                (token_ids % table_rows)[None, :],
                -1,
            ),
            axis=1,
        ),
        section * half_room,
        half_room,
    )
    asked = lax.all_to_all(
        asked.reshape(dp, room), "dp", split_axis=0, concat_axis=0, tiled=True
    ).reshape(half_room)
    table_low = table_master.astype(bf16)
    table_hit = (asked[:, None] == jnp.arange(table_rows, dtype=i32)[None, :]).astype(bf16)
    served = mm(table_hit, table_low).astype(bf16)
    served = lax.all_to_all(
        served.reshape(dp, room, D), "dp", split_axis=0, concat_axis=0, tiled=True
    ).reshape(half_room, D)
    served_low = lax.ppermute(served, "section", [(0, 1)])

    rows_f = features.astype(f32)
    local_center = jnp.mean(rows_f, axis=0)
    local_square = jnp.sum(jnp.square(rows_f - local_center), axis=0)
    vector_own = lax.dynamic_update_slice(
        jnp.zeros((vector_master.shape[0] * group,), f32),
        vector_master.astype(bf16).astype(f32),
        (me * vector_master.shape[0],),
    ).reshape(-1, CH)
    state = jnp.concatenate(
        [
            local_center[None],
            local_square[None],
            jnp.broadcast_to(crowded.astype(f32), (1, CH)),
            vector_own,
        ]
    )

    def merge(mine, other, step):
        delta = other[0] - mine[0]
        squares = mine[1] + other[1] + delta * delta * (0.5 * image_rows * step)
        return jnp.concatenate(
            [(0.5 * (mine[0] + other[0]))[None], squares[None], mine[2:] + other[2:]]
        )

    state = doubled(state, "dp", dp, merge)
    center = state[0]
    factor = lax.rsqrt(state[1] / every_patch + EPS)
    any_crowded = state[2, 0] > 0.5
    vector_full = state[3:] + lax.ppermute(state[3:], "section", [(0, 1), (1, 0)])
    bn_gain, bn_bias = vector_full[0], vector_full[1]
    flat = vector_full.reshape(-1)
    offset = 2 * CH + D
    patch_bias = flat[2 * CH : offset].reshape(1, D)
    ln_vecs = flat[offset : offset + 6 * D].reshape(6, D)
    up_bias = flat[offset + 6 * D : offset + 6 * D + FF].reshape(1, FF)
    down_bias = flat[offset + 6 * D + FF :].reshape(1, D)
    vecs_outer = ln_vecs[:4]
    vecs_three = jnp.concatenate([ln_vecs[4:], down_bias])
    bn = jnp.stack([center, factor, bn_gain, bn_bias])

    def embed_packed():
        return simple(
            unpack_rows,
            [served_low, served, place[:, None]],
            [shape((tokens, D), bf16)],
            [],
            4 * tokens * half_room * D,
        )[0]

    def embed_gathered():
        table_full = lax.all_gather(table_low, BOTH, axis=0, tiled=True)
        return jnp.take(table_full, token_ids, axis=0)

    embed = lax.cond(any_crowded, embed_gathered, embed_packed)

    half = D // 2

    def halves(width, column):
        return [at((half, width), 0, column), at((half, width), 1, column)]

    qkv_specs = halves(3 * D, 0) + halves(D, 3) + halves(D, 4)
    kv_specs = halves(D, 5) + halves(D, 6)
    patch_spec = at((CH, D), 0, 0)
    blocks = 4
    per_block = image_rows // blocks
    qkv_scratch = [
        pltpu.VMEM((D, 3 * D), bf16),
        pltpu.VMEM((D, D), bf16),
        pltpu.VMEM((D, D), bf16),
        pltpu.VMEM((LONGEST + tokens, 2 * D), bf16),
    ]

    def rows_spec(width):
        return pl.BlockSpec((per_block, width), lambda step: (step, 0))

    slot_shape = shape((half_slots, D), bf16)

    text_saved = [
        shape((tokens, 3 * D), bf16),
        shape((tokens, D), bf16),
        shape((tokens, D), f32),
        slot_shape,
        slot_shape,
    ]
    stem_saved = [shape((image_rows, D), bf16), shape((image_rows, 2 * D), bf16)]

    def first_text():
        inputs = [embed, start, pack_a, pack_b, vecs_outer]
        done = call(
            text_first,
            1,
            [whole(a) for a in inputs] + qkv_specs,
            [at(o.shape, 0, 0) for o in text_saved],
            text_saved,
            qkv_scratch,
            2 * tokens * D * 5 * D,
        )(*inputs, *[block_full] * 6)
        return (*done, *blank(stem_saved))

    def first_stem():
        done = call(
            stem_forward,
            blocks,
            [rows_spec(CH), whole(bn), patch_spec, whole(patch_bias)] + kv_specs,
            [rows_spec(D), rows_spec(2 * D)],
            stem_saved,
            [pltpu.VMEM((D, 2 * D), bf16)],
            2 * image_rows * D * (CH + 2 * D),
        )(features, bn, project_full, patch_bias, *[block_full] * 4)
        return (*blank(text_saved), *done)

    qkv_rows, mix_rows, resid_one, q_a, q_b, patches, kv = lax.cond(is_stem, first_stem, first_text)

    def exchange(block):
        return lax.all_to_all(
            block.reshape(dp, capacity * HALF_ROWS, D), "dp", split_axis=0, concat_axis=0, tiled=True
        ).reshape(half_slots, D)

    def to_stem(block_a, block_b):
        moved = lax.ppermute(block_a, "section", [(1, 0)])
        got = exchange(jnp.where(is_stem, moved, block_b))
        return got, lax.ppermute(got, "section", [(1, 0)])

    def to_text(block_a, block_b):
        moved = lax.ppermute(block_b, "section", [(0, 1)])
        got = exchange(jnp.where(is_stem, block_a, moved))
        return lax.ppermute(got, "section", [(0, 1)]), got

    q_a, q_b = to_stem(q_a, q_b)
    slot_spec = pl.BlockSpec(memory_space=pltpu.SMEM)

    def cross_stem():
        return call(
            cross_forward,
            1,
            [slot_spec, whole(q_a), whole(q_b), whole(kv)],
            [whole(q_a), whole(q_b)],
            [slot_shape, slot_shape],
            [],
            4 * IMG_DEV * BLOCK * WINDOW * D,
        )(stem_slot, q_a, q_b, kv)

    mix_a, mix_b = lax.cond(is_stem, cross_stem, lambda: blank([slot_shape, slot_shape]))
    mix_a, mix_b = to_text(mix_a, mix_b)

    chunks = 3
    wide = FF // chunks
    middle_shapes = [
        shape((tokens, D), bf16),
        shape((tokens, D), f32),
        shape((D, FF), bf16),
        shape((FF, D), bf16),
        shape((D, D), bf16),
        slot_shape,
        slot_shape,
        shape((3, D), f32),
        shape((1, FF), f32),
    ]

    def middle_text():
        inputs = [mix_a, mix_b, take_a, take_b, pack_a, pack_b, resid_one, cotangent, vecs_three]
        first_up = 8 * D // wide
        outs = [at(o.shape, *(0,) * len(o.shape)) for o in middle_shapes]
        outs[2] = pl.BlockSpec((D, wide), lambda step: (0, step))
        outs[3] = pl.BlockSpec((wide, D), lambda step: (step, 0))
        outs[8] = pl.BlockSpec((1, wide), lambda step: (0, step))
        return call(
            text_middle,
            chunks,
            [whole(a) for a in inputs]
            + [pl.BlockSpec((1, wide), lambda step: (0, step))]
            + halves(D, 7)
            + [
                pl.BlockSpec((half, wide), lambda step: (0, first_up + step)),
                pl.BlockSpec((half, wide), lambda step: (1, first_up + step)),
                pl.BlockSpec((wide, D), lambda step: (CH // wide + step, 0)),
            ],
            outs,
            middle_shapes,
            [
                pltpu.VMEM((D, D), bf16),
                pltpu.VMEM((D, wide), bf16),
                pltpu.VMEM((tokens, D), bf16),
                pltpu.VMEM((tokens, D), bf16),
                pltpu.VMEM((D, tokens), bf16),
                pltpu.VMEM((tokens, D), f32),
                pltpu.VMEM((tokens, 1), f32),
                pltpu.VMEM((tokens, D), f32),
                pltpu.VMEM((tokens, D), f32),
                pltpu.VMEM((tokens, D), bf16),
            ],
            12 * tokens * D * FF,
        )(*inputs, up_bias, *[block_full] * 4, project_full)

    (
        block_out, grad_two, grad_up_w, grad_down_w, grad_cout_w, g_a, g_b, grads_three, grad_up_bias,
    ) = lax.cond(is_stem, lambda: blank(middle_shapes), middle_text)
    g_a, g_b = to_stem(g_a, g_b)

    def cross_stem_back():
        return call(
            cross_backward,
            1,
            [slot_spec] + [whole(q_a)] * 4 + [whole(kv)],
            [whole(q_a)] * 2 + [whole(kv)],
            [slot_shape, slot_shape, shape(kv.shape, bf16)],
            [],
            10 * IMG_DEV * BLOCK * WINDOW * D,
        )(stem_slot, q_a, q_b, g_a, g_b, kv)

    grad_a, grad_b, grad_kv = lax.cond(
        is_stem, cross_stem_back, lambda: blank([slot_shape, slot_shape, shape(kv.shape, bf16)])
    )
    grad_a, grad_b = to_text(grad_a, grad_b)

    row_shape = shape((half_room, D), bf16)
    text_last_shapes = [
        shape((tokens, D), bf16),
        row_shape,
        row_shape,
        shape((D, 5 * D), bf16),
        shape((4, D), f32),
    ]
    half_channels = CH // 2
    stem_last_shapes = [
        shape((image_rows, half_channels), bf16),
        shape((image_rows, half_channels), bf16),
        shape((D, 2 * D), bf16),
        shape((CH, D), bf16),
        shape((2, CH), f32),
        shape((1, D), f32),
    ]

    def last_text():
        inputs = [
            grad_a, grad_b, take_a, take_b, place[None, :], grad_two, resid_one, embed,
            qkv_rows, mix_rows, start, vecs_outer,
        ]
        done = call(
            text_last,
            1,
            [whole(a) for a in inputs] + qkv_specs,
            [at(o.shape, 0, 0) for o in text_last_shapes],
            text_last_shapes,
            qkv_scratch
            + [
                pltpu.VMEM((tokens, D), bf16),
                pltpu.VMEM((tokens, 3 * D), bf16),
                pltpu.VMEM((LONGEST + tokens, 2 * D), f32),
            ],
            4 * tokens * D * 5 * D,
        )(*inputs, *[block_full] * 6)
        return (*done, *blank(stem_last_shapes))

    def last_stem():
        done = call(
            stem_backward,
            blocks,
            [rows_spec(CH), whole(bn), patch_spec] + kv_specs + [rows_spec(D), rows_spec(2 * D)],
            [rows_spec(half_channels)] * 2
            + [at(o.shape, *(0,) * len(o.shape)) for o in stem_last_shapes[2:]],
            stem_last_shapes,
            [
                pltpu.VMEM((D, 2 * D), bf16),
                pltpu.VMEM((D, 2 * D), f32),
                pltpu.VMEM((CH, D), f32),
            ],
            4 * image_rows * D * (CH + 2 * D),
        )(features, bn, project_full, *[block_full] * 4, patches, grad_kv)
        return (*blank(text_last_shapes), *done)

    (
        grad_embed, rows_low, rows_high, grad_w, grads_outer,
        grad_lo, grad_hi, grad_kv_w, grad_patch_w, bn_sums, patch_bias_sum,
    ) = lax.cond(is_stem, last_stem, last_text)

    def term_stem():
        return (
            jnp.concatenate(
                [jnp.zeros((D, 5 * D), bf16), grad_kv_w, jnp.zeros((D, D + FF), bf16)], axis=1
            ),
            jnp.concatenate([grad_patch_w, jnp.zeros((FF, D), bf16)]),
        )

    def term_text():
        return (
            jnp.concatenate([grad_w, jnp.zeros((D, 2 * D), bf16), grad_cout_w, grad_up_w], axis=1),
            jnp.concatenate([jnp.zeros((CH, D), bf16), grad_down_w]),
        )

    block_term, project_term = lax.cond(is_stem, term_stem, term_text)
    block_grad = lax.psum_scatter(block_term, BOTH, scatter_dimension=0, tiled=True).astype(f32)
    project_grad = lax.psum_scatter(project_term, BOTH, scatter_dimension=0, tiled=True).astype(f32)

    gone = jnp.zeros((), f32)
    vector_term = jnp.concatenate(
        [
            jnp.where(is_stem, bn_sums.reshape(-1), gone),
            jnp.where(is_stem, patch_bias_sum.reshape(-1), gone),
            jnp.where(
                is_stem,
                gone,
                jnp.concatenate(
                    [
                        grads_outer.reshape(-1),
                        grads_three[:2].reshape(-1),
                        grad_up_bias.reshape(-1),
                        grads_three[2],
                    ]
                ),
            ),
        ]
    ).reshape(-1, CH)
    vector_total = doubled(vector_term, "dp", dp, lambda mine, other, step: mine + other)
    vector_total = vector_total + lax.ppermute(vector_total, "section", [(0, 1), (1, 0)])
    vector_grad = lax.dynamic_slice_in_dim(
        vector_total.reshape(-1), me * vector_master.shape[0], vector_master.shape[0]
    )

    got_hi = lax.ppermute(grad_hi, "section", [(0, 1)])
    own_pre = jnp.where(is_stem, grad_lo, got_hi).astype(f32)
    first_channel = section * half_channels

    def own_half(array):
        return lax.dynamic_slice_in_dim(array, first_channel, half_channels, axis=array.ndim - 1)

    own_normed = (own_half(features).astype(f32) - own_half(center)) * own_half(factor)
    own_gain = own_half(bn_gain)
    feature_grad = own_half(factor) * (
        own_pre * own_gain
        - own_gain * own_half(vector_total[1]) / every_patch
        - own_normed * (own_gain * own_half(vector_total[0]) / every_patch)
    )

    def table_packed():
        moved = lax.ppermute(rows_low, "section", [(1, 0)])
        sent = jnp.where(is_stem, moved, rows_high).reshape(dp, room, D)
        got = lax.all_to_all(sent, "dp", split_axis=0, concat_axis=0, tiled=True)
        hit = (jnp.arange(table_rows, dtype=i32)[:, None] == asked[None, :]).astype(bf16)
        return mm(hit, got.reshape(half_room, D))

    def table_gathered():
        rows = jnp.where(is_stem, lax.ppermute(grad_embed, "section", [(1, 0)]), grad_embed)
        rows = lax.all_gather(rows, "dp", axis=0, tiled=True).astype(f32)
        spot = lax.all_gather(token_ids, "dp", axis=0, tiled=True) - me * table_rows
        spot = jnp.where((spot >= 0) & (spot < table_rows), spot, table_rows)
        return jnp.zeros((table_rows, D), f32).at[spot].add(rows, mode="drop")

    table_grad = lax.cond(any_crowded, table_gathered, table_packed)

    root_tokens = math.sqrt(tokens * dp)
    table_new = sgd_update(table_grad, table_momentum, table_master, table_average, 0.05)
    block_new = sgd_update(
        block_grad, block_momentum, block_master, block_average, 0.5 * D ** (-0.5) / root_tokens
    )
    project_new = sgd_update(
        project_grad,
        project_momentum,
        project_master,
        project_average,
        0.5 * FF ** (-0.5) / root_tokens,
    )
    vector_new = sgd_update(
        vector_grad, vector_momentum, vector_master, vector_average, 0.1 / root_tokens
    )
    half_width = D // 2
    got_out = lax.ppermute(block_out[:, :half_width], "section", [(1, 0)])
    block_piece = jnp.where(is_stem, got_out, block_out[:, half_width:])
    return (block_piece, feature_grad, *table_new, *block_new, *project_new, *vector_new)


def solution(mesh):
    rows = P(BOTH, None)
    flat = P(BOTH)
    placed = (
        (P("dp", None), P(), P("dp"), P("dp", None), P("dp", None))
        + (rows,) * 9
        + (flat,) * 3
    )
    return jax.shard_map(
        per_device,
        mesh=mesh,
        in_specs=placed,
        out_specs=(P("dp", "section"), P("dp", "section")) + (rows,) * 15 + (flat,) * 5,
        check_vma=False,
    )
```

time: 3100 us -> 903 us (0.29)
  waiting for transfers between devices: 2010 us -> 508 us
  starting transfers between devices: 614 us -> 54.1 us
  Pallas kernels: 0 us -> 125 us
  blocking collectives: 201 us -> 99 us
  local copies, waits for them, and re-layouts: 119 us -> 18 us
  matrix products: 41.6 us -> 5.48 us
    unnamed x7 -> x4, waiting for transfers between devices: 797 us -> 1.08 us
    all_to_all x2 -> x3, starting transfers between devices: 598 us -> 18.8 us  [the longest x1 8.31 us: per_device(): lax.all_to_all(asked.reshape(dp, room), 'dp', split_axis=0, concat_axis=0...]
    all_to_all x2 -> x3, waiting for transfers between devices: 600 us -> 23.7 us  [the longest x1 18.6 us: table_packed(): got = lax.all_to_all(sent, 'dp', split_axis=0, concat_axis=0, tiled=True)]
    all_gather x3 -> x2, waiting for transfers between devices: 612 us -> 173 us  [the longest x1 105 us: per_device(): lax.all_gather(block_master.astype(bf16), BOTH, axis=0, tiled=True)]
    reduce_scatter x2, waiting for transfers between devices: 0.01 us -> 242 us  [the longest x1 165 us: per_device(): lax.psum_scatter(block_term, BOTH, scatter_dimension=0, tiled=True)]
    pallas_call x0 -> x8, Pallas kernels: none -> 125 us  [the longest x1 43.1 us: last_stem(): call(stem_backward, blocks, [rows_spec(CH), whole(bn), patch_spec] + kv_s...]
    psum x3 -> x0, blocking collectives: 125 us -> none  [the longest x1 43.6 us: per_device(): center = lax.psum(local_sum, 'dp') / every_patch]
    all_to_all x0 -> x4, blocking collectives: none -> 99 us  [exchange(): lax.all_to_all(block.reshape(dp, capacity * HALF_ROWS, D), 'dp', split_ax...]
  transfers between devices with their start and end apart: 10 -> 29, of which waited for: 6 -> 22; matrix products, arithmetic and copies ran while one was open for 6% -> 5% of each run, Pallas kernels for 0% -> 0%
where the time goes in v1:
time: 903 us; the launch traced here: 894 us
  waiting for transfers between devices  508 us (56%)
  Pallas kernels  125 us (14%)
  blocking collectives  99 us (11%)
  other arithmetic  55.9 us (6%)
  starting transfers between devices  54.1 us (6%)
  between operations  18.2 us (2%)
  local copies, waits for them, and re-layouts  18 us (2%)
  loops' own time  10.3 us (1%)
    reduce_scatter x1, waiting for transfers between devices, per_device(): lax.psum_scatter(block_term, BOTH, scatter_dimension=0, tiled=True)  165 us
    all_gather x1, waiting for transfers between devices, per_device(): lax.all_gather(block_master.astype(bf16), BOTH, axis=0, tiled=True)  105 us
    all_to_all x4, blocking collectives, exchange(): lax.all_to_all(block.reshape(dp, capacity * HALF_ROWS, D), 'dp', split_ax...  99 us
    reduce_scatter x1, waiting for transfers between devices, per_device(): lax.psum_scatter(project_term, BOTH, scatter_dimension=0, tiled=True)  77.3 us
    all_gather x1, waiting for transfers between devices, per_device(): lax.all_gather(project_master.astype(bf16), BOTH, axis=0, tiled=True)  68.1 us
    pallas_call x1, Pallas kernels, last_stem(): call(stem_backward, blocks, [rows_spec(CH), whole(bn), patch_spec] + kv_s...  43.1 us
    ppermute x2, waiting for transfers between devices, to_stem(): moved = lax.ppermute(block_a, 'section', [(1, 0)])  36.2 us
    pallas_call x1, Pallas kernels, cross_stem_back(): call(cross_backward, 1, [slot_spec] + [whole(q_a)] * 4 + [whole(kv)], [wh...  36.1 us
  transfers between devices with their start and end apart: 29, of which 22 were waited for; matrix products, arithmetic and copies ran while one was open for 5% of the time, Pallas kernels for 0%

profile of v1, /device:TPU:0, one launch (start us, length us, event | category | flops | bytes accessed | tf_op | source)
XLA Modules:
  0.0 894.1 jit_solution(13665473207974367083)
XLA Ops:
  11.1 8.3 all-to-all-start.1
  19.5 4.0 convert_reduce_fusion
  33.3 6.9 all-to-all-start.2
  54.3 5.1 all-to-all-done.2
  67.9 4.0 conditional.8
  76.4 68.1 %all-gather.12.cloned.1.call-done = bf16[4096,768]{1,0:T(8,128)(2,1)} async-done(((bf16[128,768]{1,0:T(8,128)(2,1)}), bf16[4096,768]{1,0:T(8,128)(2,1)}) %all-gather.12.cloned.1.call-update) | async-done | bytes 6291472 | tf_op jit(solution)/shard_map/all_gather | solution.py:499
  144.5 104.7 %all-gather.10.cloned.1.call-done = bf16[768,9216]{1,0:T(8,128)(2,1)} async-done(((bf16[24,9216]{1,0:T(8,128)(2,1)}), bf16[768,9216]{1,0:T(8,128)(2,1)}) %all-gather.10.cloned.1.call-update) | async-done | bytes 14155792 | tf_op jit(solution)/shard_map/all_gather | solution.py:498
  249.1 23.8 %conditional.9 = (bf16[512,2304]{1,0:T(8,128)(2,1)}, bf16[512,768]{1,0:T(8,128)(2,1)}, f32[512,768]{1,0:T(8,128)S(1)}, bf16[512,768]{1,0:T(8,128)(2,1)}, bf16[51...) conditional(s32[]{:T(128)} %convert_element_type.74, ...), branch_computations={%region_15.16_spmd, %region_16.17_spmd} | conditional | flops 12331253760 | bytes 24674852 | solution.py:687
  249.9 23.0 %branch_1_fun.10 = (bf16[3136,768]{1,0:T(8,128)(2,1)}, bf16[3136,1536]{1,0:T(8,128)(2,1)}) custom-call(bf16[3136,1024]{1,0:T(8,128)(2,1)} %get-tuple-element.254.features, f32[4,1024]{1,0:T(4,128)S(1)} %get-tuple-element.255.bn, bf16[4096,768]{1,0:T(8,128)(2,1)} %get-tuple-element.256.w_patch, f32[1,768]{1,0:T(1,128)} %reshape.238.patch_bias, ...), custom_call_target="tpu_custom_call" | custom-call | flops 12331253760 | bytes 24662508 | tf_op jit(solution)/shard_map/cond/branch_1_fun/pallas_call | solution.py:676
  277.4 25.2 %all_to_all.38 = bf16[16,32,768]{2,1,0:T(8,128)(2,1)S(1)} all-to-all(bf16[16,32,768]{2,1,0:T(8,128)(2,1)S(1)} %bitcast.52), channel_id=1, replica_groups=mesh['section'=2,'dp'=16] {'dp'}, dimensions={0} | all-to-all | bytes 1572864 | tf_op jit(solution)/shard_map/all_to_all | solution.py:690
  306.9 20.5 %conditional.10 = ((bf16[512,768]{1,0:T(8,128)(2,1)}, bf16[512,768]{1,0:T(8,128)(2,1)})) conditional(s32[]{:T(128)} %convert_element_type.74, () %tuple.79, (s32[16]{0:T(128)S(1)}, bf16[512,768]{1,0:T(8,128)(2,1)S(1)}, bf16[512,768]{1,0:T(8,128)(2,1)}, bf16[3136,1536]{1,0:T(8,128)(2,1)}) %tuple.178), branch_computations={%region_17.18_spmd, %region_18.19_spmd} | conditional | flops 1308622848 | bytes 2617253 | solution.py:718
  306.9 20.5 %branch_1_fun.11 = (bf16[512,768]{1,0:T(8,128)(2,1)}, bf16[512,768]{1,0:T(8,128)(2,1)}) custom-call(s32[16]{0:T(128)S(1)} %get-tuple-element.261.slot, bf16[512,768]{1,0:T(8,128)(2,1)S(1)} %get-tuple-element.262.q_a, bf16[512,768]{1,0:T(8,128)(2,1)} %get-tuple-element.263.q_b, bf16[3136,1536]{1,0:T(8,128)(2,1)} %get-tuple-element.264.kv), custom_call_target="tpu_custom_call" | custom-call | flops 1308622848 | bytes 2617245 | tf_op jit(solution)/shard_map/cond/branch_1_fun/pallas_call | solution.py:708
  332.0 24.2 %all_to_all.39 = bf16[16,32,768]{2,1,0:T(8,128)(2,1)} all-to-all(bf16[16,32,768]{2,1,0:T(8,128)(2,1)S(1)} %bitcast.53), channel_id=1, replica_groups=mesh['section'=2,'dp'=16] {'dp'}, dimensions={0} | all-to-all | bytes 1572864 | tf_op jit(solution)/shard_map/all_to_all | solution.py:690
  363.0 33.1 %collective-permute-done.13 = bf16[512,768]{1,0:T(8,128)(2,1)S(1)} collective-permute-done((bf16[512,768]{1,0:T(8,128)(2,1)}, bf16[512,768]{1,0:T(8,128)(2,1)S(1)}, u32[]{:S(2)}, u32[]{:S(2)}) %collective-permute-start.13) | collective-permute-done | bytes 786464 | tf_op jit(solution)/shard_map/ppermute | solution.py:695
  396.1 25.2 %all_to_all.40 = bf16[16,32,768]{2,1,0:T(8,128)(2,1)} all-to-all(bf16[16,32,768]{2,1,0:T(8,128)(2,1)S(1)} %bitcast.54), channel_id=1, replica_groups=mesh['section'=2,'dp'=16] {'dp'}, dimensions={0} | all-to-all | bytes 1572864 | tf_op jit(solution)/shard_map/all_to_all | solution.py:690
  425.8 36.1 %conditional.12 = ((bf16[512,768]{1,0:T(8,128)(2,1)}, bf16[512,768]{1,0:T(8,128)(2,1)}, bf16[3136,1536]{1,0:T(8,128)(2,1)})) conditional(s32[]{:T(128)} %convert_element_type.74, () %tuple.87, (s32[16]{0:T(128)S(1)}, bf16[512,768]{1,0:T(8,128)(2,1)S(1)}, bf16[512,768]{1,0:T(8,128)(2,1)}, bf16[512,768]{1,0:T(8,128)(2,1)}, ...), branch_computations={%region_21.22_spmd, %region_22.23_spmd} | conditional | flops 3271557120 | bytes 6543122 | solution.py:786
  425.8 36.1 %branch_1_fun.12 = (bf16[512,768]{1,0:T(8,128)(2,1)}, bf16[512,768]{1,0:T(8,128)(2,1)}, bf16[3136,1536]{1,0:T(8,128)(2,1)}) custom-call(s32[16]{0:T(128)S(1)} %get-tuple-element.295.slot, bf16[512,768]{1,0:T(8,128)(2,1)S(1)} %get-tuple-element.296.q_a, bf16[512,768]{1,0:T(8,128)(2,1)} %get-tuple-element.297.q_b, bf16[512,768]{1,0:T(8,128)(2,1)} %get-tuple-element.298.g_a, ...), custom_call_target="tpu_custom_call" | custom-call | flops 3271557120 | bytes 6543114 | tf_op jit(solution)/shard_map/cond/branch_1_fun/pallas_call | solution.py:776
  466.6 24.3 %all_to_all.41 = bf16[16,32,768]{2,1,0:T(8,128)(2,1)S(1)} all-to-all(bf16[16,32,768]{2,1,0:T(8,128)(2,1)S(1)} %bitcast.55), channel_id=1, replica_groups=mesh['section'=2,'dp'=16] {'dp'}, dimensions={0} | all-to-all | bytes 1572864 | tf_op jit(solution)/shard_map/all_to_all | solution.py:690
  494.1 52.4 %conditional.13 = (bf16[512,768]{1,0:T(8,128)(2,1)}, bf16[512,768]{1,0:T(8,128)(2,1)}, bf16[512,768]{1,0:T(8,128)(2,1)}, bf16[768,3840]{1,0:T(8,128)(2,1)}, f32[...) conditional(s32[]{:T(128)} %convert_element_type.74, ...), branch_computations={%region_23.24_spmd, %region_24.25_spmd} | conditional | flops 24662507520 | bytes 49325104 | solution.py:850
  503.4 43.1 %branch_1_fun.14 = (bf16[3136,512]{1,0:T(8,128)(2,1)}, bf16[3136,512]{1,0:T(8,128)(2,1)}, bf16[768,1536]{1,0:T(8,128)(2,1)S(1)}, bf16[1024,768]{1,0:T(8,128)(2,1...) custom-call(bf16[3136,1024]{1,0:T(8,128)(2,1)} %get-tuple-element.330.features, f32[4,1024]{1,0:T(4,128)S(1)} %get-tuple-element.331.bn, ...), custom_call_target="tpu_custom_call" | custom-call | flops 24662507520 | bytes 49325016 | tf_op jit(solution)/shard_map/cond/branch_1_fun/pallas_call | solution.py:831
  546.5 13.3 %conditional.15 = (bf16[768,9216]{1,0:T(8,128)(2,1)}, bf16[4096,768]{1,0:T(8,128)(2,1)}) conditional(s32[]{:T(128)} %convert_element_type.74, (bf16[768,3840]{1,0:T(8,128)(2,1)}, bf16[768,768]{1,0:T(8,128)(2,1)}, bf16[768,3072]{1,0:T(8,128)(2,1)}, bf16[3072,768]{1,0:T(8,128)(2,1)}) %tuple.93, (bf16[768,1536]{1,0:T(8,128)(2,1)S(1)}, ...), branch_computations={%region_28.29_spmd, %region_29.30_spmd} | conditional | flops 56623104 | bytes 79472712 | solution.py:866
  546.5 4.4 concatenate.27
  551.3 8.5 pad_maximum_fusion.1
  559.8 32.1 %conditional.14 = (f32[1000,768]{1,0:T(8,128)S(1)}) conditional(s32[]{:T(128)} %bitcast.8, (s32[16,1,32]{2,1,0:T(1,128)S(1)}, pred[]{:T(512)}, bf16[512,768]{1,0:T(8,128)(2,1)}, bf16[512,768]{1,0:T(8,128)(2,1)}) %tuple.184, (s32[512]{0:T(512)S(1)}, s32[]{:T(128)}, pred[]{:T(512)}, bf16[512,768]{1,0:T(8,128)(2,1)}) %tuple.183), branch_computations={%region_25.26_spmd, %region_26.28_spmd} | conditional | flops 787337216 | bytes 61433964 | solution.py:924
  565.2 3.6 all-to-all-start
  570.1 18.6 %all-to-all-done = bf16[16,32,768]{2,1,0:T(8,128)(2,1)S(1)} async-done(((bf16[16,32,768]{2,1,0:T(8,128)(2,1)}), bf16[16,32,768]{2,1,0:T(8,128)(2,1)S(1)}, u32[]{:S(2)}, u32[]{:S(2)}) %all-to-all-start) | async-done | bytes 786464 | tf_op jit(solution)/shard_map/cond/branch_0_fun/all_to_all | solution.py:913
  593.7 4.6 collective-permute-start.17
  602.9 3.5 collective-permute-done.18
  618.4 6.1 fusion.21
  629.7 6.2 subtract_multiply_fusion
  635.9 77.3 %reduce-scatter.5.cloned.1.call-done = bf16[128,768]{1,0:T(8,128)(2,1)} async-done(((bf16[4096,768]{1,0:T(8,128)(2,1)}), bf16[128,768]{1,0:T(8,128)(2,1)}) %reduce-scatter.5.cloned.1.call-update) | async-done | bytes 196624 | tf_op jit(solution)/shard_map/reduce_scatter | solution.py:868
  717.2 165.1 %reduce-scatter.3.cloned.1.call-done = bf16[24,9216]{1,0:T(8,128)(2,1)} async-done(((bf16[768,9216]{1,0:T(8,128)(2,1)}), bf16[24,9216]{1,0:T(8,128)(2,1)}) %reduce-scatter.3.cloned.1.call-update) | async-done | bytes 442384 | tf_op jit(solution)/shard_map/reduce_scatter | solution.py:867
  (240 shorter events, 117.9 us)
Async XLA Ops:
  11.1 17.6 %all-to-all-start.1 = ((s32[16,1,32]{2,1,0:T(1,128)}), s32[16,1,32]{2,1,0:T(1,128)S(1)}, u32[]{:S(2)}, u32[]{:S(2)}) async-start(s32[16,1,32]{2,1,0:T(1,128)} %all_to_all.24), calls=%async_computation.1 | async-start | bytes 16384 | tf_op jit(solution)/shard_map/all_to_all | solution.py:565
  33.3 26.1 %all-to-all-start.2 = ((bf16[16,32,768]{2,1,0:T(8,128)(2,1)}), bf16[16,32,768]{2,1,0:T(8,128)(2,1)S(1)}, u32[]{:S(2)}, u32[]{:S(2)}) async-start(bf16[16,32,768]{2,1,0:T(8,128)(2,1)} %bitcast.9), calls=%async_computation.2 | async-start | bytes 1572864 | tf_op jit(solution)/shard_map/all_to_all | solution.py:571
  40.3 5.3 collective-permute-start.2
  46.3 5.1 collective-permute-start.3
  52.1 8.7 collective-permute-start.4
  59.4 8.4 collective-permute-start.7
  61.4 5.2 collective-permute-start.5
  71.9 72.6 %all-gather.12.cloned.1.call-start = ((), (), s32[]{:S(2)}) async-start(), calls=%async_computation.12 | async-start | bytes 6488064 | tf_op jit(solution)/shard_map/all_gather | solution.py:499
  72.5 176.6 %all-gather.10.cloned.1.call-start = ((), (), s32[]{:S(2)}) async-start(), calls=%async_computation.11 | async-start | bytes 14598144 | tf_op jit(solution)/shard_map/all_gather | solution.py:498
  75.0 1.3 collective-permute-start.6
  272.9 4.4 collective-permute-start.8
  302.6 4.3 collective-permute-start.9
  327.4 3.4 collective-permute-start.10
  356.2 3.5 collective-permute-start.11
  361.7 34.4 %collective-permute-start.13 = (bf16[512,768]{1,0:T(8,128)(2,1)}, bf16[512,768]{1,0:T(8,128)(2,1)S(1)}, u32[]{:S(2)}, u32[]{:S(2)}) collective-permute-start(bf16[512,768]{1,0:T(8,128)(2,1)} %get-tuple-element.419), channel_id=1, source_target_pairs={{16,0},{17,1},{18,2},{19,3},{20,4},{21,5},{22,6},{23,7},{24,8},{25... | collective-permute-start | bytes 2359304 | tf_op jit(solution)/shard_map/ppermute | solution.py:695
  421.3 4.5 collective-permute-start.14
  461.9 3.4 collective-permute-start.15
  490.9 3.2 collective-permute-start.16
  559.8 4.4 collective-permute-start.1
  565.2 23.5 %all-to-all-start = ((bf16[16,32,768]{2,1,0:T(8,128)(2,1)}), bf16[16,32,768]{2,1,0:T(8,128)(2,1)S(1)}, u32[]{:S(2)}, u32[]{:S(2)}) async-start(bf16[16,32,768]{2,1,0:T(8,128)(2,1)} %bitcast.2), calls=%async_computation | async-start | bytes 1572864 | tf_op jit(solution)/shard_map/cond/branch_0_fun/all_to_all | solution.py:913
  592.0 121.2 %reduce-scatter.5.cloned.1.call-start = ((), (), s32[]{:S(2)}) async-start(), calls=%async_computation.14 | async-start | bytes 6488064 | tf_op jit(solution)/shard_map/reduce_scatter | solution.py:868
  592.6 289.7 %reduce-scatter.3.cloned.1.call-start = ((), (), s32[]{:S(2)}) async-start(), calls=%async_computation.13 | async-start | bytes 14598144 | tf_op jit(solution)/shard_map/reduce_scatter | solution.py:867
  593.7 36.0 %collective-permute-start.17 = (bf16[3136,512]{1,0:T(8,128)(2,1)}, bf16[3136,512]{1,0:T(8,128)(2,1)}, u32[]{:S(2)}, u32[]{:S(2)}) collective-permute-start(bf16[3136,512]{1,0:T(8,128)(2,1)} %get-tuple-element.429), channel_id=1, source_target_pairs={{0,16},{1,17},{2,18},{3,19},{4,20},{5,21},{6,22},{7,23},{8,24},{9,... | collective-permute-start | bytes 9633800 | tf_op jit(solution)/shard_map/ppermute | solution.py:895
  599.3 14.8 %collective-permute-start.12 = (bf16[512,384]{1,0:T(8,128)(2,1)S(1)}, bf16[512,384]{1,0:T(8,128)(2,1)}, u32[]{:S(2)}, u32[]{:S(2)}) collective-permute-start(bf16[512,384]{1,0:T(8,128)(2,1)S(1)} %slice.142), channel_id=1, source_target_pairs={{16,0},{17,1},{18,2},{19,3},{20,4},{21,5},{22,6},{23,7},{24,8},{25... | collective-permute-start | bytes 1179656 | tf_op jit(solution)/shard_map/ppermute | solution.py:942
  602.1 4.3 collective-permute-start.18
  606.4 4.8 collective-permute-start.19
  611.3 5.0 collective-permute-start.20
  616.3 8.2 collective-permute-start.21
  624.5 3.8 collective-permute-start.22
  629.7 252.6 %copy-start.7 = (f32[24,9216]{1,0:T(8,128)S(1)}, f32[24,9216]{1,0:T(8,128)}, u32[]{:S(2)}) copy-start(f32[24,9216]{1,0:T(8,128)} %param.41) | copy-start | bytes 2654212
  629.7 252.6 %copy-start.15 = (f32[24,9216]{1,0:T(8,128)S(1)}, f32[24,9216]{1,0:T(8,128)}, u32[]{:S(2)}) copy-start(f32[24,9216]{1,0:T(8,128)} %param.42) | copy-start | bytes 2654212
  635.9 248.9 %copy-start.14 = (f32[24,9216]{1,0:T(8,128)S(1)}, f32[24,9216]{1,0:T(8,128)}, u32[]{:S(2)}) copy-start(f32[24,9216]{1,0:T(8,128)} %param.43) | copy-start | bytes 2654212
  (35 other events, 760.0 us)
Sparse Core Ops, SparseCore 1:
  75.8 68.6 all-gather.11
  147.8 101.3 all-gather.9
  598.1 115.1 reduce-scatter.4
  720.3 161.9 reduce-scatter.2

commit v2 on v1

v2 whole, which is shorter than its diff:
```python
import math

import jax
import jax.numpy as jnp
from jax import lax
from jax.experimental import pallas as pl
from jax.experimental.pallas import tpu as pltpu
from jax.sharding import PartitionSpec as P

D = 768
HEADS = 12
HEAD_DIM = 64
QUAD = 4 * HEAD_DIM
QUADS = HEADS // 4
FF = 3072
CH = 1024
PATCH = 196
WINDOW = 208
IMG_DEV = 16
GROUPS_DEV = 32
LONGEST = 32
HALF = D // 2
ROWS = 256
BLOCK = 128
SPAN = BLOCK + LONGEST
SCALE = HEAD_DIM ** (-0.5)
EPS = 1e-05
NEG = -1e30
BOTH = ("section", "dp")
VMEM_BYTES = 58 * 1024 * 1024
bf16 = jnp.bfloat16
f32 = jnp.float32
i32 = jnp.int32


def mm(left, right):
    return jnp.dot(left, right, preferred_element_type=f32)


def mm_rt(left, right):
    return lax.dot_general(left, right, (((1,), (1,)), ((), ())), preferred_element_type=f32)


def mm_lt(left, right):
    return lax.dot_general(left, right, (((0,), (0,)), ((), ())), preferred_element_type=f32)


def normalise(values):
    shifted = values - jnp.mean(values, axis=-1, keepdims=True)
    factor = lax.rsqrt(jnp.mean(shifted * shifted, axis=-1, keepdims=True) + EPS)
    return shifted * factor, factor


def norm_back(incoming, unit, factor, gain):
    scaled = incoming * gain
    mean_grad = jnp.mean(scaled, axis=-1, keepdims=True)
    mean_cross = jnp.mean(scaled * unit, axis=-1, keepdims=True)
    return factor * (scaled - mean_grad - unit * mean_cross)


GELU_C = math.sqrt(2.0 / math.pi)


def gelu_parts(values):
    square = values * values
    bend = jnp.tanh(GELU_C * values * (1.0 + 0.044715 * square))
    half = 0.5 * (1.0 + bend)
    slope = half + 0.5 * values * (1.0 - bend * bend) * (GELU_C * (1.0 + 3 * 0.044715 * square))
    return values * half, slope


def gelu_only(values):
    bend = jnp.tanh(GELU_C * values * (1.0 + 0.044715 * (values * values)))
    return 0.5 * values * (1.0 + bend)


def head_masks(dtype, width=QUAD):
    lanes = lax.broadcasted_iota(i32, (1, width), 1) // HEAD_DIM
    return [jnp.where(lanes == h, 1.0, 0.0).astype(dtype) for h in range(width // HEAD_DIM)]


def spread_heads(rows, masks):
    return jnp.concatenate([rows * m for m in masks], axis=0)


def join_heads(stacked, masks):
    count = stacked.shape[0] // len(masks)
    total = stacked[:count] * masks[0]
    for h in range(1, len(masks)):
        total = total + stacked[h * count : (h + 1) * count] * masks[h]
    return total


def softmax(scores, allowed):
    scores = jnp.where(allowed, scores * SCALE, NEG)
    weights = jnp.exp(scores - jnp.max(scores, axis=-1, keepdims=True))
    return weights * (1.0 / jnp.sum(weights, axis=-1, keepdims=True))


def one_hot_cols(index_col, width):
    places = lax.broadcasted_iota(i32, (index_col.shape[0], width), 1)
    return jnp.where(places == index_col, 1.0, 0.0).astype(bf16)


def one_hot_rows(index_row, height, offset=0):
    places = lax.broadcasted_iota(i32, (height, index_row.shape[1]), 0) + offset
    return jnp.where(places == index_row, 1.0, 0.0).astype(bf16)


def join_halves(target, low_ref, high_ref):
    count = low_ref.shape[0]
    target[:count, :] = low_ref[...]
    target[count : 2 * count, :] = high_ref[...]


def key_span(first):
    return pl.multiple_of(jnp.maximum(first - LONGEST, 0), LONGEST)


def self_allowed(start_rows, first, key_first):
    rows = lax.broadcasted_iota(i32, (BLOCK, SPAN), 0) + first
    keys = lax.broadcasted_iota(i32, (BLOCK, SPAN), 1) + key_first
    allowed = (keys <= rows) & (keys >= start_rows)
    return jnp.concatenate([jnp.where(allowed, 1, 0)] * 4, axis=0) > 0


def chunks_of(count, size, body):
    def step(index, carry):
        body(pl.multiple_of(index * size, size))
        return carry

    lax.fori_loop(0, count, step, 0)


def text_first(
    blocks, embed, start, pack, vecs,
    qkv_lo, qkv_hi, out_lo, out_hi, cq_lo, cq_hi,
    qkv_rows, mix_rows, resid_one, slots_a, slots_b,
    w_qkv, w_out, w_cq, queries,
):
    count = blocks[0]
    join_halves(w_qkv, qkv_lo, qkv_hi)
    join_halves(w_out, out_lo, out_hi)
    join_halves(w_cq, cq_lo, cq_hi)
    queries[...] = jnp.zeros_like(queries)
    masks = head_masks(bf16)
    masks_f = head_masks(f32)

    def project(first):
        rows = pl.ds(first, ROWS)
        unit, _ = normalise(embed[rows, :].astype(f32))
        normed = (unit * vecs[0:1, :] + vecs[1:2, :]).astype(bf16)
        for third in range(3):
            columns = slice(third * D, (third + 1) * D)
            qkv_rows[rows, columns] = mm(normed, w_qkv[:, columns]).astype(bf16)

    def attend(first):
        rows = pl.ds(first, BLOCK)
        key_first = key_span(first)
        span = pl.ds(key_first, SPAN)
        allowed = self_allowed(start[rows, :], first, key_first)
        for quad in range(QUADS):
            lanes, keys, values = quad_lanes(quad)
            query = spread_heads(qkv_rows[rows, lanes], masks)
            shares = softmax(mm_rt(query, qkv_rows[span, keys]), allowed)
            mixed = mm(shares.astype(bf16), qkv_rows[span, values])
            mix_rows[rows, lanes] = join_heads(mixed, masks_f).astype(bf16)

    def finish(first):
        rows = pl.ds(first, ROWS)
        resid = embed[rows, :].astype(f32) + mm(mix_rows[rows, :], w_out[...])
        resid_one[rows, :] = resid
        unit, _ = normalise(resid)
        normed = (unit * vecs[2:3, :] + vecs[3:4, :]).astype(bf16)
        queries[rows, :] = mm(normed, w_cq[...]).astype(bf16)

    chunks_of(count, ROWS, project)
    chunks_of(count * (ROWS // BLOCK), BLOCK, attend)
    chunks_of(count, ROWS, finish)
    packed = mm(one_hot_cols(pack[...], queries.shape[0]), queries[...]).astype(bf16)
    slots_a[...] = packed[:, :HALF]
    slots_b[...] = packed[:, HALF:]


def quad_lanes(quad):
    return [slice(part * D + quad * QUAD, part * D + (quad + 1) * QUAD) for part in range(3)]


def text_middle(
    blocks, mix_a, mix_b, take, pack, resid_one, cotangent, vecs, up_bias,
    cout_lo, cout_hi, up_lo, up_hi, down_part,
    block_out, grad_two, late_lo, late_hi, slots_a, slots_b,
    vec_grad, up_bias_grad,
    w_cout, w_up, mixed, normed, normed_t, factor_s, total, back, grad_down_t,
    up_sum, down_sum, up_buffer, down_buffer, w_down_t, sems,
):
    step = pl.program_id(0)
    last = pl.num_programs(0) - 1
    count = blocks[0]
    wide = w_up.shape[1]
    by_owner = down_buffer.shape[1] != D

    def copies(chunk):
        slot = chunk % 2
        place = (chunk + 1) % 4
        columns = slice(chunk * wide, (chunk + 1) * wide)
        pairs = [
            (up_buffer.at[slot, :HALF, :], late_lo.at[:, columns]),
            (up_buffer.at[slot, HALF:, :], late_hi.at[:, columns]),
        ]
        if by_owner:
            height = down_buffer.shape[1]
            rows = slice(place % 2 * height, (place % 2 + 1) * height)
            target = late_lo if place < 2 else late_hi
            pairs.append((down_buffer.at[slot], target.at[rows, CH + FF :]))
        else:
            columns = slice(CH + FF + place * wide, CH + FF + (place + 1) * wide)
            pairs.append((down_buffer.at[slot, :HALF, :], late_lo.at[:, columns]))
            pairs.append((down_buffer.at[slot, HALF:, :], late_hi.at[:, columns]))
        return [
            pltpu.make_async_copy(source, target, sems.at[slot, i])
            for i, (source, target) in enumerate(pairs)
        ]

    for chunk in (0, 1):

        @pl.when(step == chunk + 2)
        def _():
            for copy in copies(chunk):
                copy.wait()

    @pl.when(step == 0)
    def _():
        w_cout[:HALF, :] = cout_lo[:, :D]
        w_cout[HALF:, :] = cout_hi[:, :D]
        normed[...] = jnp.zeros_like(normed)
        block_out[...] = jnp.zeros_like(block_out)
        vec_grad[...] = jnp.zeros_like(vec_grad)

        def begin(first):
            rows = pl.ds(first, ROWS)
            places = lax.broadcasted_iota(i32, (ROWS, take.shape[1]), 0) + first
            hit = jnp.where(places == take[...], 1.0, 0.0).astype(bf16)
            mixed[rows, :HALF] = mm(hit, mix_a[...]).astype(bf16)
            mixed[rows, HALF:] = mm(hit, mix_b[...]).astype(bf16)
            resid_two = resid_one[rows, :] + mm(mixed[rows, :], w_cout[...])
            unit, factor = normalise(resid_two)
            grad_two[rows, :] = unit
            factor_s[rows, :] = factor
            low = (unit * vecs[0:1, :] + vecs[1:2, :]).astype(bf16)
            normed[rows, :] = low
            normed_t[:, rows] = low.T
            total[rows, :] = resid_two + vecs[2:3, :]
            back[rows, :] = jnp.zeros((ROWS, D), f32)
            grad_down_t[:, rows] = cotangent[rows, :].T

        chunks_of(count, ROWS, begin)

    @pl.when(step < last)
    def _():
        join_halves(w_up, up_lo, up_hi)
        parts = wide // 128
        if by_owner:
            height = down_buffer.shape[1] // parts
            for i in range(0, parts, 2):
                pair = down_part[i * height : (i + 2) * height, :].astype(f32)
                for h in range(2):
                    one = pair[h * height : (h + 1) * height]
                    one = jnp.concatenate([one[:, j : j + 128] for j in range(0, CH + FF, 128)], axis=0)
                    w_down_t[:, (i + h) * 128 : (i + h + 1) * 128] = one.astype(bf16)
        else:
            w_down_t[...] = down_part[...]
        up_sum[...] = jnp.zeros_like(up_sum)
        down_sum[...] = jnp.zeros_like(down_sum)
        up_bias_grad[...] = jnp.zeros_like(up_bias_grad)

        def forward_back(first):
            rows = pl.ds(first, ROWS)
            act, slope = gelu_parts(mm(normed[rows, :], w_up[...]) + up_bias[...])
            act = act.astype(bf16)
            total[rows, :] += mm_rt(act, w_down_t[...])
            grad_up = (mm(cotangent[rows, :], w_down_t[...]) * slope).astype(bf16)
            up_bias_grad[...] += jnp.sum(grad_up.astype(f32), axis=0, keepdims=True)
            up_sum[...] += mm(normed_t[:, rows], grad_up)
            down_sum[...] += mm(grad_down_t[:, rows], act)
            back[rows, :] += mm_rt(grad_up, w_up[...])

        chunks_of(count, ROWS, forward_back)
        slot = step % 2
        up_buffer[slot] = up_sum[...].astype(bf16)
        if by_owner:
            pieces = [
                jnp.concatenate(
                    [down_sum[j : j + height, first : first + 128] for j in range(0, D, height)],
                    axis=1,
                )
                for first in range(0, wide, 128)
            ]
            for i in range(0, parts, 2):
                pair = jnp.concatenate(pieces[i : i + 2], axis=0).astype(bf16)
                down_buffer[slot, i * height : (i + 2) * height, :] = pair
        else:
            down_buffer[slot] = down_sum[...].astype(bf16)

    for chunk in range(3):

        @pl.when(step == chunk)
        def _():
            for copy in copies(chunk):
                copy.start()

    @pl.when(step == last)
    def _():
        up_sum[:, :D] = jnp.zeros((D, D), f32)

        def end(first):
            rows = pl.ds(first, ROWS)
            block_out[rows, :] = total[rows, :].astype(bf16)
            incoming, unit = back[rows, :], grad_two[rows, :]
            vec_grad[0:1, :] += jnp.sum(incoming * unit, axis=0, keepdims=True)
            vec_grad[1:2, :] += jnp.sum(incoming, axis=0, keepdims=True)
            grad = norm_back(incoming, unit, factor_s[rows, :], vecs[0:1, :])
            grad = cotangent[rows, :].astype(f32) + grad
            grad_two[rows, :] = grad
            grad = grad.astype(bf16)
            up_sum[:, :D] += mm_lt(mixed[rows, :], grad)
            normed[rows, :] = mm_rt(grad, w_cout[...]).astype(bf16)

        chunks_of(count, ROWS, end)
        slot = step % 2
        up_buffer[slot, :, :D] = up_sum[:, :D].astype(bf16)
        up_buffer[slot, :, D:] = jnp.zeros((D, wide - D), bf16)
        down_buffer[slot] = jnp.zeros(down_buffer.shape[1:], bf16)
        for copy in copies(3):
            copy.start()
        packed = mm(one_hot_cols(pack[...], normed.shape[0]), normed[...]).astype(bf16)
        slots_a[...] = packed[:, :HALF]
        slots_b[...] = packed[:, HALF:]
        for chunk in (2, 3):
            for copy in copies(chunk):
                copy.wait()


def text_last(
    blocks, grad_a, grad_b, take, place, grad_two, resid_one, embed, qkv_rows, mix_rows, start, vecs,
    qkv_lo, qkv_hi, out_lo, out_hi, cq_lo, cq_hi,
    grad_embed, rows_a, rows_b, grad_lo, grad_hi, vec_grad,
    grad_mix, grad_queries, total, sums, grad_one,
):
    count = blocks[0]

    def keep(first, value):
        low = value.astype(bf16)
        width = value.shape[1]
        grad_lo[:, first : first + width] = low[:HALF]
        grad_hi[:, first : first + width] = low[HALF:]

    def turned_back(rows, lo, hi):
        return jnp.concatenate([mm_rt(rows, lo[...]), mm_rt(rows, hi[...])], axis=1)

    masks = head_masks(bf16)
    masks_f = head_masks(f32)
    vec_grad[...] = jnp.zeros_like(vec_grad)
    total[...] = jnp.zeros_like(total)
    sums[...] = jnp.zeros_like(sums)
    grad_embed[...] = jnp.zeros_like(grad_embed)

    def begin(first):
        rows = pl.ds(first, ROWS)
        places = lax.broadcasted_iota(i32, (ROWS, take.shape[1]), 0) + first
        hit = jnp.where(places == take[...], 1.0, 0.0).astype(bf16)
        grad_q = jnp.concatenate([mm(hit, grad_a[...]), mm(hit, grad_b[...])], axis=1).astype(bf16)
        unit, factor = normalise(resid_one[rows, :])
        normed = (unit * vecs[2:3, :] + vecs[3:4, :]).astype(bf16)
        sums[:, :D] += mm_lt(normed, grad_q)
        incoming = turned_back(grad_q, cq_lo, cq_hi)
        vec_grad[2:3, :] += jnp.sum(incoming * unit, axis=0, keepdims=True)
        vec_grad[3:4, :] += jnp.sum(incoming, axis=0, keepdims=True)
        grad = grad_two[rows, :] + norm_back(incoming, unit, factor, vecs[2:3, :])
        grad_one[rows, :] = grad
        grad = grad.astype(bf16)
        sums[:, D : 2 * D] += mm_lt(mix_rows[rows, :], grad)
        grad_mix[rows, :] = turned_back(grad, out_lo, out_hi).astype(bf16)

    def attend(first):
        rows = pl.ds(first, BLOCK)
        key_first = key_span(first)
        span = pl.ds(key_first, SPAN)
        allowed = self_allowed(start[rows, :], first, key_first)
        for quad in range(QUADS):
            lanes, keys, values = quad_lanes(quad)
            query = spread_heads(qkv_rows[rows, lanes], masks)
            grad = spread_heads(grad_mix[rows, lanes], masks)
            key_rows = qkv_rows[span, keys]
            shares = softmax(mm_rt(query, key_rows), allowed)
            grad_shares = mm_rt(grad, qkv_rows[span, values])
            inner = jnp.sum(grad_shares * shares, axis=-1, keepdims=True)
            grad_scores = (shares * (grad_shares - inner)).astype(bf16)
            back = join_heads(mm(grad_scores, key_rows), masks_f) * SCALE
            grad_queries[rows, lanes] = back.astype(bf16)
            later = slice(D + quad * QUAD, D + (quad + 1) * QUAD)
            total[span, lanes] += mm_lt(grad_scores, query) * SCALE
            total[span, later] += mm_lt(shares.astype(bf16), grad)

    def end(first):
        rows = pl.ds(first, ROWS)
        unit, factor = normalise(embed[rows, :].astype(f32))
        normed = (unit * vecs[0:1, :] + vecs[1:2, :]).astype(bf16)
        grad = jnp.concatenate([grad_queries[rows, :], total[rows, :].astype(bf16)], axis=1)
        for third in range(3):
            columns = slice(third * D, (third + 1) * D)
            sums[:, columns] += mm_lt(normed, grad[:, columns])
        incoming = turned_back(grad, qkv_lo, qkv_hi)
        vec_grad[0:1, :] += jnp.sum(incoming * unit, axis=0, keepdims=True)
        vec_grad[1:2, :] += jnp.sum(incoming, axis=0, keepdims=True)
        grad = grad_one[rows, :] + norm_back(incoming, unit, factor, vecs[0:1, :])
        grad_embed[rows, :] = grad.astype(bf16)

    chunks_of(count, ROWS, begin)
    keep(4 * D, sums[:, :D])
    keep(3 * D, sums[:, D : 2 * D])
    chunks_of(count * (ROWS // BLOCK), BLOCK, attend)
    sums[...] = jnp.zeros_like(sums)
    chunks_of(count, ROWS, end)
    keep(0, sums[...])
    half = rows_a.shape[0]
    rows_a[...] = mm(one_hot_rows(place[...], half), grad_embed[...]).astype(bf16)
    rows_b[...] = mm(one_hot_rows(place[...], half, half), grad_embed[...]).astype(bf16)


def unpack_rows(rows_a, rows_b, place, embed):
    count = rows_a.shape[0]
    total = mm(one_hot_cols(place[...], count), rows_a[...])
    total = total + mm(one_hot_cols(place[...] - count, count), rows_b[...])
    embed[...] = total.astype(bf16)


def pack_half(index, rows, packed):
    packed[...] = mm(one_hot_cols(index[...], rows.shape[0]), rows[...].astype(bf16)).astype(bf16)


def join_cotangent(arrival, own, slots_a, slots_b, rows, joined):
    height = joined.shape[0]
    low = mm(one_hot_rows(own[...], height), rows[...].astype(bf16))
    hit = one_hot_rows(arrival[...], height)
    joined[:, :HALF] = (low[:, :HALF] + mm(hit, slots_a[...])).astype(bf16)
    joined[:, HALF:] = (low[:, HALF:] + mm(hit, slots_b[...])).astype(bf16)


def join_output(slot_rows, own, slots, rows, joined):
    height = joined.shape[0]
    total = mm(one_hot_rows(slot_rows[...], height), slots[...])
    total = total + mm(one_hot_cols(own[...], rows.shape[0]), rows[...])
    joined[...] = total.astype(bf16)


def join_kv(w_kv, k_lo, k_hi, v_lo, v_hi):
    for first, (lo, hi) in enumerate(((k_lo, k_hi), (v_lo, v_hi))):
        for part in range(2):
            columns = slice((2 * part + first) * HALF, (2 * part + first + 1) * HALF)
            w_kv[:HALF, columns] = lo[:, part * HALF : (part + 1) * HALF]
            w_kv[HALF:, columns] = hi[:, part * HALF : (part + 1) * HALF]


def stem_forward(
    features, bn, w_patch, patch_bias, k_lo, k_hi, v_lo, v_hi, patches, kv_lo, kv_hi, w_kv
):
    @pl.when(pl.program_id(0) == 0)
    def _():
        join_kv(w_kv, k_lo, k_hi, v_lo, v_hi)

    normed = (features[...].astype(f32) - bn[0:1, :]) * bn[1:2, :]
    hidden = gelu_only(normed * bn[2:3, :] + bn[3:4, :]).astype(bf16)
    rows = (mm(hidden, w_patch[...]) + patch_bias[...]).astype(bf16)
    patches[...] = rows
    kv_lo[...] = mm(rows, w_kv[:, :D]).astype(bf16)
    kv_hi[...] = mm(rows, w_kv[:, D:]).astype(bf16)


def image_window(image):
    first = image * PATCH
    aligned = pl.multiple_of(first // 16 * 16, 16)
    lanes = lax.broadcasted_iota(i32, (1, WINDOW), 1) + (aligned - first)
    return aligned, (lanes >= 0) & (lanes < PATCH)


def cross_forward(queries, kv, mixed):
    masks = head_masks(bf16, HALF)
    masks_f = head_masks(f32, HALF)

    def image(index, carry):
        aligned, allowed = image_window(index)
        window = pl.ds(aligned, WINDOW)
        place = pl.ds(pl.multiple_of(index * LONGEST, LONGEST), LONGEST)
        scores = mm_rt(spread_heads(queries[place, :], masks), kv[window, :HALF])
        shares = softmax(scores, allowed).astype(bf16)
        mixed[place, :] = join_heads(mm(shares, kv[window, HALF:]), masks_f).astype(bf16)
        return carry

    lax.fori_loop(0, IMG_DEV, image, 0, unroll=4)


def cross_backward(queries, grads, kv, grad_q, grad_kv):
    grad_kv[...] = jnp.zeros_like(grad_kv)
    masks = head_masks(bf16, HALF)
    masks_f = head_masks(f32, HALF)

    def image(index, carry):
        aligned, allowed = image_window(index)
        window = pl.ds(aligned, WINDOW)
        place = pl.ds(pl.multiple_of(index * LONGEST, LONGEST), LONGEST)
        query = spread_heads(queries[place, :], masks)
        grad = spread_heads(grads[place, :], masks)
        keys = kv[window, :HALF]
        shares = softmax(mm_rt(query, keys), allowed)
        grad_shares = mm_rt(grad, kv[window, HALF:])
        inner = jnp.sum(grad_shares * shares, axis=-1, keepdims=True)
        grad_scores = (shares * (grad_shares - inner)).astype(bf16)
        grad_q[place, :] = (join_heads(mm(grad_scores, keys), masks_f) * SCALE).astype(bf16)
        grad_kv[window, :HALF] += (mm_lt(grad_scores, query) * SCALE).astype(bf16)
        grad_kv[window, HALF:] += mm_lt(shares.astype(bf16), grad).astype(bf16)
        return carry

    lax.fori_loop(0, IMG_DEV, image, 0, unroll=4)


def stem_backward_kv(
    k_lo, k_hi, v_lo, v_hi, patches, grad_kv_lo, grad_kv_hi,
    grad_rows, grad_lo, grad_hi, bias_sum,
    w_kv, total,
):
    step = pl.program_id(0)

    @pl.when(step == 0)
    def _():
        join_kv(w_kv, k_lo, k_hi, v_lo, v_hi)
        total[...] = jnp.zeros_like(total)
        bias_sum[...] = jnp.zeros_like(bias_sum)

    rows = mm_rt(grad_kv_lo[...], w_kv[:, :D]) + mm_rt(grad_kv_hi[...], w_kv[:, D:])
    rows = rows.astype(bf16)
    grad_rows[...] = rows
    bias_sum[...] += jnp.sum(rows.astype(f32), axis=0, keepdims=True)
    turned = patches[...].T
    total[:, :D] += mm(turned, grad_kv_lo[...])
    total[:, D:] += mm(turned, grad_kv_hi[...])

    @pl.when(step == pl.num_programs(0) - 1)
    def _():
        for first in range(2):
            for part in range(2):
                source = slice((2 * part + first) * HALF, (2 * part + first + 1) * HALF)
                target = slice((2 * first + part) * HALF, (2 * first + part + 1) * HALF)
                grad_lo[:, target] = total[:HALF, source].astype(bf16)
                grad_hi[:, target] = total[HALF:, source].astype(bf16)


def stem_backward(
    features, bn, w_patch, grad_rows, grad_lo, grad_hi, grad_patch_w, sums, patch_acc
):
    step = pl.program_id(0)

    @pl.when(step == 0)
    def _():
        patch_acc[...] = jnp.zeros_like(patch_acc)
        sums[...] = jnp.zeros_like(sums)

    normed = (features[...].astype(f32) - bn[0:1, :]) * bn[1:2, :]
    hidden, slope = gelu_parts(normed * bn[2:3, :] + bn[3:4, :])
    patch_acc[...] += mm_lt(hidden.astype(bf16), grad_rows[...])
    grad_pre = mm_rt(grad_rows[...], w_patch[...]) * slope
    sums[0:1, :] += jnp.sum(grad_pre * normed, axis=0, keepdims=True)
    sums[1:2, :] += jnp.sum(grad_pre, axis=0, keepdims=True)
    grad_low = grad_pre.astype(bf16)
    grad_lo[...] = grad_low[:, : CH // 2]
    grad_hi[...] = grad_low[:, CH // 2 :]

    @pl.when(step == pl.num_programs(0) - 1)
    def _():
        grad_patch_w[...] = patch_acc[...].astype(bf16)


def place_pieces(where_, two, four, two_other, four_other, out, sems):
    dp_index, section = where_[0], where_[1]
    copies = []
    for core, sources in ((1 - section, (two_other, four_other)), (section, (two, four))):
        for z in range(4):
            for far, turn, bits in ((0, 0, 0), (0, 1, 1 + core), (1, 0, 2 - core), (1, 1, 3)):
                target = dp_index ^ (4 * z) ^ bits
                copies.append((sources[far].at[turn, z], out.at[core, target]))
    started = [
        pltpu.make_async_copy(source, target, sems.at[i])
        for i, (source, target) in enumerate(copies)
    ]
    for copy in started:
        copy.start()
    for copy in started:
        copy.wait()


def shape(dims, dtype):
    return jax.ShapeDtypeStruct(dims, dtype)


def whole(array):
    zeros = (0,) * len(array.shape)
    return pl.BlockSpec(array.shape, lambda *_: zeros, pipeline_mode=pl.Buffered(1))


def at(dims, *index):
    return pl.BlockSpec(dims, lambda *_: index)


def call(kernel, steps, in_specs, out_specs, outs, scratch, flops):
    return pl.pallas_call(
        kernel,
        grid=(steps,),
        in_specs=in_specs,
        out_specs=out_specs,
        out_shape=outs,
        scratch_shapes=scratch,
        compiler_params=pltpu.CompilerParams(vmem_limit_bytes=VMEM_BYTES),
        cost_estimate=pl.CostEstimate(flops=flops, bytes_accessed=0, transcendentals=0),
    )


def simple(kernel, inputs, outs, scratch, flops):
    return call(
        kernel,
        1,
        [whole(a) for a in inputs],
        [at(o.shape, *(0,) * len(o.shape)) for o in outs],
        outs,
        scratch,
        flops,
    )(*inputs)


def blank(outs):
    return pl.pallas_call(
        lambda *refs: None,
        out_shape=outs,
        out_specs=[pl.BlockSpec(memory_space=pl.ANY) for _ in outs],
    )()


barrier = lax.optimization_barrier


class Lines:
    def __init__(self, dp, dp_index, section):
        self.dp, self.dp_index, self.section = dp, dp_index, section
        self.is_stem = section == 0
        self.by_hand = dp == 16
        self.x, self.y, self.z = dp_index & 1, dp_index // 2 & 1, dp_index // 4

    def across(self, array, low, high):
        count = self.dp
        pairs = [(d, d ^ low) for d in range(count)]
        pairs += [(count + d, count + (d ^ high)) for d in range(count)]
        return lax.ppermute(array, BOTH, pairs)

    def swap(self, array):
        return lax.ppermute(array, "section", [(0, 1), (1, 0)])

    def gather_line(self, shard):
        return jnp.stack([shard] + [self.across(shard, 4 * k, 4 * k) for k in (1, 2, 3)])

    def gather_first(self, line):
        return jnp.stack([line, self.across(line, 1, 2)])

    def gather_second(self, two):
        return two, self.across(two, 2, 1)

    def gather_place(self, two, four):
        inputs = [two, four, self.swap(two), self.swap(four)]
        any_spec = pl.BlockSpec(memory_space=pl.ANY)
        rows, width = two.shape[2:]
        count = 2 * self.dp
        placed = pl.pallas_call(
            place_pieces,
            in_specs=[pl.BlockSpec(memory_space=pltpu.SMEM)] + [any_spec] * 4,
            out_specs=pl.BlockSpec(memory_space=pltpu.VMEM),
            out_shape=shape((2, self.dp, rows, width), bf16),
            scratch_shapes=[pltpu.SemaphoreType.DMA((count,))],
            compiler_params=pltpu.CompilerParams(vmem_limit_bytes=VMEM_BYTES),
        )(jnp.stack([self.dp_index, self.section]), *inputs)
        return placed.reshape(count * rows, width)

    def share_patch(self, project_low):
        count = self.dp // 2
        half = project_low.shape[0] // 2
        moved = lax.ppermute(project_low[half:], BOTH, [(d, d + count) for d in range(count)])
        mine = jnp.where(self.z < 2, project_low[:half], moved)
        moved = lax.ppermute(mine[half // 2 :], "section", [(0, 1)])
        return jnp.where(self.is_stem, mine[: half // 2], moved)

    def fold_patch(self, part, rows):
        rest = part.shape[0] - rows
        width = D * rest // rows
        tail = [part[rows:, first : first + width] for first in range(0, D, width)]
        return jnp.concatenate([part[:rows], jnp.concatenate(tail)], axis=1)

    def unfold_patch(self, parts):
        count, rows, width = parts.shape
        rest = rows * (width - D) // D
        tail = [parts[:, first : first + rest, D:] for first in range(0, rows, rest)]
        parts = jnp.concatenate([parts[:, :, :D], jnp.concatenate(tail, axis=2)], axis=1)
        parts = parts.reshape(2, 2, self.dp // 2, rows + rest, D)
        return parts.transpose(2, 1, 0, 3, 4).reshape(-1, D)

    def pick(self, places, axis, place):
        return lax.dynamic_index_in_dim(places, place, axis, keepdims=False)

    def first_half(self, terms, flip):
        along_y = [self.pick(stem, 1, self.y ^ flip) for stem, _ in terms]
        along_x = [self.pick(text, 2, self.x ^ flip) for _, text in terms]
        parts = [jnp.where(self.is_stem, *both) for both in zip(along_y, along_x)]
        return jnp.concatenate(parts, axis=-1)

    def second_half(self, terms, got, flip):
        place = jnp.where(self.is_stem, self.x, self.y) ^ flip
        kept = self.pick(self.first_half(terms, 0), 1, place).astype(f32)
        return (kept + self.pick(got, 1, place).astype(f32)).astype(bf16)

    def sum_first(self, terms):
        return self.across(self.first_half(terms, 1), 2, 1)

    def sum_second(self, terms, got):
        return self.across(self.second_half(terms, got, 1), 1, 2)

    def line_of(self, terms, got, got_two):
        kept = self.second_half(terms, got, 0).astype(f32)
        return (kept + got_two.astype(f32)).astype(bf16)

    def sum_line(self, line):
        parts = [self.pick(line, 0, self.z ^ k) for k in (1, 2, 3)]
        return [self.across(p, 4 * k, 4 * k) for k, p in zip((1, 2, 3), parts)]

    def line_total(self, line, parts):
        return self.pick(line, 0, self.z).astype(f32) + sum(part.astype(f32) for part in parts)

    def sum_low_first(self, line):
        return self.across(line, 8, 8)

    def sum_low_last(self, line, got):
        line = (line.astype(f32) + got.astype(f32)).astype(bf16)
        low = self.z & 1
        got = self.across(self.pick(line, 0, 1 - low), 4, 4)
        return self.pick(line, 0, low).astype(f32) + got.astype(f32)

    def scatter_plain(self, w_lo, w_hi, kv_lo, kv_hi, patch):
        def total(term):
            return lax.psum_scatter(term, BOTH, scatter_dimension=0, tiled=True).astype(f32)

        own_w = jnp.concatenate([w_lo, w_hi])
        own_kv = jnp.concatenate([kv_lo, kv_hi])
        own_patch = jnp.concatenate([patch, jnp.zeros((FF, D), bf16)])
        return (
            total(
                jnp.concatenate(
                    [
                        jnp.where(self.is_stem, jnp.zeros_like(own_w), own_w),
                        jnp.where(self.is_stem, own_kv, jnp.zeros_like(own_kv)),
                    ],
                    axis=1,
                )
            ),
            total(jnp.where(self.is_stem, own_patch, jnp.zeros_like(own_patch))),
        )


def sgd_update(gradient, momentum, master, average, step_rate):
    new_momentum = 0.9 * momentum + gradient
    new_master = master - step_rate * (gradient + 0.9 * new_momentum)
    new_average = 0.8 * average + 0.2 * new_master
    return (gradient, new_momentum, new_average, new_master, new_master.astype(bf16))


def per_device(
    features,
    image_group,
    token_ids,
    text_lengths,
    cotangent,
    table_master,
    table_momentum,
    table_average,
    block_master,
    block_momentum,
    block_average,
    project_master,
    project_momentum,
    project_average,
    vector_master,
    vector_momentum,
    vector_average,
):
    dp = lax.axis_size("dp")
    group = lax.axis_size(BOTH)
    dp_index = lax.axis_index("dp")
    section = lax.axis_index("section")
    is_stem = section == 0
    me = section * dp + dp_index
    tokens = token_ids.shape[0]
    image_rows = features.shape[0]
    every_patch = image_rows * dp
    table_rows = table_master.shape[0]
    images = image_group.shape[0]

    lines = Lines(dp, dp_index, section)
    block_low = block_master.astype(bf16)
    project_low = project_master.astype(bf16)
    early = block_low[:, : 7 * D]
    late_low = jnp.concatenate(
        [
            block_low[:, 8 * D :],
            block_low[:, 7 * D : 8 * D],
            jnp.zeros((block_low.shape[0], CH - D), bf16),
        ],
        axis=1,
    )
    project_rows = project_master.shape[0]
    if lines.by_hand:
        patch_part = lines.share_patch(project_low)
        rows = late_low.shape[0]
        down_low = project_low.T.reshape(-1, rows, 128).transpose(1, 0, 2).reshape(rows, CH + FF)
        late_low = jnp.concatenate([down_low, late_low], axis=1)

    def send(block):
        return lax.all_to_all(block, "dp", split_axis=0, concat_axis=0, tiled=True)

    capacity = (2 * IMG_DEV + dp - 1) // dp
    slots = dp * capacity
    destination = image_group // GROUPS_DEV
    by_source = destination.reshape(dp, IMG_DEV)
    order = jnp.arange(IMG_DEV, dtype=i32)
    earlier = order[None, :] < order[:, None]
    rank_all = jnp.sum(
        ((by_source[:, :, None] == by_source[:, None, :]) & earlier[None]).astype(i32), axis=2
    ).reshape(images)
    my_dest = lax.dynamic_slice_in_dim(destination, dp_index * IMG_DEV, IMG_DEV)
    my_rank = lax.dynamic_slice_in_dim(rank_all, dp_index * IMG_DEV, IMG_DEV)
    stem_slot = my_dest * capacity + my_rank
    slot_of_image = jnp.where(
        destination == dp_index,
        jnp.arange(images, dtype=i32) // IMG_DEV * capacity + rank_all,
        -1,
    )
    lengths = text_lengths[0]
    group_ends = jnp.cumsum(lengths)
    group_starts = group_ends - lengths
    places = jnp.arange(tokens, dtype=i32)
    groups = jnp.arange(GROUPS_DEV, dtype=i32)
    named = jnp.any(image_group[None, :] == (dp_index * GROUPS_DEV + groups)[:, None], axis=1)
    within_group = (group_starts[None, :] <= places[:, None]) & (
        places[:, None] < group_ends[None, :]
    )
    token_start = jnp.sum(jnp.where(within_group, group_starts[None, :], 0), axis=1)
    token_named = jnp.any(within_group & named[None, :], axis=1)
    match = slot_of_image[None, :] == jnp.arange(slots, dtype=i32)[:, None]
    slot_group = jnp.max(jnp.where(match, (image_group % GROUPS_DEV)[None, :], -1), axis=1)
    group_hit = slot_group[:, None] == groups[None, :]
    slot_start = jnp.sum(jnp.where(group_hit, group_starts[None, :], 0), axis=1)
    slot_length = jnp.sum(jnp.where(group_hit, lengths[None, :], 0), axis=1)
    within = jnp.arange(LONGEST, dtype=i32)
    slot_rows = jnp.where(
        within[None, :] < slot_length[:, None], slot_start[:, None] + within[None, :], -1
    ).reshape(slots * LONGEST)
    slot_ids = jnp.max(
        jnp.where(slot_rows[:, None] == places[None, :], token_ids[None, :], -1), axis=1
    )

    if lines.by_hand:
        patch_part, slot_ids = barrier((patch_part, slot_ids))
        patch_part = lines.gather_line(lines.fold_patch(patch_part, early.shape[0]))
        early = jnp.concatenate([lines.gather_line(early), patch_part], axis=2)
    got_ids = send(slot_ids.reshape(dp, capacity * LONGEST)).reshape(slots, LONGEST)
    slot_hit = stem_slot[:, None] == jnp.arange(slots, dtype=i32)[None, :]
    image_ids = jnp.max(jnp.where(slot_hit[:, :, None], got_ids[None], -1), axis=1)
    ids = jnp.concatenate([image_ids.reshape(-1), jnp.where(token_named, -1, token_ids)])
    height = ids.shape[0]
    here = ids >= 0
    candidates = jnp.arange(height, dtype=i32)
    before = candidates[None, :] < candidates[:, None]
    row = jnp.sum((before & here[None, :]).astype(i32), axis=1)
    row = jnp.where(here, row, -1)
    row_count = jnp.sum(here.astype(i32))
    row_blocks = ((row_count + ROWS - 1) // ROWS).reshape(1)
    depth = jnp.concatenate(
        [jnp.tile(within, IMG_DEV), places - token_start]
    )
    image_row, own_row = row[: IMG_DEV * LONGEST], row[IMG_DEV * LONGEST :]
    arrival_row = jnp.max(
        jnp.where(slot_hit[:, :, None], image_row.reshape(IMG_DEV, 1, LONGEST), -1), axis=0
    ).reshape(slots * LONGEST)
    chosen = row[None, :] == candidates[:, None]
    start = jnp.max(jnp.where(chosen, (row - depth)[None, :], -1), axis=1)
    start = jnp.where(candidates < row_count, start, candidates)[:, None]

    room = max(16, (2 * tokens + 2 * tokens // 4) // group)
    half_room = dp * room
    owner = ids // table_rows
    same = (ids[:, None] == ids[None, :]) & here[None, :]
    is_first = here & ~jnp.any(same & before, axis=1)
    rank = jnp.sum(
        ((owner[:, None] == owner[None, :]) & before & is_first[None, :]).astype(i32), axis=1
    )
    rounds_here = jnp.max(jnp.where(is_first, rank, 0)) // room + 1
    table_low = table_master.astype(bf16)

    def round_of(turn):
        turn_rank = rank - turn * room
        first_place = jnp.where(
            is_first & (turn_rank >= 0) & (turn_rank < room), owner * room + turn_rank, -1
        )
        place = jnp.max(jnp.where(same, first_place[None, :], -1), axis=1)
        place = jnp.max(jnp.where(chosen, place[None, :], -1), axis=1)
        slot = jnp.arange(half_room, dtype=i32) + section * half_room
        asked = jnp.max(
            jnp.where(first_place[None, :] == slot[:, None], (ids % table_rows)[None, :], -1),
            axis=1,
        )
        return place, asked.reshape(dp, room)

    def serve(asked):
        hit = (asked[:, None] == jnp.arange(table_rows, dtype=i32)[None, :]).astype(bf16)
        served = mm(hit, table_low).astype(bf16)
        return send(served.reshape(dp, room, D)).reshape(half_room, D)

    def unpacked(place, served, served_low):
        return simple(
            unpack_rows,
            [served_low, served, place[:, None]],
            [shape((height, D), bf16)],
            [],
            4 * 10**9,
        )[0]

    rows_f = features.astype(f32)
    local_center = jnp.mean(rows_f, axis=0)
    local_square = jnp.sum(jnp.square(rows_f - local_center), axis=0)
    vector_own = lax.dynamic_update_slice(
        jnp.zeros((vector_master.shape[0] * group,), f32),
        lax.reduce_precision(vector_master, 8, 7),
        (me * vector_master.shape[0],),
    ).reshape(-1, CH)
    state = jnp.concatenate([local_center[None], local_square[None], vector_own])

    def merge(mine, other, step):
        delta = other[0] - mine[0]
        squares = mine[1] + other[1] + delta * delta * (0.5 * image_rows * step)
        return jnp.concatenate(
            [(0.5 * (mine[0] + other[0]))[None], squares[None], mine[2:] + other[2:]]
        )

    def merged(state, first, last, merge):
        step = first
        while step < last:
            other = lax.ppermute(state, "dp", [(i, i ^ step) for i in range(dp)])
            state = merge(state, other, step)
            step *= 2
        return state

    def merge_all(mine, other, step):
        return jnp.concatenate(
            [merge(mine[:-1], other[:-1], step), jnp.maximum(mine[-1:], other[-1:])]
        )

    state = merged(state, 1, 4, merge)
    if lines.by_hand:
        got_ids, state, early = barrier((got_ids, state, early))
        early = lines.gather_first(early)
    place, asked = round_of(0)
    rounds_row = jnp.broadcast_to(rounds_here.astype(f32), (1, CH))
    asked = send(asked).reshape(half_room)
    state = merged(jnp.concatenate([state, rounds_row]), 4, dp, merge_all)
    if lines.by_hand:
        asked, state, early = barrier((asked, state, early))
        early = lines.gather_second(early)
    served = serve(asked)
    served_low = lax.ppermute(served, "section", [(0, 1)])
    rounds_row = merged(state[-1:, :128], 1, 4, lambda mine, other, step: jnp.maximum(mine, other))
    vectors = state[2:-1]
    vector_full = vectors + lax.ppermute(vectors, "section", [(0, 1), (1, 0)])
    arrival_shape = shape((slots * LONGEST, HALF), bf16)
    cot_sent = simple(
        pack_half,
        [slot_rows[:, None], lax.dynamic_slice_in_dim(cotangent, section * HALF, HALF, axis=1)],
        [arrival_shape],
        [],
        3 * 10**9,
    )[0]
    if lines.by_hand:
        served, served_low, state, vector_full, early, rounds_row, cot_sent, late_low = barrier(
            (served, served_low, state, vector_full, early, rounds_row, cot_sent, late_low)
        )
        w_late = w_down = lax.all_gather(late_low, BOTH, axis=0, tiled=True)
    else:
        w_late = lax.all_gather(late_low, BOTH, axis=0, tiled=True)
        project_full = lax.all_gather(project_low, BOTH, axis=0, tiled=True)
        w_down = project_full.T
    center = state[0]
    factor = lax.rsqrt(state[1] / every_patch + EPS)
    rounds = rounds_row[0, 0].astype(i32)
    bn_gain, bn_bias = vector_full[0], vector_full[1]
    flat = vector_full.reshape(-1)
    offset = 2 * CH + D
    patch_bias = flat[2 * CH : offset].reshape(1, D)
    ln_vecs = flat[offset : offset + 6 * D].reshape(6, D)
    up_bias = flat[offset + 6 * D : offset + 6 * D + FF].reshape(1, FF)
    down_bias = flat[offset + 6 * D + FF :].reshape(1, D)
    vecs_outer = ln_vecs[:4]
    vecs_three = jnp.concatenate([ln_vecs[4:], down_bias])
    bn = jnp.stack([center, factor, bn_gain, bn_bias])

    def embed_more(turn, embed):
        place, asked = round_of(turn)
        served = serve(send(asked).reshape(half_room))
        return embed + unpacked(place, served, lax.ppermute(served, "section", [(0, 1)]))

    cot_b = send(cot_sent.reshape(dp, capacity * LONGEST, HALF)).reshape(slots * LONGEST, HALF)
    embed = lax.fori_loop(1, rounds, embed_more, unpacked(place, served, served_low))

    if lines.by_hand:
        w_early = lines.gather_place(*early)
        w_patch = w_early[:, 7 * D :].reshape(2 * dp, -1, w_early.shape[1] - 7 * D)
        w_patch = lines.unfold_patch(w_patch)
        w_early, w_patch, embed, cot_b = barrier((w_early, w_patch, embed, cot_b))
    else:
        w_early, w_patch = lax.all_gather(early, BOTH, axis=0, tiled=True), project_full

    def halves(width, column):
        return [at((HALF, width), 0, column), at((HALF, width), 1, column)]

    qkv_specs = halves(3 * D, 0) + halves(D, 3) + halves(D, 4)
    qkv_inputs = [w_early] * 6
    kv_specs = halves(D, 5) + halves(D, 6)
    kv_inputs = [w_early] * 4
    patch_spec = at((CH, D), 0, 0)
    blocks = 7
    per_block = image_rows // blocks
    qkv_scratch = [
        pltpu.VMEM((D, 3 * D), bf16),
        pltpu.VMEM((D, D), bf16),
        pltpu.VMEM((D, D), bf16),
        pltpu.VMEM((height, D), bf16),
    ]

    def rows_spec(width):
        return pl.BlockSpec((per_block, width), lambda step: (step, 0))

    slot_shape = shape((IMG_DEV * LONGEST, HALF), bf16)
    blocks_spec = pl.BlockSpec(memory_space=pltpu.SMEM)
    pack, take = image_row[:, None], image_row[None, :]
    rows_shape = shape((image_rows, D), bf16)

    text_saved = [
        shape((height, 3 * D), bf16),
        shape((height, D), bf16),
        shape((height, D), f32),
        slot_shape,
        slot_shape,
    ]
    stem_saved = [rows_shape] * 3

    def first_text():
        inputs = [embed, start, pack, vecs_outer]
        done = call(
            text_first,
            1,
            [blocks_spec] + [whole(a) for a in inputs] + qkv_specs,
            [whole(o) for o in text_saved],
            text_saved,
            qkv_scratch,
            15 * 10**9,
        )(row_blocks, *inputs, *qkv_inputs)
        return (*done, *blank(stem_saved))

    def first_stem():
        done = call(
            stem_forward,
            blocks,
            [rows_spec(CH), whole(bn), patch_spec, whole(patch_bias)] + kv_specs,
            [rows_spec(D)] * 3,
            stem_saved,
            [pltpu.VMEM((D, 2 * D), bf16)],
            23 * 10**9,
        )(features, bn, w_patch, patch_bias, *kv_inputs)
        return (*blank(text_saved), *done)

    qkv_rows, mix_rows, resid_one, q_a, q_b, patches, kv_lo, kv_hi = lax.cond(
        is_stem, first_stem, first_text
    )

    kv_moved = lax.ppermute(kv_hi, "section", [(0, 1)])

    def to_cores(block_a, block_b):
        return jnp.where(is_stem, lax.ppermute(block_a, "section", [(1, 0)]), block_b)

    q_here = to_cores(q_a, q_b)
    def cross(kv):
        return call(
            cross_forward,
            1,
            [whole(q_here), whole(kv)],
            [whole(q_here)],
            [slot_shape],
            [],
            8 * 10**9,
        )(q_here, kv)[0]

    mix_b = lax.cond(is_stem, lambda: cross(kv_lo), lambda: cross(kv_moved))

    mix_a = lax.ppermute(mix_b, "section", [(0, 1)])
    cot_a = lax.ppermute(cot_b, "section", [(0, 1)])
    grad_out = simple(
        join_cotangent,
        [arrival_row[None, :], own_row[None, :], cot_a, cot_b, cotangent],
        [shape((height, D), bf16)],
        [],
        4 * 10**9,
    )[0]

    chunks = 3
    wide = FF // chunks
    middle_shapes = [
        shape((height, D), bf16),
        shape((height, D), f32),
        shape((HALF, 2 * (CH + FF)), bf16),
        shape((HALF, 2 * (CH + FF)), bf16),
        slot_shape,
        slot_shape,
        shape((2, D), f32),
        shape((1, FF), f32),
    ]

    def middle_text():
        inputs = [mix_a, mix_b, take, pack, resid_one, grad_out, vecs_three]

        def chunk(step):
            return jnp.minimum(step, chunks - 1)

        if lines.by_hand:
            first_up = (CH + FF) // wide
            down_rows = D // (chunks + 1)
            down_spec = pl.BlockSpec((down_rows, CH + FF), lambda step: (1 + chunk(step), 0))
        else:
            first_up = 0
            down_rows = D
            down_spec = pl.BlockSpec((D, wide), lambda step: (0, 1 + chunk(step)))
        down_width = wide * D // down_rows
        outs = [whole(o) for o in middle_shapes]
        outs[2] = outs[3] = pl.BlockSpec(memory_space=pl.ANY)
        outs[7] = pl.BlockSpec((1, wide), lambda step: (0, chunk(step)))
        return call(
            text_middle,
            chunks + 1,
            [blocks_spec]
            + [whole(a) for a in inputs]
            + [pl.BlockSpec((1, wide), lambda step: (0, chunk(step)))]
            + halves(wide, first_up + chunks)
            + [
                pl.BlockSpec((HALF, wide), lambda step: (0, first_up + chunk(step))),
                pl.BlockSpec((HALF, wide), lambda step: (1, first_up + chunk(step))),
                down_spec,
            ],
            outs,
            middle_shapes,
            [
                pltpu.VMEM((D, D), bf16),
                pltpu.VMEM((D, wide), bf16),
                pltpu.VMEM((height, D), bf16),
                pltpu.VMEM((height, D), bf16),
                pltpu.VMEM((D, height), bf16),
                pltpu.VMEM((height, 1), f32),
                pltpu.VMEM((height, D), f32),
                pltpu.VMEM((height, D), f32),
                pltpu.VMEM((D, height), bf16),
                pltpu.VMEM((D, wide), f32),
                pltpu.VMEM((D, wide), f32),
                pltpu.VMEM((2, D, wide), bf16),
                pltpu.VMEM((2, down_rows, down_width), bf16),
                pltpu.VMEM((D, wide), bf16),
                pltpu.SemaphoreType.DMA((2, 4)),
            ],
            29 * 10**9,
        )(row_blocks, *inputs, up_bias, *[w_late] * 4, w_down)

    (
        block_out, grad_two, late_w_lo, late_w_hi, g_a, g_b, grads_three, grad_up_bias,
    ) = lax.cond(is_stem, lambda: tuple(blank(middle_shapes)), middle_text)
    g_here = to_cores(g_a, g_b)
    g_here, late_w_lo = barrier((g_here, late_w_lo))
    if lines.by_hand:
        late_sum = (lax.ppermute(late_w_lo, "section", [(1, 0)]), late_w_hi)
        late_sum = tuple(w.reshape(4, 2, 2, HALF // dp, w.shape[1]) for w in late_sum)
    else:
        late_term = jnp.concatenate([late_w_lo, late_w_hi])
        late_term = jnp.where(is_stem, jnp.zeros_like(late_term), late_term)
        late_grad = lax.psum_scatter(
            late_term[:, : CH + FF], BOTH, scatter_dimension=0, tiled=True
        )
        down_turned = lax.psum_scatter(
            late_term[:, CH + FF :], BOTH, scatter_dimension=1, tiled=True
        )
    out_here = to_cores(block_out[:, :HALF], block_out[:, HALF:])
    sent = simple(pack_half, [arrival_row[:, None], out_here], [arrival_shape], [], 3 * 10**9)[0]
    g_here, sent = barrier((g_here, sent))
    got_out = send(sent.reshape(dp, capacity * LONGEST, HALF)).reshape(slots * LONGEST, HALF)

    def cross_back(kv):
        return tuple(
            call(
                cross_backward,
                1,
                [whole(q_here), whole(g_here), whole(kv)],
                [whole(q_here), whole(kv)],
                [slot_shape, rows_shape],
                [],
                17 * 10**9,
            )(q_here, g_here, kv)
        )

    grad_here, grad_kv = lax.cond(is_stem, lambda: cross_back(kv_lo), lambda: cross_back(kv_moved))
    if lines.by_hand:
        grad_here, grad_kv, late_sum, got_out = barrier((grad_here, grad_kv, late_sum, got_out))
        late_got = lines.sum_first([late_sum])
    grad_kv_moved = lax.ppermute(grad_kv, "section", [(1, 0)])

    stem_kv_shapes = [
        rows_shape,
        shape((HALF, 2 * D), bf16),
        shape((HALF, 2 * D), bf16),
        shape((1, D), f32),
    ]

    def stem_kv():
        return tuple(
            call(
                stem_backward_kv,
                blocks,
                kv_specs + [rows_spec(D)] * 3,
                [rows_spec(D)] + [at(o.shape, 0, 0) for o in stem_kv_shapes[1:]],
                stem_kv_shapes,
                [pltpu.VMEM((D, 2 * D), bf16), pltpu.VMEM((D, 2 * D), f32)],
                23 * 10**9,
            )(*kv_inputs, patches, grad_kv, grad_kv_moved)
        )

    grad_b = grad_here
    grad_rows, kv_w_lo, kv_w_hi, patch_bias_sum = lax.cond(
        is_stem, stem_kv, lambda: tuple(blank(stem_kv_shapes))
    )
    grad_a = lax.ppermute(grad_b, "section", [(0, 1)])
    grad_a, grad_rows = barrier((grad_a, grad_rows))

    row_shape = shape((half_room, D), bf16)
    text_last_shapes = [
        shape((height, D), bf16),
        row_shape,
        row_shape,
        shape((HALF, 5 * D), bf16),
        shape((HALF, 5 * D), bf16),
        shape((4, D), f32),
    ]
    half_channels = CH // 2
    stem_last_shapes = [
        shape((image_rows, half_channels), bf16),
        shape((image_rows, half_channels), bf16),
        shape((CH, D), bf16),
        shape((2, CH), f32),
    ]

    def last_text():
        inputs = [
            grad_a, grad_b, take, place[None, :], grad_two, resid_one, embed,
            qkv_rows, mix_rows, start, vecs_outer,
        ]
        done = call(
            text_last,
            1,
            [blocks_spec] + [whole(a) for a in inputs] + qkv_specs,
            [whole(o) for o in text_last_shapes],
            text_last_shapes,
            [
                pltpu.VMEM((height, D), bf16),
                pltpu.VMEM((height, D), bf16),
                pltpu.VMEM((height, 2 * D), f32),
                pltpu.VMEM((D, 3 * D), f32),
                pltpu.VMEM((height, D), f32),
            ],
            25 * 10**9,
        )(row_blocks, *inputs, *qkv_inputs)
        return (*done, *blank(stem_last_shapes))

    def last_stem():
        done = call(
            stem_backward,
            blocks,
            [rows_spec(CH), whole(bn), patch_spec, rows_spec(D)],
            [rows_spec(half_channels)] * 2 + [at(o.shape, 0, 0) for o in stem_last_shapes[2:]],
            stem_last_shapes,
            [pltpu.VMEM((CH, D), f32)],
            22 * 10**9,
        )(features, bn, w_patch, grad_rows)
        return (*blank(text_last_shapes), *done)

    (
        grad_embed, rows_low, rows_high, grad_w_lo, grad_w_hi, grads_outer,
        grad_lo, grad_hi, grad_patch_w, bn_sums,
    ) = lax.cond(is_stem, last_stem, last_text)

    gone = jnp.zeros((), f32)
    vector_term = jnp.concatenate(
        [
            jnp.where(is_stem, bn_sums.reshape(-1), gone),
            jnp.where(is_stem, patch_bias_sum.reshape(-1), gone),
            jnp.where(
                is_stem,
                gone,
                jnp.concatenate(
                    [
                        grads_outer.reshape(-1),
                        grads_three.reshape(-1),
                        grad_up_bias.reshape(-1),
                        jnp.sum(cotangent, axis=0),
                    ]
                ),
            ),
        ]
    ).reshape(-1, CH)

    def summed(vector, first, last):
        step = first
        while step < last:
            vector = vector + lax.ppermute(vector, "dp", [(i, i ^ step) for i in range(dp)])
            step *= 2
        return vector

    grad_w_lo, grad_w_hi, kv_w_lo, kv_w_hi = barrier(
        (grad_w_lo, grad_w_hi, kv_w_lo, kv_w_hi)
    )
    if lines.by_hand:
        late_got, grad_w_lo = barrier((late_got, grad_w_lo))
    moved_rows = lax.ppermute(rows_low, "section", [(1, 0)])
    got_hi = lax.ppermute(grad_hi, "section", [(0, 1)])
    block_piece = simple(
        join_output,
        [slot_rows[None, :], own_row[:, None], got_out, out_here],
        [shape((tokens, HALF), bf16)],
        [],
        3 * 10**9,
    )[0]

    def sent_rows():
        return send(jnp.where(is_stem, moved_rows, rows_high).reshape(dp, room, D))

    if lines.by_hand:
        owners = CH // project_rows
        parts = grad_patch_w.reshape(owners, 2, project_rows // 2, D)
        terms = [
            (lax.ppermute(grad_w_lo, "section", [(1, 0)]), grad_w_hi),
            (kv_w_lo, lax.ppermute(kv_w_hi, "section", [(0, 1)])),
        ]
        terms = [
            tuple(w.reshape(4, 2, 2, HALF // dp, w.shape[1]) for w in term) for term in terms
        ]
        patch = (parts[:, 0], lax.ppermute(parts[:, 1], "section", [(0, 1)]))
        patch = [tuple(w.reshape(2, 2, 2, project_rows // 2, D) for w in patch)]
        late_got_two = lines.sum_second([late_sum], late_got)
        terms, patch, moved_rows = barrier((terms, patch, moved_rows))
        got = lines.sum_first(terms)
        patch_got = lines.sum_first(patch)
        got_rows = sent_rows()
        vector_total = summed(vector_term, 1, dp)
        late_line = lines.line_of([late_sum], late_got, late_got_two)
        late_parts = lines.sum_line(late_line)
        got, patch_got, vector_total = barrier((got, patch_got, vector_total))
        got_two = lines.sum_second(terms, got)
        patch_got_two = lines.sum_second(patch, patch_got)
        got_two, patch_got_two, late_parts = barrier((got_two, patch_got_two, late_parts))
        line = lines.line_of(terms, got, got_two)
        line_parts = lines.sum_line(line)
        patch_line = lines.line_of(patch, patch_got, patch_got_two)
        patch_got = lines.sum_low_first(patch_line)
        late_grad = lines.line_total(late_line, late_parts)
        tail_grad = lines.line_total(line, line_parts)
        patch_low = lines.sum_low_last(patch_line, patch_got)
        patch_high = lax.ppermute(patch_low, "section", [(1, 0)])
        down_grad = late_grad[:, CH + FF :].astype(f32).reshape(late_grad.shape[0], -1, 128)
        down_grad = down_grad.transpose(1, 0, 2).reshape(D, 128).T
        project_grad = down_grad + jnp.where(
            is_stem & (dp_index < owners), jnp.concatenate([patch_low, patch_high]), 0.0
        )
    else:
        vector_total = summed(vector_term, 1, dp)
        got_rows = sent_rows()
        tail_grad, patch_grad = lines.scatter_plain(
            grad_w_lo, grad_w_hi, kv_w_lo, kv_w_hi, grad_patch_w
        )
        project_grad = down_turned.astype(f32).T + patch_grad
    late_grad = late_grad.astype(f32)
    block_grad = jnp.concatenate(
        [tail_grad, late_grad[:, FF : FF + D], late_grad[:, :FF]], axis=1
    )
    vector_total = vector_total + lax.ppermute(vector_total, "section", [(0, 1), (1, 0)])
    vector_grad = lax.dynamic_slice_in_dim(
        vector_total.reshape(-1), me * vector_master.shape[0], vector_master.shape[0]
    )

    own_pre = jnp.where(is_stem, grad_lo, got_hi).astype(f32)
    first_channel = section * half_channels

    def own_half(array):
        return lax.dynamic_slice_in_dim(array, first_channel, half_channels, axis=array.ndim - 1)

    own_normed = (own_half(features).astype(f32) - own_half(center)) * own_half(factor)
    own_gain = own_half(bn_gain)
    feature_grad = own_half(factor) * (
        own_pre * own_gain
        - own_gain * own_half(vector_total[1]) / every_patch
        - own_normed * (own_gain * own_half(vector_total[0]) / every_patch)
    )

    def row_sums(asked, rows):
        hit = (jnp.arange(table_rows, dtype=i32)[:, None] == asked[None, :]).astype(bf16)
        return mm(hit, rows.reshape(half_room, D))

    def table_more(turn, total):
        place, asked = round_of(turn)
        slot = jnp.arange(group * room, dtype=i32)
        rows = mm((slot[:, None] == place[None, :]).astype(bf16), grad_embed).astype(bf16)
        moved = lax.ppermute(rows[:half_room], "section", [(1, 0)])
        rows = jnp.where(is_stem, moved, rows[half_room:]).reshape(dp, room, D)
        return total + row_sums(send(asked).reshape(half_room), send(rows))

    root_tokens = math.sqrt(tokens * dp)

    def table_update(total):
        return sgd_update(total, table_momentum, table_master, table_average, 0.05)

    table_new = lax.cond(
        rounds > 1,
        lambda: table_update(lax.fori_loop(1, rounds, table_more, row_sums(asked, got_rows))),
        lambda: table_update(row_sums(asked, got_rows)),
    )
    block_new = sgd_update(
        block_grad, block_momentum, block_master, block_average, 0.5 * D ** (-0.5) / root_tokens
    )
    project_new = sgd_update(
        project_grad,
        project_momentum,
        project_master,
        project_average,
        0.5 * FF ** (-0.5) / root_tokens,
    )
    vector_new = sgd_update(
        vector_grad, vector_momentum, vector_master, vector_average, 0.1 / root_tokens
    )
    return (block_piece, feature_grad, *table_new, *block_new, *project_new, *vector_new)


def solution(mesh):
    rows = P(BOTH, None)
    flat = P(BOTH)
    placed = (
        (P("dp", None), P(), P("dp"), P("dp", None), P("dp", None))
        + (rows,) * 9
        + (flat,) * 3
    )
    return jax.shard_map(
        per_device,
        mesh=mesh,
        in_specs=placed,
        out_specs=(P("dp", "section"), P("dp", "section")) + (rows,) * 15 + (flat,) * 5,
        check_vma=False,
    )
```

time: 903 us -> 623 us (0.69)
  waiting for transfers between devices: 508 us -> 170 us
  blocking collectives: 99 us -> 0 us
  starting transfers between devices: 54.1 us -> 150 us
  other arithmetic: 55.9 us -> 94.2 us
  local copies, waits for them, and re-layouts: 18 us -> 40.1 us
    reduce_scatter x2 -> x0, waiting for transfers between devices: 242 us -> none  [the longest x1 165 us: per_device(): lax.psum_scatter(block_term, BOTH, scatter_dimension=0, tiled=True)]
    all_gather x2 -> x1, waiting for transfers between devices: 173 us -> 9.92 us  [per_device(): w_late = w_down = lax.all_gather(late_low, BOTH, axis=0, tiled=True)]
    all_to_all x4 -> x0, blocking collectives: 99 us -> none  [exchange(): lax.all_to_all(block.reshape(dp, capacity * HALF_ROWS, D), 'dp', split_ax...]
    ppermute x19 -> x51, starting transfers between devices: 29.1 us -> 90.1 us  [the longest x22 37.7 us: across(): return lax.ppermute(array, BOTH, pairs)]
    ppermute x19 -> x51, waiting for transfers between devices: 68.3 us -> 119 us  [the longest x3 49.6 us: to_cores(): lax.ppermute(block_a, 'section', [(1, 0)])]
    all_to_all x3 -> x6, starting transfers between devices: 18.8 us -> 52.9 us  [send(): return lax.all_to_all(block, 'dp', split_axis=0, concat_axis=0, tiled=True)]
    pallas_call x3 -> x5, Pallas kernels: 99.7 us -> 78.5 us  [the longest x1 22.6 us: stem_kv(): call(stem_backward_kv, blocks, kv_specs + [rows_spec(D)] * 3, [rows_spec(...]
    pallas_call x1 -> x5, Pallas kernels: 2.23 us -> 20.8 us  [simple(): call(kernel, 1, [whole(a) for a in inputs], [at(o.shape, *(0,) * len(o.sh...]
  transfers between devices with their start and end apart: 29 -> 61, of which waited for: 22 -> 25; matrix products, arithmetic and copies ran while one was open for 5% -> 18% of each run, Pallas kernels for 0% -> 20%
where the time goes in v2:
time: 623 us; the launch traced here: 611 us
  waiting for transfers between devices  170 us (27%)
  starting transfers between devices  150 us (24%)
  Pallas kernels  122 us (20%)
  other arithmetic  94.2 us (15%)
  local copies, waits for them, and re-layouts  40.1 us (6%)
  between operations  18.9 us (3%)
  matrix products  9.55 us (2%)
    all_to_all x6, starting transfers between devices, send(): return lax.all_to_all(block, 'dp', split_axis=0, concat_axis=0, tiled=True)  52.9 us
    ppermute x3, waiting for transfers between devices, to_cores(): lax.ppermute(block_a, 'section', [(1, 0)])  49.6 us
    ppermute x22, waiting for transfers between devices, across(): return lax.ppermute(array, BOTH, pairs)  47.6 us
    all_to_all x6, waiting for transfers between devices, send(): return lax.all_to_all(block, 'dp', split_axis=0, concat_axis=0, tiled=True)  41 us
    ppermute x22, starting transfers between devices, across(): return lax.ppermute(array, BOTH, pairs)  37.7 us
    pallas_call x1, Pallas kernels, first_stem(): call(stem_forward, blocks, [rows_spec(CH), whole(bn), patch_spec, whole(p...  22.8 us
    pallas_call x1, Pallas kernels, stem_kv(): call(stem_backward_kv, blocks, kv_specs + [rows_spec(D)] * 3, [rows_spec(...  22.6 us
    pallas_call x1, Pallas kernels, last_stem(): call(stem_backward, blocks, [rows_spec(CH), whole(bn), patch_spec, rows_s...  22.5 us
  transfers between devices with their start and end apart: 61, of which 25 were waited for; matrix products, arithmetic and copies ran while one was open for 18% of the time, Pallas kernels for 20%

profile of v2, /device:TPU:0, one launch (start us, length us, event | category | flops | bytes accessed | tf_op | source)
XLA Modules:
  0.0 610.8 jit_solution(18293622119932880071)
XLA Ops:
  41.6 9.7 %all-to-all-start.4 = ((s32[16,1,64]{2,1,0:T(1,128)}), s32[16,1,64]{2,1,0:T(1,128)S(1)}, u32[]{:S(2)}, u32[]{:S(2)}) async-start(s32[16,1,64]{2,1,0:T(1,128)} %all_to_all.54), calls=%async_computation.4 | async-start | bytes 16384 | tf_op jit(solution)/shard_map/all_to_all | solution.py:831
  90.5 5.9 all-to-all-done.5
  112.9 16.9 %all-to-all-done.6 = bf16[16,40,768]{2,1,0:T(8,128)(2,1)S(1)} async-done(((bf16[16,40,768]{2,1,0:T(8,128)(2,1)}), bf16[16,40,768]{2,1,0:T(8,128)(2,1)S(1)}, u32[]{:S(2)}, u32[]{:S(2)}) %all-to-all-start.6) | async-done | bytes 983072 | tf_op jit(solution)/shard_map/all_to_all | solution.py:831
  141.4 5.6 collective-permute-done.19
  158.9 4.8 all-to-all-start.7
  166.4 8.4 %shard_map.337 = bf16[2,16,24,6400]{3,2,1,0:T(8,128)(2,1)} custom-call(s32[2]{0:T(128)} %pad_add_fusion.2.where_, bf16[2,4,24,6400]{3,2,1,0:T(8,128)(2,1)} %pad_maximum_fusion.two, bf16[2,4,24,6400]{3,2,1,0:T(8,128)(2,1)} %collective-permute-done.17.four, bf16[2,4,24,6400]{3,2,1,0:T(8,128)(2,1)} %collective-permute-done.20.two_other, ...), custom_call_target="tpu_custom_call" | custom-call | tf_op jit(solution)/shard_map/pallas_call | solution.py:680
  176.9 9.7 %all-to-all-done.7 = bf16[16,64,384]{2,1,0:T(8,128)(2,1)} async-done(((bf16[16,64,384]{2,1,0:T(8,128)(2,1)}), bf16[16,64,384]{2,1,0:T(8,128)(2,1)}, u32[]{:S(2)}, u32[]{:S(2)}) %all-to-all-start.7) | async-done | bytes 786464 | tf_op jit(solution)/shard_map/all_to_all | solution.py:831
  186.6 23.6 %conditional.17 = (bf16[1024,2304]{1,0:T(8,128)(2,1)}, bf16[1024,768]{1,0:T(8,128)(2,1)}, f32[1024,768]{1,0:T(8,128)}, bf16[512,384]{1,0:T(8,128)(2,1)}, bf16[51...) conditional(s32[]{:T(128)} %convert_element_type.257, ...), branch_computations={%region_26.27_spmd, %region_27.28_spmd} | conditional | flops 23000000512 | bytes 12352 | solution.py:1092
  187.4 22.8 %branch_1_fun.9 = (bf16[3136,768]{1,0:T(8,128)(2,1)}, bf16[3136,768]{1,0:T(8,128)(2,1)}, bf16[3136,768]{1,0:T(8,128)(2,1)}) custom-call(bf16[3136,1024]{1,0:T(8,128)(2,1)} %get-tuple-element.506.features, f32[4,1024]{1,0:T(4,128)S(1)} %get-tuple-element.507.bn, bf16[1024,768]{1,0:T(8,128)(2,1)S(1)} %get-tuple-element.508.w_patch, ...), custom_call_target="tpu_custom_call" | custom-call | flops 23000000512 | tf_op jit(solution)/shard_map/cond/branch_1_fun/pallas_call | solution.py:1081
  223.1 8.5 %conditional.18 = (bf16[512,384]{1,0:T(8,128)(2,1)}) conditional(s32[]{:T(128)} %convert_element_type.257, (bf16[512,384]{1,0:T(8,128)(2,1)S(1)}, bf16[3136,768]{1,0:T(8,128)(2,1)}) %tuple.127, (bf16[512,384]{1,0:T(8,128)(2,1)S(1)}, bf16[3136,768]{1,0:T(8,128)(2,1)}) %tuple.128), branch_computations={%region_28.29_spmd, %region_29.30_spmd} | conditional | flops 8000000000 | bytes 8 | solution.py:1113
  223.1 8.5 %branch_1_fun.10 = bf16[512,384]{1,0:T(8,128)(2,1)} custom-call(bf16[512,384]{1,0:T(8,128)(2,1)S(1)} %get-tuple-element.516.queries, bf16[3136,768]{1,0:T(8,128)(2,1)} %get-tuple-element.517.kv), custom_call_target="tpu_custom_call" | custom-call | flops 8000000000 | tf_op jit(solution)/shard_map/cond/branch_1_fun/pallas_call | solution.py:1103
  236.2 6.5 %shard_map.339 = bf16[1024,768]{1,0:T(8,128)(2,1)} custom-call(s32[1,1024]{1,0:T(1,128)} %broadcast_in_dim_reshape.4.arrival, s32[1,512]{1,0:T(1,128)} %bitcast.251, bf16[1024,384]{1,0:T(8,128)(2,1)} %copy-done.103, bf16[1024,384]{1,0:T(8,128)(2,1)} %bitcast.42.slots_b, f32[512,768]{1,0:T(8,128)} %rows.1), custom_call_target="tpu_custom_call" | custom-call | flops 4000000000 | tf_op jit(solution)/shard_map/pallas_call | solution.py:628
  242.7 9.9 %all-gather.2.cloned.1.call-done = bf16[768,8192]{1,0:T(8,128)(2,1)} async-done(((bf16[24,8192]{1,0:T(8,128)(2,1)}), bf16[768,8192]{1,0:T(8,128)(2,1)}) %all-gather.2.cloned.1.call-update) | async-done | bytes 12582928 | tf_op jit(solution)/shard_map/all_gather | solution.py:998
  257.9 39.5 %collective-permute-done.26 = bf16[512,384]{1,0:T(8,128)(2,1)S(1)} collective-permute-done((bf16[512,384]{1,0:T(8,128)(2,1)}, bf16[512,384]{1,0:T(8,128)(2,1)S(1)}, u32[]{:S(2)}, u32[]{:S(2)}) %collective-permute-start.26) | collective-permute-done | bytes 393248 | tf_op jit(solution)/shard_map/ppermute | solution.py:1099
  303.1 8.6 %collective-permute-done.27 = bf16[1024,384]{1,0:T(8,128)(2,1)} collective-permute-done((bf16[1024,384]{1,0:T(8,128)(2,1)}, bf16[1024,384]{1,0:T(8,128)(2,1)}, u32[]{:S(2)}, u32[]{:S(2)}) %collective-permute-start.27) | collective-permute-done | bytes 786464 | tf_op jit(solution)/shard_map/ppermute | solution.py:1099
  317.4 26.2 %all-to-all-start.8 = ((bf16[16,64,384]{2,1,0:T(8,128)(2,1)}), bf16[16,64,384]{2,1,0:T(8,128)(2,1)S(1)}, u32[]{:S(2)}, u32[]{:S(2)}) async-start(bf16[16,64,384]{2,1,0:T(8,128)(2,1)} %bitcast.231), calls=%async_computation.8 | async-start | bytes 1572864 | tf_op jit(solution)/shard_map/all_to_all | solution.py:831
  343.6 16.8 %conditional.20 = ((bf16[512,384]{1,0:T(8,128)(2,1)S(1)}, bf16[3136,768]{1,0:T(8,128)(2,1)})) conditional(s32[]{:T(128)} %convert_element_type.257, (bf16[512,384]{1,0:T(8,128)(2,1)S(1)}, bf16[512,384]{1,0:T(8,128)(2,1)S(1)}, bf16[3136,768]{1,0:T(8,128)(2,1)}) %tuple.297, (bf16[512,384]{1,0:T(8,128)(2,1)S(1)}, bf16[512,384]{1,0:T(8,128)(2,1)S(1)}, ...), branch_computations={%region_33.34_spmd, %region_34.35_spmd} | conditional | flops 16999999488 | bytes 8 | solution.py:1225
  343.8 16.6 %branch_1_fun.12 = (bf16[512,384]{1,0:T(8,128)(2,1)S(1)}, bf16[3136,768]{1,0:T(8,128)(2,1)}) custom-call(bf16[512,384]{1,0:T(8,128)(2,1)S(1)} %get-tuple-element.531.queries, bf16[512,384]{1,0:T(8,128)(2,1)S(1)} %get-tuple-element.532.grads, bf16[3136,768]{1,0:T(8,128)(2,1)} %get-tuple-element.533.kv), custom_call_target="tpu_custom_call" | custom-call | flops 16999999488 | tf_op jit(solution)/shard_map/cond/branch_1_fun/pallas_call | solution.py:1214
  367.1 5.8 bitcast_select_fusion
  376.6 24.8 %conditional.21 = ((bf16[3136,768]{1,0:T(8,128)(2,1)}, bf16[384,1536]{1,0:T(8,128)(2,1)}, bf16[384,1536]{1,0:T(8,128)(2,1)}, f32[1,768]{1,0:T(1,128)S(1)})) conditional(s32[]{:T(128)} %convert_element_type.257, () %tuple.136, (bf16[768,6400]{1,0:T(8,128)(2,1)}, bf16[3136,768]{1,0:T(8,128)(2,1)}, bf16[3136,768]{1,0:T(8,128)(2,1)}, ...), branch_computations={%region_35.36_spmd, %region_36.37_spmd} | conditional | flops 23000000512 | bytes 19267620 | solution.py:1252
  378.8 22.6 %branch_1_fun.13 = (bf16[3136,768]{1,0:T(8,128)(2,1)}, bf16[384,1536]{1,0:T(8,128)(2,1)}, bf16[384,1536]{1,0:T(8,128)(2,1)}, f32[1,768]{1,0:T(1,128)S(1)}) custom-call(bf16[768,6400]{1,0:T(8,128)(2,1)} %get-tuple-element.534.k_lo.k_hi.v_lo.v_hi, bf16[768,6400]{1,0:T(8,128)(2,1)} %get-tuple-element.534.k_lo.k_hi.v_lo.v_hi, ...), custom_call_target="tpu_custom_call" | custom-call | flops 23000000512 | tf_op jit(solution)/shard_map/cond/branch_1_fun/pallas_call | solution.py:1240
  402.2 23.0 %conditional.22 = (bf16[1024,768]{1,0:T(8,128)(2,1)}, bf16[640,768]{1,0:T(8,128)(2,1)}, bf16[640,768]{1,0:T(8,128)(2,1)}, bf16[384,3840]{1,0:T(8,128)(2,1)}, bf1...) conditional(s32[]{:T(128)} %convert_element_type.257, ...), branch_computations={%region_37.38_spmd, %region_38.39_spmd} | conditional | flops 24999999488 | bytes 8272 | solution.py:1312
  402.6 22.5 %branch_1_fun.15 = (bf16[3136,512]{1,0:T(8,128)(2,1)}, bf16[3136,512]{1,0:T(8,128)(2,1)}, bf16[1024,768]{1,0:T(8,128)(2,1)}, f32[2,1024]{1,0:T(2,128)S(1)}) custom-call(bf16[3136,1024]{1,0:T(8,128)(2,1)} %get-tuple-element.567.features, f32[4,1024]{1,0:T(4,128)S(1)} %get-tuple-element.568.bn, bf16[1024,768]{1,0:T(8,128)(2,1)} %get-tuple-element.569.w_patch, ...), custom_call_target="tpu_custom_call" | custom-call | flops 22000001024 | tf_op jit(solution)/shard_map/cond/branch_1_fun/pallas_call | solution.py:1298
  439.4 7.5 %collective-permute-start.34 = (bf16[384,1536]{1,0:T(8,128)(2,1)}, bf16[384,1536]{1,0:T(8,128)(2,1)S(1)}, u32[]{:S(2)}, u32[]{:S(2)}) collective-permute-start(bf16[384,1536]{1,0:T(8,128)(2,1)} %get-tuple-element.781), channel_id=1, source_target_pairs={{0,16},{1,17},{2,18},{3,19},{4,20},{5,21},{6,22},{7,23},{8,24},{9,... | collective-permute-start | bytes 3538952 | tf_op jit(solution)/shard_map/ppermute | solution.py:1364
  456.7 4.3 collective-permute-done.42
  478.0 23.6 %collective-permute-done.46 = bf16[4,24,8192]{2,1,0:T(8,128)(2,1)} collective-permute-done((bf16[4,24,8192]{2,1,0:T(8,128)(2,1)S(1)}, bf16[4,24,8192]{2,1,0:T(8,128)(2,1)}, u32[]{:S(2)}, u32[]{:S(2)}) %collective-permute-start.46) | collective-permute-done | bytes 1572896 | tf_op jit(solution)/shard_map/ppermute | solution.py:661
  509.5 14.1 %conditional.24 = (f32[1000,768]{1,0:T(8,128)S(1)}, f32[1000,768]{1,0:T(8,128)S(1)}, f32[1000,768]{1,0:T(8,128)S(1)}, f32[1000,768]{1,0:T(8,128)}, bf16[1000,768]{1,0:T(8,128)(2,1)}) conditional(s32[]{:T(128)} %convert_element_type.269, (s32[640]{0:T(1024)S(1)}, bf16[16,40,768]{2,1,0:T(8,128)(2,1)}, f32[1000,768]{1,0:T(8,128)}, ...), branch_computations={%region_40.41_spmd, %region_41.47_spmd} | conditional | flops 3998031872 | bytes 100077136
  509.6 7.3 %fusion.57 = (bf16[1000,768]{1,0:T(8,128)(2,1)}, f32[1000,768]{1,0:T(8,128)}, f32[1000,768]{1,0:T(8,128)S(1)}, f32[1000,768]{1,0:T(8,128)S(1)}) fusion(f32[1000,768]{1,0:T(8,128)} %get-tuple-element.579, f32[1000,768]{1,0:T(8,128)} %get-tuple-element.577, bf16[640,768]{1,0:T(8,128)(2,1)} %bitcast.6, s32[640]{0:T(1024)S(1)} %get-tuple-element.575), kind=kOutput, calls=%fused_computation.246 | convolution fusion | flops 989056000 | bytes 17881600 | tf_op jit(solution)/shard_map/cond/branch_0_fun/dot_general | solution.py:37
  541.0 5.4 subtract_multiply_fusion
  559.5 9.0 %collective-permute-start.53 = (bf16[2,64,768]{2,1,0:T(8,128)(2,1)}, bf16[2,64,768]{2,1,0:T(8,128)(2,1)}, u32[]{:S(2)}, u32[]{:S(2)}) collective-permute-start(bf16[2,64,768]{2,1,0:T(8,128)(2,1)} %fusion.36), channel_id=1, source_target_pairs={{0,8},{1,9},{2,10},{3,11},{4,12},{5,13},{6,14},{7,15},{8,0},{9,1},... | collective-permute-start | bytes 589832 | tf_op jit(solution)/shard_map/ppermute | solution.py:661
  580.0 6.5 %collective-permute-done.50 = bf16[24,5376]{1,0:T(8,128)(2,1)S(1)} collective-permute-done((bf16[24,5376]{1,0:T(8,128)(2,1)}, bf16[24,5376]{1,0:T(8,128)(2,1)S(1)}, u32[]{:S(2)}, u32[]{:S(2)}) %collective-permute-start.50) | collective-permute-done | bytes 258080 | tf_op jit(solution)/shard_map/ppermute | solution.py:661
  586.5 8.8 %collective-permute-done.51 = bf16[24,5376]{1,0:T(8,128)(2,1)S(1)} collective-permute-done((bf16[24,5376]{1,0:T(8,128)(2,1)}, bf16[24,5376]{1,0:T(8,128)(2,1)S(1)}, u32[]{:S(2)}, u32[]{:S(2)}) %collective-permute-start.51) | collective-permute-done | bytes 258080 | tf_op jit(solution)/shard_map/ppermute | solution.py:661
  (501 shorter events, 267.2 us)
Async XLA Ops:
  10.0 63.0 %collective-permute-start.6 = (bf16[24,5376]{1,0:T(8,128)(2,1)}, bf16[24,5376]{1,0:T(8,128)(2,1)}, u32[]{:S(2)}, u32[]{:S(2)}) collective-permute-start(bf16[24,5376]{1,0:T(8,128)(2,1)} %get-tuple-element.1143), channel_id=1, source_target_pairs={{0,4},{1,5},{2,6},{3,7},{4,0},{5,1},{6,2},{7,3},{8,12},{9,13},{10,... | collective-permute-start | bytes 774152 | tf_op jit(solution)/shard_map/ppermute | solution.py:661
  13.0 59.9 %collective-permute-start.7 = (bf16[24,5376]{1,0:T(8,128)(2,1)}, bf16[24,5376]{1,0:T(8,128)(2,1)}, u32[]{:S(2)}, u32[]{:S(2)}) collective-permute-start(bf16[24,5376]{1,0:T(8,128)(2,1)} %get-tuple-element.1143), channel_id=1, source_target_pairs={{0,8},{1,9},{2,10},{3,11},{4,12},{5,13},{6,14},{7,15},{8,0},{9,1},... | collective-permute-start | bytes 774152 | tf_op jit(solution)/shard_map/ppermute | solution.py:661
  15.6 57.4 %collective-permute-start.8 = (bf16[24,5376]{1,0:T(8,128)(2,1)}, bf16[24,5376]{1,0:T(8,128)(2,1)}, u32[]{:S(2)}, u32[]{:S(2)}) collective-permute-start(bf16[24,5376]{1,0:T(8,128)(2,1)} %get-tuple-element.1143), channel_id=1, source_target_pairs={{0,12},{1,13},{2,14},{3,15},{4,8},{5,9},{6,10},{7,11},{8,4},{9,5},... | collective-permute-start | bytes 774152 | tf_op jit(solution)/shard_map/ppermute | solution.py:661
  41.6 16.9 %all-to-all-start.4 = ((s32[16,1,64]{2,1,0:T(1,128)}), s32[16,1,64]{2,1,0:T(1,128)S(1)}, u32[]{:S(2)}, u32[]{:S(2)}) async-start(s32[16,1,64]{2,1,0:T(1,128)} %all_to_all.54), calls=%async_computation.4 | async-start | bytes 16384 | tf_op jit(solution)/shard_map/all_to_all | solution.py:831
  76.2 23.5 %collective-permute-start.14 = (bf16[4,24,6400]{2,1,0:T(8,128)(2,1)}, bf16[4,24,6400]{2,1,0:T(8,128)(2,1)}, u32[]{:S(2)}, u32[]{:S(2)}) collective-permute-start(bf16[4,24,6400]{2,1,0:T(8,128)(2,1)} %maximum_maximum_fusion.1), channel_id=1, source_target_pairs={{0,1},{1,0},{2,3},{3,2},{4,5},{5,4},{6,7},{7,6},{8,9},{9,8},{10,11... | collective-permute-start | bytes 3686408 | tf_op jit(solution)/shard_map/ppermute | solution.py:661
  81.2 16.7 %collective-permute-start.13 = (f32[14,1024]{1,0:T(8,128)}, f32[14,1024]{1,0:T(8,128)}, u32[]{:S(2)}, u32[]{:S(2)}) collective-permute-start(f32[14,1024]{1,0:T(8,128)} %pad_maximum_fusion.6), channel_id=1, source_target_pairs={{0,8},{1,9},{2,10},{3,11},{4,12},{5,13},{6,14},{7,15},{8,0},{9,1},... | collective-permute-start | bytes 172040 | tf_op jit(solution)/shard_map/ppermute | solution.py:960
  105.3 24.5 %all-to-all-start.6 = ((bf16[16,40,768]{2,1,0:T(8,128)(2,1)}), bf16[16,40,768]{2,1,0:T(8,128)(2,1)S(1)}, u32[]{:S(2)}, u32[]{:S(2)}) async-start(bf16[16,40,768]{2,1,0:T(8,128)(2,1)} %bitcast.226), calls=%async_computation.6 | async-start | bytes 1966080 | tf_op jit(solution)/shard_map/all_to_all | solution.py:831
  109.1 143.6 %all-gather.2.cloned.1.call-start = ((), (), s32[]{:S(2)}) async-start(), calls=%async_computation.10 | async-start | bytes 12976128 | tf_op jit(solution)/shard_map/all_gather | solution.py:998
  111.0 36.1 %collective-permute-start.17 = (bf16[2,4,24,6400]{3,2,1,0:T(8,128)(2,1)}, bf16[2,4,24,6400]{3,2,1,0:T(8,128)(2,1)}, u32[]{:S(2)}, u32[]{:S(2)}) collective-permute-start(bf16[2,4,24,6400]{3,2,1,0:T(8,128)(2,1)} %pad_maximum_fusion.two), channel_id=1, source_target_pairs={{0,2},{1,3},{2,0},{3,1},{4,6},{5,7},{6,4},{7,5},{8,10},{9,11},{10,... | collective-permute-start | bytes 7372808 | tf_op jit(solution)/shard_map/ppermute | solution.py:661
  129.8 17.2 %collective-permute-start.15 = (bf16[640,768]{1,0:T(8,128)(2,1)S(1)}, bf16[640,768]{1,0:T(8,128)(2,1)}, u32[]{:S(2)}, u32[]{:S(2)}) collective-permute-start(bf16[640,768]{1,0:T(8,128)(2,1)S(1)} %bitcast.224), channel_id=1, source_target_pairs={{0,16},{1,17},{2,18},{3,19},{4,20},{5,21},{6,22},{7,23},{8,24},{9,... | collective-permute-start | bytes 2949128 | tf_op jit(solution)/shard_map/ppermute | solution.py:982
  158.9 27.6 %all-to-all-start.7 = ((bf16[16,64,384]{2,1,0:T(8,128)(2,1)}), bf16[16,64,384]{2,1,0:T(8,128)(2,1)}, u32[]{:S(2)}, u32[]{:S(2)}) async-start(bf16[16,64,384]{2,1,0:T(8,128)(2,1)} %bitcast.230), calls=%async_computation.7 | async-start | bytes 1572864 | tf_op jit(solution)/shard_map/all_to_all | solution.py:831
  213.6 21.7 %collective-permute-start.25 = (bf16[1024,384]{1,0:T(8,128)(2,1)}, bf16[1024,384]{1,0:T(8,128)(2,1)S(1)}, u32[]{:S(2)}, u32[]{:S(2)}) collective-permute-start(bf16[1024,384]{1,0:T(8,128)(2,1)} %bitcast.42.slots_b), channel_id=1, source_target_pairs={{0,16},{1,17},{2,18},{3,19},{4,20},{5,21},{6,22},{7,23},{8,24},{9,... | collective-permute-start | bytes 2359304 | tf_op jit(solution)/shard_map/ppermute | solution.py:1116
  256.7 40.8 %collective-permute-start.26 = (bf16[512,384]{1,0:T(8,128)(2,1)}, bf16[512,384]{1,0:T(8,128)(2,1)S(1)}, u32[]{:S(2)}, u32[]{:S(2)}) collective-permute-start(bf16[512,384]{1,0:T(8,128)(2,1)} %get-tuple-element.1041), channel_id=1, source_target_pairs={{16,0},{17,1},{18,2},{19,3},{20,4},{21,5},{22,6},{23,7},{24,8},{25... | collective-permute-start | bytes 1179656 | tf_op jit(solution)/shard_map/ppermute | solution.py:1099
  298.2 64.3 %collective-permute-start.28 = (bf16[384,8192]{1,0:T(8,128)(2,1)}, bf16[384,8192]{1,0:T(8,128)(2,1)}, u32[]{:S(2)}, u32[]{:S(2)}) collective-permute-start(bf16[384,8192]{1,0:T(8,128)(2,1)} %get-tuple-element.756), channel_id=1, source_target_pairs={{16,0},{17,1},{18,2},{19,3},{20,4},{21,5},{22,6},{23,7},{24,8},{25... | collective-permute-start | bytes 18874376 | tf_op jit(solution)/shard_map/ppermute | solution.py:1196
  317.4 45.1 %all-to-all-start.8 = ((bf16[16,64,384]{2,1,0:T(8,128)(2,1)}), bf16[16,64,384]{2,1,0:T(8,128)(2,1)S(1)}, u32[]{:S(2)}, u32[]{:S(2)}) async-start(bf16[16,64,384]{2,1,0:T(8,128)(2,1)} %bitcast.231), calls=%async_computation.8 | async-start | bytes 1572864 | tf_op jit(solution)/shard_map/all_to_all | solution.py:831
  372.9 52.3 %collective-permute-start.32 = (bf16[4,2,24,8192]{3,2,0,1:T(8,128)(2,1)}, bf16[4,2,24,8192]{3,2,0,1:T(8,128)(2,1)}, u32[]{:S(2)}, u32[]{:S(2)}) collective-permute-start(bf16[4,2,24,8192]{3,2,0,1:T(8,128)(2,1)} %get-tuple-element.1124), channel_id=1, source_target_pairs={{0,2},{1,3},{2,0},{3,1},{4,6},{5,7},{6,4},{7,5},{8,10},{9,11},{10,... | collective-permute-start | bytes 9437192 | tf_op jit(solution)/shard_map/ppermute | solution.py:661
  374.5 26.9 %collective-permute-start.29 = (bf16[512,384]{1,0:T(8,128)(2,1)S(1)}, bf16[512,384]{1,0:T(8,128)(2,1)S(1)}, u32[]{:S(2)}, u32[]{:S(2)}) collective-permute-start(bf16[512,384]{1,0:T(8,128)(2,1)S(1)} %get-tuple-element.760), channel_id=1, source_target_pairs={{0,16},{1,17},{2,18},{3,19},{4,20},{5,21},{6,22},{7,23},{8,24},{9,... | collective-permute-start | bytes 1179656 | tf_op jit(solution)/shard_map/ppermute | solution.py:1255
  425.2 40.6 %collective-permute-start.33 = (bf16[384,3840]{1,0:T(8,128)(2,1)}, bf16[384,3840]{1,0:T(8,128)(2,1)}, u32[]{:S(2)}, u32[]{:S(2)}) collective-permute-start(bf16[384,3840]{1,0:T(8,128)(2,1)} %get-tuple-element.778), channel_id=1, source_target_pairs={{16,0},{17,1},{18,2},{19,3},{20,4},{21,5},{22,6},{23,7},{24,8},{25... | collective-permute-start | bytes 8847368 | tf_op jit(solution)/shard_map/ppermute | solution.py:1363
  439.4 26.4 %collective-permute-start.34 = (bf16[384,1536]{1,0:T(8,128)(2,1)}, bf16[384,1536]{1,0:T(8,128)(2,1)S(1)}, u32[]{:S(2)}, u32[]{:S(2)}) collective-permute-start(bf16[384,1536]{1,0:T(8,128)(2,1)} %get-tuple-element.781), channel_id=1, source_target_pairs={{0,16},{1,17},{2,18},{3,19},{4,20},{5,21},{6,22},{7,23},{8,24},{9,... | collective-permute-start | bytes 3538952 | tf_op jit(solution)/shard_map/ppermute | solution.py:1364
  446.9 19.0 %collective-permute-start.36 = (bf16[640,768]{1,0:T(8,128)(2,1)}, bf16[640,768]{1,0:T(8,128)(2,1)S(1)}, u32[]{:S(2)}, u32[]{:S(2)}) collective-permute-start(bf16[640,768]{1,0:T(8,128)(2,1)} %get-tuple-element.783), channel_id=1, source_target_pairs={{16,0},{17,1},{18,2},{19,3},{20,4},{21,5},{22,6},{23,7},{24,8},{25... | collective-permute-start | bytes 2949128 | tf_op jit(solution)/shard_map/ppermute | solution.py:1346
  461.0 40.6 %collective-permute-start.46 = (bf16[4,24,8192]{2,1,0:T(8,128)(2,1)S(1)}, bf16[4,24,8192]{2,1,0:T(8,128)(2,1)}, u32[]{:S(2)}, u32[]{:S(2)}) collective-permute-start(bf16[4,24,8192]{2,1,0:T(8,128)(2,1)S(1)} %fusion.28), channel_id=1, source_target_pairs={{0,1},{1,0},{2,3},{3,2},{4,5},{5,4},{6,7},{7,6},{8,9},{9,8},{10,11... | collective-permute-start | bytes 4718600 | tf_op jit(solution)/shard_map/ppermute | solution.py:661
  462.8 77.5 %collective-permute-start.31 = (bf16[3136,512]{1,0:T(8,128)(2,1)}, bf16[3136,512]{1,0:T(8,128)(2,1)}, u32[]{:S(2)}, u32[]{:S(2)}) collective-permute-start(bf16[3136,512]{1,0:T(8,128)(2,1)} %get-tuple-element.770), channel_id=1, source_target_pairs={{0,16},{1,17},{2,18},{3,19},{4,20},{5,21},{6,22},{7,23},{8,24},{9,... | collective-permute-start | bytes 9633800 | tf_op jit(solution)/shard_map/ppermute | solution.py:1347
  472.2 61.5 %collective-permute-start.37 = (bf16[4,2,24,5376]{3,2,0,1:T(8,128)(2,1)}, bf16[4,2,24,5376]{3,2,0,1:T(8,128)(2,1)}, u32[]{:S(2)}, u32[]{:S(2)}) collective-permute-start(bf16[4,2,24,5376]{3,2,0,1:T(8,128)(2,1)} %pad_maximum_fusion.1), channel_id=1, source_target_pairs={{0,2},{1,3},{2,0},{3,1},{4,6},{5,7},{6,4},{7,5},{8,10},{9,11},{10,... | collective-permute-start | bytes 6193160 | tf_op jit(solution)/shard_map/ppermute | solution.py:661
  473.7 35.8 %all-to-all-start.9 = ((bf16[16,40,768]{2,1,0:T(8,128)(2,1)}), bf16[16,40,768]{2,1,0:T(8,128)(2,1)}, u32[]{:S(2)}, u32[]{:S(2)}) async-start(bf16[16,40,768]{2,1,0:T(8,128)(2,1)} %bitcast.73), calls=%async_computation.9 | async-start | bytes 1966080 | tf_op jit(solution)/shard_map/all_to_all | solution.py:831
  504.8 24.9 %collective-permute-start.38 = (bf16[2,2,64,768]{3,2,1,0:T(8,128)(2,1)S(1)}, bf16[2,2,64,768]{3,2,1,0:T(8,128)(2,1)}, u32[]{:S(2)}, u32[]{:S(2)}) collective-permute-start(bf16[2,2,64,768]{3,2,1,0:T(8,128)(2,1)S(1)} %bitcast_select_fusion.6), channel_id=1, source_target_pairs={{0,2},{1,3},{2,0},{3,1},{4,6},{5,7},{6,4},{7,5},{8,10},{9,11},{10,... | collective-permute-start | bytes 1179656 | tf_op jit(solution)/shard_map/ppermute | solution.py:661
  506.9 42.8 %collective-permute-start.47 = (bf16[24,8192]{1,0:T(8,128)(2,1)}, bf16[24,8192]{1,0:T(8,128)(2,1)}, u32[]{:S(2)}, u32[]{:S(2)}) collective-permute-start(bf16[24,8192]{1,0:T(8,128)(2,1)} %get-tuple-element.1133), channel_id=1, source_target_pairs={{0,4},{1,5},{2,6},{3,7},{4,0},{5,1},{6,2},{7,3},{8,12},{9,13},{10,... | collective-permute-start | bytes 1179656 | tf_op jit(solution)/shard_map/ppermute | solution.py:661
  525.3 28.3 %collective-permute-start.48 = (bf16[24,8192]{1,0:T(8,128)(2,1)}, bf16[24,8192]{1,0:T(8,128)(2,1)}, u32[]{:S(2)}, u32[]{:S(2)}) collective-permute-start(bf16[24,8192]{1,0:T(8,128)(2,1)} %get-tuple-element.1132), channel_id=1, source_target_pairs={{0,8},{1,9},{2,10},{3,11},{4,12},{5,13},{6,14},{7,15},{8,0},{9,1},... | collective-permute-start | bytes 1179656 | tf_op jit(solution)/shard_map/ppermute | solution.py:661
  529.7 23.9 %collective-permute-start.49 = (bf16[24,8192]{1,0:T(8,128)(2,1)}, bf16[24,8192]{1,0:T(8,128)(2,1)}, u32[]{:S(2)}, u32[]{:S(2)}) collective-permute-start(bf16[24,8192]{1,0:T(8,128)(2,1)} %get-tuple-element.1131), channel_id=1, source_target_pairs={{0,12},{1,13},{2,14},{3,15},{4,8},{5,9},{6,10},{7,11},{8,4},{9,5},... | collective-permute-start | bytes 1179656 | tf_op jit(solution)/shard_map/ppermute | solution.py:661
  559.5 19.4 %collective-permute-start.53 = (bf16[2,64,768]{2,1,0:T(8,128)(2,1)}, bf16[2,64,768]{2,1,0:T(8,128)(2,1)}, u32[]{:S(2)}, u32[]{:S(2)}) collective-permute-start(bf16[2,64,768]{2,1,0:T(8,128)(2,1)} %fusion.36), channel_id=1, source_target_pairs={{0,8},{1,9},{2,10},{3,11},{4,12},{5,13},{6,14},{7,15},{8,0},{9,1},... | collective-permute-start | bytes 589832 | tf_op jit(solution)/shard_map/ppermute | solution.py:661
  571.9 23.4 %collective-permute-start.51 = (bf16[24,5376]{1,0:T(8,128)(2,1)}, bf16[24,5376]{1,0:T(8,128)(2,1)S(1)}, u32[]{:S(2)}, u32[]{:S(2)}) collective-permute-start(bf16[24,5376]{1,0:T(8,128)(2,1)} %get-tuple-element.1141), channel_id=1, source_target_pairs={{0,8},{1,9},{2,10},{3,11},{4,12},{5,13},{6,14},{7,15},{8,0},{9,1},... | collective-permute-start | bytes 774152 | tf_op jit(solution)/shard_map/ppermute | solution.py:661
  572.9 22.4 %collective-permute-start.52 = (bf16[24,5376]{1,0:T(8,128)(2,1)}, bf16[24,5376]{1,0:T(8,128)(2,1)S(1)}, u32[]{:S(2)}, u32[]{:S(2)}) collective-permute-start(bf16[24,5376]{1,0:T(8,128)(2,1)} %get-tuple-element.1140), channel_id=1, source_target_pairs={{0,12},{1,13},{2,14},{3,15},{4,8},{5,9},{6,10},{7,11},{8,4},{9,5},... | collective-permute-start | bytes 774152 | tf_op jit(solution)/shard_map/ppermute | solution.py:661
  579.9 18.4 %collective-permute-start.54 = (bf16[64,768]{1,0:T(8,128)(2,1)S(1)}, bf16[64,768]{1,0:T(8,128)(2,1)S(1)}, u32[]{:S(2)}, u32[]{:S(2)}) collective-permute-start(bf16[64,768]{1,0:T(8,128)(2,1)S(1)} %dynamic-slice_bitcast_fusion.8), channel_id=1, source_target_pairs={{0,4},{1,5},{2,6},{3,7},{4,0},{5,1},{6,2},{7,3},{8,12},{9,13},{10,... | collective-permute-start | bytes 294920 | tf_op jit(solution)/shard_map/ppermute | solution.py:661
  (132 other events, 1781.1 us)
Sparse Core Ops, SparseCore 0:
  147.2 105.3 all-gather.1

commit v3 on v2

--- a/solution.py
+++ b/solution.py
@@ -1,3 +1,4 @@
+import functools
 import math
 
 import jax
@@ -124,12 +125,26 @@
     return jnp.concatenate([jnp.where(allowed, 1, 0)] * 4, axis=0) > 0
 
 
-def chunks_of(count, size, body):
+def each_block(count, body):
     def step(index, carry):
-        body(pl.multiple_of(index * size, size))
+        body(pl.multiple_of(index * BLOCK, BLOCK))
         return carry
 
     lax.fori_loop(0, count, step, 0)
+
+
+def each_pair(count, body):
+    pairs = count // 2
+
+    def step(index, carry):
+        body(pl.multiple_of(index * ROWS, ROWS), ROWS)
+        return carry
+
+    lax.fori_loop(0, pairs, step, 0)
+
+    @pl.when(count % 2 == 1)
+    def _():
+        body(pl.multiple_of(pairs * ROWS, ROWS), BLOCK)
 
 
 def text_first(
@@ -146,8 +161,8 @@
     masks = head_masks(bf16)
     masks_f = head_masks(f32)
 
-    def project(first):
-        rows = pl.ds(first, ROWS)
+    def project(first, size):
+        rows = pl.ds(first, size)
         unit, _ = normalise(embed[rows, :].astype(f32))
         normed = (unit * vecs[0:1, :] + vecs[1:2, :]).astype(bf16)
         for third in range(3):
@@ -166,17 +181,17 @@
             mixed = mm(shares.astype(bf16), qkv_rows[span, values])
             mix_rows[rows, lanes] = join_heads(mixed, masks_f).astype(bf16)
 
-    def finish(first):
-        rows = pl.ds(first, ROWS)
+    def finish(first, size):
+        rows = pl.ds(first, size)
         resid = embed[rows, :].astype(f32) + mm(mix_rows[rows, :], w_out[...])
         resid_one[rows, :] = resid
         unit, _ = normalise(resid)
         normed = (unit * vecs[2:3, :] + vecs[3:4, :]).astype(bf16)
         queries[rows, :] = mm(normed, w_cq[...]).astype(bf16)
 
-    chunks_of(count, ROWS, project)
-    chunks_of(count * (ROWS // BLOCK), BLOCK, attend)
-    chunks_of(count, ROWS, finish)
+    each_pair(count, project)
+    each_block(count, attend)
+    each_pair(count, finish)
     packed = mm(one_hot_cols(pack[...], queries.shape[0]), queries[...]).astype(bf16)
     slots_a[...] = packed[:, :HALF]
     slots_b[...] = packed[:, HALF:]
@@ -187,12 +202,12 @@
 
 
 def text_middle(
-    blocks, mix_a, mix_b, take, pack, resid_one, cotangent, vecs, up_bias,
+    blocks, mix_a, mix_b, take, pack, arrival, own, resid_one, cotangent, vecs, up_bias,
     cout_lo, cout_hi, up_lo, up_hi, down_part,
-    block_out, grad_two, late_lo, late_hi, slots_a, slots_b,
+    out_lo, out_hi, own_lo, own_hi, grad_two, late, slots_a, slots_b,
     vec_grad, up_bias_grad,
     w_cout, w_up, mixed, normed, normed_t, factor_s, total, back, grad_down_t,
-    up_sum, down_sum, up_buffer, down_buffer, w_down_t, sems,
+    up_sum, down_sum, up_buffer, down_buffer, w_down_t, block_out, sems,
 ):
     step = pl.program_id(0)
     last = pl.num_programs(0) - 1
@@ -204,19 +219,14 @@
         slot = chunk % 2
         place = (chunk + 1) % 4
         columns = slice(chunk * wide, (chunk + 1) * wide)
-        pairs = [
-            (up_buffer.at[slot, :HALF, :], late_lo.at[:, columns]),
-            (up_buffer.at[slot, HALF:, :], late_hi.at[:, columns]),
-        ]
+        pairs = [(up_buffer.at[slot], late.at[:, columns])]
         if by_owner:
             height = down_buffer.shape[1]
-            rows = slice(place % 2 * height, (place % 2 + 1) * height)
-            target = late_lo if place < 2 else late_hi
-            pairs.append((down_buffer.at[slot], target.at[rows, CH + FF :]))
+            rows = slice(place * height, (place + 1) * height)
+            pairs.append((down_buffer.at[slot], late.at[rows, CH + FF :]))
         else:
             columns = slice(CH + FF + place * wide, CH + FF + (place + 1) * wide)
-            pairs.append((down_buffer.at[slot, :HALF, :], late_lo.at[:, columns]))
-            pairs.append((down_buffer.at[slot, HALF:, :], late_hi.at[:, columns]))
+            pairs.append((down_buffer.at[slot], late.at[:, columns]))
         return [
             pltpu.make_async_copy(source, target, sems.at[slot, i])
             for i, (source, target) in enumerate(pairs)
@@ -237,9 +247,9 @@
         block_out[...] = jnp.zeros_like(block_out)
         vec_grad[...] = jnp.zeros_like(vec_grad)
 
-        def begin(first):
-            rows = pl.ds(first, ROWS)
-            places = lax.broadcasted_iota(i32, (ROWS, take.shape[1]), 0) + first
+        def begin(first, size):
+            rows = pl.ds(first, size)
+            places = lax.broadcasted_iota(i32, (size, take.shape[1]), 0) + first
             hit = jnp.where(places == take[...], 1.0, 0.0).astype(bf16)
             mixed[rows, :HALF] = mm(hit, mix_a[...]).astype(bf16)
             mixed[rows, HALF:] = mm(hit, mix_b[...]).astype(bf16)
@@ -251,10 +261,10 @@
             normed[rows, :] = low
             normed_t[:, rows] = low.T
             total[rows, :] = resid_two + vecs[2:3, :]
-            back[rows, :] = jnp.zeros((ROWS, D), f32)
+            back[rows, :] = jnp.zeros((size, D), f32)
             grad_down_t[:, rows] = cotangent[rows, :].T
 
-        chunks_of(count, ROWS, begin)
+        each_pair(count, begin)
 
     @pl.when(step < last)
     def _():
@@ -274,8 +284,8 @@
         down_sum[...] = jnp.zeros_like(down_sum)
         up_bias_grad[...] = jnp.zeros_like(up_bias_grad)
 
-        def forward_back(first):
-            rows = pl.ds(first, ROWS)
+        def forward_back(first, size):
+            rows = pl.ds(first, size)
             act, slope = gelu_parts(mm(normed[rows, :], w_up[...]) + up_bias[...])
             act = act.astype(bf16)
             total[rows, :] += mm_rt(act, w_down_t[...])
@@ -285,7 +295,7 @@
             down_sum[...] += mm(grad_down_t[:, rows], act)
             back[rows, :] += mm_rt(grad_up, w_up[...])
 
-        chunks_of(count, ROWS, forward_back)
+        each_pair(count, forward_back)
         slot = step % 2
         up_buffer[slot] = up_sum[...].astype(bf16)
         if by_owner:
@@ -313,8 +323,8 @@
     def _():
         up_sum[:, :D] = jnp.zeros((D, D), f32)
 
-        def end(first):
-            rows = pl.ds(first, ROWS)
+        def end(first, size):
+            rows = pl.ds(first, size)
             block_out[rows, :] = total[rows, :].astype(bf16)
             incoming, unit = back[rows, :], grad_two[rows, :]
             vec_grad[0:1, :] += jnp.sum(incoming * unit, axis=0, keepdims=True)
@@ -326,16 +336,23 @@
             up_sum[:, :D] += mm_lt(mixed[rows, :], grad)
             normed[rows, :] = mm_rt(grad, w_cout[...]).astype(bf16)
 
-        chunks_of(count, ROWS, end)
+        each_pair(count, end)
         slot = step % 2
         up_buffer[slot, :, :D] = up_sum[:, :D].astype(bf16)
         up_buffer[slot, :, D:] = jnp.zeros((D, wide - D), bf16)
         down_buffer[slot] = jnp.zeros(down_buffer.shape[1:], bf16)
         for copy in copies(3):
             copy.start()
-        packed = mm(one_hot_cols(pack[...], normed.shape[0]), normed[...]).astype(bf16)
-        slots_a[...] = packed[:, :HALF]
-        slots_b[...] = packed[:, HALF:]
+        for index, rows, lo, hi in (
+            (pack, normed, slots_a, slots_b),
+            (arrival, block_out, out_lo, out_hi),
+            (own, block_out, own_lo, own_hi),
+        ):
+            for at_row in range(0, index.shape[0], 512):
+                some = slice(at_row, at_row + 512)
+                packed = mm(one_hot_cols(index[some, :], rows.shape[0]), rows[...]).astype(bf16)
+                lo[some, :] = packed[:, :HALF]
+                hi[some, :] = packed[:, HALF:]
         for chunk in (2, 3):
             for copy in copies(chunk):
                 copy.wait()
@@ -365,9 +382,9 @@
     sums[...] = jnp.zeros_like(sums)
     grad_embed[...] = jnp.zeros_like(grad_embed)
 
-    def begin(first):
-        rows = pl.ds(first, ROWS)
-        places = lax.broadcasted_iota(i32, (ROWS, take.shape[1]), 0) + first
+    def begin(first, size):
+        rows = pl.ds(first, size)
+        places = lax.broadcasted_iota(i32, (size, take.shape[1]), 0) + first
         hit = jnp.where(places == take[...], 1.0, 0.0).astype(bf16)
         grad_q = jnp.concatenate([mm(hit, grad_a[...]), mm(hit, grad_b[...])], axis=1).astype(bf16)
         unit, factor = normalise(resid_one[rows, :])
@@ -402,8 +419,8 @@
             total[span, lanes] += mm_lt(grad_scores, query) * SCALE
             total[span, later] += mm_lt(shares.astype(bf16), grad)
 
-    def end(first):
-        rows = pl.ds(first, ROWS)
+    def end(first, size):
+        rows = pl.ds(first, size)
         unit, factor = normalise(embed[rows, :].astype(f32))
         normed = (unit * vecs[0:1, :] + vecs[1:2, :]).astype(bf16)
         grad = jnp.concatenate([grad_queries[rows, :], total[rows, :].astype(bf16)], axis=1)
@@ -416,12 +433,12 @@
         grad = grad_one[rows, :] + norm_back(incoming, unit, factor, vecs[0:1, :])
         grad_embed[rows, :] = grad.astype(bf16)
 
-    chunks_of(count, ROWS, begin)
+    each_pair(count, begin)
     keep(4 * D, sums[:, :D])
     keep(3 * D, sums[:, D : 2 * D])
-    chunks_of(count * (ROWS // BLOCK), BLOCK, attend)
+    each_block(count, attend)
     sums[...] = jnp.zeros_like(sums)
-    chunks_of(count, ROWS, end)
+    each_pair(count, end)
     keep(0, sums[...])
     half = rows_a.shape[0]
     rows_a[...] = mm(one_hot_rows(place[...], half), grad_embed[...]).astype(bf16)
@@ -447,11 +464,9 @@
     joined[:, HALF:] = (low[:, HALF:] + mm(hit, slots_b[...])).astype(bf16)
 
 
-def join_output(slot_rows, own, slots, rows, joined):
-    height = joined.shape[0]
-    total = mm(one_hot_rows(slot_rows[...], height), slots[...])
-    total = total + mm(one_hot_cols(own[...], rows.shape[0]), rows[...])
-    joined[...] = total.astype(bf16)
+def join_output(slot_rows, slots, own, joined):
+    total = mm(one_hot_rows(slot_rows[...], joined.shape[0]), slots[...])
+    joined[...] = (total + own[...].astype(f32)).astype(bf16)
 
 
 def join_kv(w_kv, k_lo, k_hi, v_lo, v_hi):
@@ -580,22 +595,44 @@
         grad_patch_w[...] = patch_acc[...].astype(bf16)
 
 
-def place_pieces(where_, two, four, two_other, four_other, out, sems):
+def place_pieces(where_, two, four, two_other, four_other, first, second, *scratch, split):
     dp_index, section = where_[0], where_[1]
-    copies = []
-    for core, sources in ((1 - section, (two_other, four_other)), (section, (two, four))):
-        for z in range(4):
-            for far, turn, bits in ((0, 0, 0), (0, 1, 1 + core), (1, 0, 2 - core), (1, 1, 3)):
-                target = dp_index ^ (4 * z) ^ bits
-                copies.append((sources[far].at[turn, z], out.at[core, target]))
-    started = [
-        pltpu.make_async_copy(source, target, sems.at[i])
-        for i, (source, target) in enumerate(copies)
-    ]
-    for copy in started:
-        copy.start()
-    for copy in started:
-        copy.wait()
+    width, all_width = first.shape[-1], two.shape[-1]
+    cuts = (slice(0, width), slice(width, all_width))
+    sems = scratch[-1]
+
+    def pieces(part, jobs):
+        copies = []
+        for core, sources in ((1 - part, (two_other, four_other)), (part, (two, four))):
+            for z in range(4):
+                for far, turn, bits in ((0, 0, 0), (0, 1, 1 + core), (1, 0, 2 - core), (1, 1, 3)):
+                    target = dp_index ^ (4 * z) ^ bits
+                    for cut, place in jobs:
+                        copies.append(
+                            pltpu.make_async_copy(
+                                sources[far].at[turn, z, :, cut],
+                                place.at[core, target],
+                                sems.at[len(copies)],
+                            )
+                        )
+        for copy in copies:
+            copy.start()
+        for copy in copies:
+            copy.wait()
+
+    for part in range(2):
+
+        @pl.when(section == part)
+        def _():
+            if split:
+                out = (second, first)[part]
+                buffer = (scratch[1], scratch[0])[part]
+                pieces(part, [(cuts[1 - part], buffer)])
+                final = pltpu.make_async_copy(buffer, out, sems.at[0])
+                final.start()
+                final.wait()
+            else:
+                pieces(part, [(cuts[0], first), (cuts[1], second)])
 
 
 def shape(dims, dtype):
@@ -672,20 +709,44 @@
     def gather_second(self, two):
         return two, self.across(two, 2, 1)
 
-    def gather_place(self, two, four):
+    def gather_place(self, two, four, text_width):
         inputs = [two, four, self.swap(two), self.swap(four)]
+        split = text_width is not None
         any_spec = pl.BlockSpec(memory_space=pl.ANY)
         rows, width = two.shape[2:]
         count = 2 * self.dp
+        first = text_width if split else CH
+        shapes = [(2, self.dp, rows, w) for w in (first, width - first)]
+        buffers = [pltpu.VMEM(dims, bf16) for dims in shapes] if split else []
+        out_spec = any_spec if split else pl.BlockSpec(memory_space=pltpu.VMEM)
         placed = pl.pallas_call(
-            place_pieces,
+            functools.partial(place_pieces, split=split),
             in_specs=[pl.BlockSpec(memory_space=pltpu.SMEM)] + [any_spec] * 4,
-            out_specs=pl.BlockSpec(memory_space=pltpu.VMEM),
-            out_shape=shape((2, self.dp, rows, width), bf16),
-            scratch_shapes=[pltpu.SemaphoreType.DMA((count,))],
+            out_specs=[out_spec] * 2,
+            out_shape=[shape(dims, bf16) for dims in shapes],
+            scratch_shapes=buffers + [pltpu.SemaphoreType.DMA((2 * count,))],
             compiler_params=pltpu.CompilerParams(vmem_limit_bytes=VMEM_BYTES),
         )(jnp.stack([self.dp_index, self.section]), *inputs)
-        return placed.reshape(count * rows, width)
+        return [p.reshape(count * rows, p.shape[-1]) for p in placed]
+
+    def fold_small(self, stats, vector, rows):
+        first = lax.reduce_precision(stats, 8, 7)
+        second = lax.reduce_precision(stats - first, 8, 7)
+        third = stats - first - second
+        terms = jnp.stack([first, second, third]).astype(bf16).reshape(rows, -1)
+        count = rows * 128 - vector.shape[0]
+        vector = jnp.concatenate([vector.astype(bf16), jnp.zeros((count,), bf16)])
+        return jnp.concatenate([terms, vector.reshape(rows, 128)], axis=1)
+
+    def unfold_small(self, shared, count, each):
+        shared = shared.reshape(2, self.dp, -1, shared.shape[-1])
+        stats = shared[0, :, :, :-128].astype(f32).reshape(self.dp, 3, 2, CH)
+        stats = stats[:, 0] + stats[:, 1] + stats[:, 2]
+        center = jnp.mean(stats[:, 0], axis=0)
+        squares = jnp.sum(stats[:, 1] + each * jnp.square(stats[:, 0] - center), axis=0)
+        lines = (count + 127) // 128
+        vector = shared[:, :, :lines, -128:].reshape(2 * self.dp, lines * 128)[:, :count]
+        return center, squares, vector.reshape(-1).astype(f32)
 
     def share_patch(self, project_low):
         count = self.dp // 2
@@ -822,7 +883,6 @@
     )
     project_rows = project_master.shape[0]
     if lines.by_hand:
-        patch_part = lines.share_patch(project_low)
         rows = late_low.shape[0]
         down_low = project_low.T.reshape(-1, rows, 128).transpose(1, 0, 2).reshape(rows, CH + FF)
         late_low = jnp.concatenate([down_low, late_low], axis=1)
@@ -871,10 +931,22 @@
         jnp.where(slot_rows[:, None] == places[None, :], token_ids[None, :], -1), axis=1
     )
 
+    slot_ids, features = barrier((slot_ids, features))
+    rows_f = features.astype(f32)
+    local_center = jnp.mean(rows_f, axis=0)
+    local_square = jnp.sum(jnp.square(rows_f - local_center), axis=0)
+    state = jnp.stack([local_center, local_square])
+    vector_low = lax.reduce_precision(vector_master, 8, 7)
     if lines.by_hand:
-        patch_part, slot_ids = barrier((patch_part, slot_ids))
-        patch_part = lines.gather_line(lines.fold_patch(patch_part, early.shape[0]))
-        early = jnp.concatenate([lines.gather_line(early), patch_part], axis=2)
+        later = jnp.concatenate(
+            [
+                lines.fold_patch(lines.share_patch(project_low), early.shape[0]),
+                lines.fold_small(state, vector_low, early.shape[0]),
+            ],
+            axis=1,
+        )
+        early = lines.gather_line(early)
+
     got_ids = send(slot_ids.reshape(dp, capacity * LONGEST)).reshape(slots, LONGEST)
     slot_hit = stem_slot[:, None] == jnp.arange(slots, dtype=i32)[None, :]
     image_ids = jnp.max(jnp.where(slot_hit[:, :, None], got_ids[None], -1), axis=1)
@@ -886,7 +958,7 @@
     row = jnp.sum((before & here[None, :]).astype(i32), axis=1)
     row = jnp.where(here, row, -1)
     row_count = jnp.sum(here.astype(i32))
-    row_blocks = ((row_count + ROWS - 1) // ROWS).reshape(1)
+    row_blocks = jnp.maximum((row_count + BLOCK - 1) // BLOCK, 2).reshape(1)
     depth = jnp.concatenate(
         [jnp.tile(within, IMG_DEV), places - token_start]
     )
@@ -937,52 +1009,6 @@
             4 * 10**9,
         )[0]
 
-    rows_f = features.astype(f32)
-    local_center = jnp.mean(rows_f, axis=0)
-    local_square = jnp.sum(jnp.square(rows_f - local_center), axis=0)
-    vector_own = lax.dynamic_update_slice(
-        jnp.zeros((vector_master.shape[0] * group,), f32),
-        lax.reduce_precision(vector_master, 8, 7),
-        (me * vector_master.shape[0],),
-    ).reshape(-1, CH)
-    state = jnp.concatenate([local_center[None], local_square[None], vector_own])
-
-    def merge(mine, other, step):
-        delta = other[0] - mine[0]
-        squares = mine[1] + other[1] + delta * delta * (0.5 * image_rows * step)
-        return jnp.concatenate(
-            [(0.5 * (mine[0] + other[0]))[None], squares[None], mine[2:] + other[2:]]
-        )
-
-    def merged(state, first, last, merge):
-        step = first
-        while step < last:
-            other = lax.ppermute(state, "dp", [(i, i ^ step) for i in range(dp)])
-            state = merge(state, other, step)
-            step *= 2
-        return state
-
-    def merge_all(mine, other, step):
-        return jnp.concatenate(
-            [merge(mine[:-1], other[:-1], step), jnp.maximum(mine[-1:], other[-1:])]
-        )
-
-    state = merged(state, 1, 4, merge)
-    if lines.by_hand:
-        got_ids, state, early = barrier((got_ids, state, early))
-        early = lines.gather_first(early)
-    place, asked = round_of(0)
-    rounds_row = jnp.broadcast_to(rounds_here.astype(f32), (1, CH))
-    asked = send(asked).reshape(half_room)
-    state = merged(jnp.concatenate([state, rounds_row]), 4, dp, merge_all)
-    if lines.by_hand:
-        asked, state, early = barrier((asked, state, early))
-        early = lines.gather_second(early)
-    served = serve(asked)
-    served_low = lax.ppermute(served, "section", [(0, 1)])
-    rounds_row = merged(state[-1:, :128], 1, 4, lambda mine, other, step: jnp.maximum(mine, other))
-    vectors = state[2:-1]
-    vector_full = vectors + lax.ppermute(vectors, "section", [(0, 1), (1, 0)])
     arrival_shape = shape((slots * LONGEST, HALF), bf16)
     cot_sent = simple(
         pack_half,
@@ -992,19 +1018,47 @@
         3 * 10**9,
     )[0]
     if lines.by_hand:
-        served, served_low, state, vector_full, early, rounds_row, cot_sent, late_low = barrier(
-            (served, served_low, state, vector_full, early, rounds_row, cot_sent, late_low)
+        got_ids, early, later, cot_sent = barrier((got_ids, early, later, cot_sent))
+        early = lines.gather_first(early)
+        later = lines.gather_line(later)
+    place, asked = round_of(0)
+    asked = jnp.concatenate([asked, jnp.broadcast_to(rounds_here, (dp, 1))], axis=1)
+    asked = send(asked)
+    if lines.by_hand:
+        asked, early, later, cot_sent = barrier((asked, early, later, cot_sent))
+        early = lines.gather_second(early)
+        later = lines.gather_first(later)
+        cot_b = send(cot_sent.reshape(dp, capacity * LONGEST, HALF))
+        cot_b = cot_b.reshape(slots * LONGEST, HALF)
+    rounds = jnp.max(asked[:, room])
+    asked = asked[:, :room].reshape(half_room)
+    served = serve(asked)
+    served_low = lax.ppermute(served, "section", [(0, 1)])
+    if lines.by_hand:
+        served, served_low, early, later, place, start, late_low, cot_b = barrier(
+            (served, served_low, early, later, place, start, late_low, cot_b)
         )
         w_late = w_down = lax.all_gather(late_low, BOTH, axis=0, tiled=True)
+        later = lines.gather_second(later)
+        w_text, w_kv = lines.gather_place(*early, 5 * D)
+        w_patch, shared = lines.gather_place(*later, None)
+        w_patch = lines.unfold_patch(w_patch.reshape(2 * dp, -1, CH))
+        center, squares, flat = lines.unfold_small(shared, vector_master.shape[0], image_rows)
     else:
+        w_text = lax.all_gather(early[:, : 5 * D], BOTH, axis=0, tiled=True)
+        w_kv = lax.all_gather(early[:, 5 * D :], BOTH, axis=0, tiled=True)
+        cot_b = send(cot_sent.reshape(dp, capacity * LONGEST, HALF))
+        cot_b = cot_b.reshape(slots * LONGEST, HALF)
         w_late = lax.all_gather(late_low, BOTH, axis=0, tiled=True)
         project_full = lax.all_gather(project_low, BOTH, axis=0, tiled=True)
         w_down = project_full.T
-    center = state[0]
-    factor = lax.rsqrt(state[1] / every_patch + EPS)
-    rounds = rounds_row[0, 0].astype(i32)
-    bn_gain, bn_bias = vector_full[0], vector_full[1]
-    flat = vector_full.reshape(-1)
+        w_patch = project_full[:CH]
+        stats = lax.all_gather(state, "dp")
+        center = jnp.mean(stats[:, 0], axis=0)
+        squares = jnp.sum(stats[:, 1] + image_rows * jnp.square(stats[:, 0] - center), axis=0)
+        flat = lax.all_gather(vector_low, BOTH, axis=0, tiled=True)
+    factor = lax.rsqrt(squares / every_patch + EPS)
+    bn_gain, bn_bias = flat[:CH], flat[CH : 2 * CH]
     offset = 2 * CH + D
     patch_bias = flat[2 * CH : offset].reshape(1, D)
     ln_vecs = flat[offset : offset + 6 * D].reshape(6, D)
@@ -1019,24 +1073,18 @@
         served = serve(send(asked).reshape(half_room))
         return embed + unpacked(place, served, lax.ppermute(served, "section", [(0, 1)]))
 
-    cot_b = send(cot_sent.reshape(dp, capacity * LONGEST, HALF)).reshape(slots * LONGEST, HALF)
     embed = lax.fori_loop(1, rounds, embed_more, unpacked(place, served, served_low))
 
     if lines.by_hand:
-        w_early = lines.gather_place(*early)
-        w_patch = w_early[:, 7 * D :].reshape(2 * dp, -1, w_early.shape[1] - 7 * D)
-        w_patch = lines.unfold_patch(w_patch)
-        w_early, w_patch, embed, cot_b = barrier((w_early, w_patch, embed, cot_b))
-    else:
-        w_early, w_patch = lax.all_gather(early, BOTH, axis=0, tiled=True), project_full
+        w_text, w_kv, w_patch, embed = barrier((w_text, w_kv, w_patch, embed))
 
     def halves(width, column):
         return [at((HALF, width), 0, column), at((HALF, width), 1, column)]
 
     qkv_specs = halves(3 * D, 0) + halves(D, 3) + halves(D, 4)
-    qkv_inputs = [w_early] * 6
-    kv_specs = halves(D, 5) + halves(D, 6)
-    kv_inputs = [w_early] * 4
+    qkv_inputs = [w_text] * 6
+    kv_specs = halves(D, 0) + halves(D, 1)
+    kv_inputs = [w_kv] * 4
     patch_spec = at((CH, D), 0, 0)
     blocks = 7
     per_block = image_rows // blocks
@@ -1124,11 +1172,14 @@
 
     chunks = 3
     wide = FF // chunks
+    own_shape = shape((tokens, HALF), bf16)
     middle_shapes = [
-        shape((height, D), bf16),
+        arrival_shape,
+        arrival_shape,
+        own_shape,
+        own_shape,
         shape((height, D), f32),
-        shape((HALF, 2 * (CH + FF)), bf16),
-        shape((HALF, 2 * (CH + FF)), bf16),
+        shape((D, 2 * (CH + FF)), bf16),
         slot_shape,
         slot_shape,
         shape((2, D), f32),
@@ -1136,7 +1187,10 @@
     ]
 
     def middle_text():
-        inputs = [mix_a, mix_b, take, pack, resid_one, grad_out, vecs_three]
+        inputs = [
+            mix_a, mix_b, take, pack, arrival_row[:, None], own_row[:, None],
+            resid_one, grad_out, vecs_three,
+        ]
 
         def chunk(step):
             return jnp.minimum(step, chunks - 1)
@@ -1151,8 +1205,8 @@
             down_spec = pl.BlockSpec((D, wide), lambda step: (0, 1 + chunk(step)))
         down_width = wide * D // down_rows
         outs = [whole(o) for o in middle_shapes]
-        outs[2] = outs[3] = pl.BlockSpec(memory_space=pl.ANY)
-        outs[7] = pl.BlockSpec((1, wide), lambda step: (0, chunk(step)))
+        outs[5] = pl.BlockSpec(memory_space=pl.ANY)
+        outs[9] = pl.BlockSpec((1, wide), lambda step: (0, chunk(step)))
         return call(
             text_middle,
             chunks + 1,
@@ -1182,32 +1236,33 @@
                 pltpu.VMEM((2, D, wide), bf16),
                 pltpu.VMEM((2, down_rows, down_width), bf16),
                 pltpu.VMEM((D, wide), bf16),
-                pltpu.SemaphoreType.DMA((2, 4)),
+                pltpu.VMEM((height, D), bf16),
+                pltpu.SemaphoreType.DMA((2, 2)),
             ],
             29 * 10**9,
         )(row_blocks, *inputs, up_bias, *[w_late] * 4, w_down)
 
+    def middle_stem():
+        made = list(blank(middle_shapes))
+        made[5] = jnp.zeros(middle_shapes[5].shape, bf16)
+        return tuple(made)
+
     (
-        block_out, grad_two, late_w_lo, late_w_hi, g_a, g_b, grads_three, grad_up_bias,
-    ) = lax.cond(is_stem, lambda: tuple(blank(middle_shapes)), middle_text)
-    g_here = to_cores(g_a, g_b)
-    g_here, late_w_lo = barrier((g_here, late_w_lo))
+        out_lo, out_hi, own_lo, own_hi, grad_two, late_term, g_a, g_b, grads_three, grad_up_bias,
+    ) = lax.cond(is_stem, middle_stem, middle_text)
     if lines.by_hand:
-        late_sum = (lax.ppermute(late_w_lo, "section", [(1, 0)]), late_w_hi)
-        late_sum = tuple(w.reshape(4, 2, 2, HALF // dp, w.shape[1]) for w in late_sum)
+        late_grad = lax.psum_scatter(late_term, BOTH, scatter_dimension=0, tiled=True)
     else:
-        late_term = jnp.concatenate([late_w_lo, late_w_hi])
-        late_term = jnp.where(is_stem, jnp.zeros_like(late_term), late_term)
         late_grad = lax.psum_scatter(
             late_term[:, : CH + FF], BOTH, scatter_dimension=0, tiled=True
         )
         down_turned = lax.psum_scatter(
             late_term[:, CH + FF :], BOTH, scatter_dimension=1, tiled=True
         )
-    out_here = to_cores(block_out[:, :HALF], block_out[:, HALF:])
-    sent = simple(pack_half, [arrival_row[:, None], out_here], [arrival_shape], [], 3 * 10**9)[0]
-    g_here, sent = barrier((g_here, sent))
-    got_out = send(sent.reshape(dp, capacity * LONGEST, HALF)).reshape(slots * LONGEST, HALF)
+    g_here = to_cores(g_a, g_b)
+    out_here = to_cores(out_lo, out_hi)
+    g_here, out_here = barrier((g_here, out_here))
+    got_out = send(out_here.reshape(dp, capacity * LONGEST, HALF)).reshape(slots * LONGEST, HALF)
 
     def cross_back(kv):
         return tuple(
@@ -1218,14 +1273,12 @@
                 [whole(q_here), whole(kv)],
                 [slot_shape, rows_shape],
                 [],
-                17 * 10**9,
+                0,
             )(q_here, g_here, kv)
         )
 
     grad_here, grad_kv = lax.cond(is_stem, lambda: cross_back(kv_lo), lambda: cross_back(kv_moved))
-    if lines.by_hand:
-        grad_here, grad_kv, late_sum, got_out = barrier((grad_here, grad_kv, late_sum, got_out))
-        late_got = lines.sum_first([late_sum])
+    grad_here, grad_kv, got_out = barrier((grad_here, grad_kv, got_out))
     grad_kv_moved = lax.ppermute(grad_kv, "section", [(1, 0)])
 
     stem_kv_shapes = [
@@ -1290,7 +1343,7 @@
                 pltpu.VMEM((D, 3 * D), f32),
                 pltpu.VMEM((height, D), f32),
             ],
-            25 * 10**9,
+            0,
         )(row_blocks, *inputs, *qkv_inputs)
         return (*done, *blank(stem_last_shapes))
 
@@ -1302,7 +1355,7 @@
             [rows_spec(half_channels)] * 2 + [at(o.shape, 0, 0) for o in stem_last_shapes[2:]],
             stem_last_shapes,
             [pltpu.VMEM((CH, D), f32)],
-            22 * 10**9,
+            0,
         )(features, bn, w_patch, grad_rows)
         return (*blank(text_last_shapes), *done)
 
@@ -1331,30 +1384,24 @@
         ]
     ).reshape(-1, CH)
 
-    def summed(vector, first, last):
-        step = first
-        while step < last:
+    def summed(vector, steps):
+        for step in steps:
             vector = vector + lax.ppermute(vector, "dp", [(i, i ^ step) for i in range(dp)])
-            step *= 2
         return vector
 
     grad_w_lo, grad_w_hi, kv_w_lo, kv_w_hi = barrier(
         (grad_w_lo, grad_w_hi, kv_w_lo, kv_w_hi)
     )
-    if lines.by_hand:
-        late_got, grad_w_lo = barrier((late_got, grad_w_lo))
-    moved_rows = lax.ppermute(rows_low, "section", [(1, 0)])
-    got_hi = lax.ppermute(grad_hi, "section", [(0, 1)])
-    block_piece = simple(
-        join_output,
-        [slot_rows[None, :], own_row[:, None], got_out, out_here],
-        [shape((tokens, HALF), bf16)],
-        [],
-        3 * 10**9,
-    )[0]
-
-    def sent_rows():
-        return send(jnp.where(is_stem, moved_rows, rows_high).reshape(dp, room, D))
+    own_here = to_cores(own_lo, own_hi)
+
+    def output(got_out):
+        return simple(
+            join_output,
+            [slot_rows[None, :], got_out, own_here],
+            [own_shape],
+            [],
+            3 * 10**9,
+        )[0]
 
     if lines.by_hand:
         owners = CH // project_rows
@@ -1368,23 +1415,27 @@
         ]
         patch = (parts[:, 0], lax.ppermute(parts[:, 1], "section", [(0, 1)]))
         patch = [tuple(w.reshape(2, 2, 2, project_rows // 2, D) for w in patch)]
-        late_got_two = lines.sum_second([late_sum], late_got)
-        terms, patch, moved_rows = barrier((terms, patch, moved_rows))
-        got = lines.sum_first(terms)
+        terms, patch = barrier((terms, patch))
+        first = lines.first_half(terms, 1)
+        first, rows_low, vector_term = barrier((first, rows_low, vector_term))
+        got = lines.across(first, 2, 1)
         patch_got = lines.sum_first(patch)
-        got_rows = sent_rows()
-        vector_total = summed(vector_term, 1, dp)
-        late_line = lines.line_of([late_sum], late_got, late_got_two)
-        late_parts = lines.sum_line(late_line)
-        got, patch_got, vector_total = barrier((got, patch_got, vector_total))
+        vector_term = summed(vector_term, (4, 8))
+        sent_rows = to_cores(rows_low, rows_high).reshape(dp, room, D)
+        got_rows = send(sent_rows)
+        got, patch_got, got_rows, vector_term = barrier((got, patch_got, got_rows, vector_term))
         got_two = lines.sum_second(terms, got)
         patch_got_two = lines.sum_second(patch, patch_got)
-        got_two, patch_got_two, late_parts = barrier((got_two, patch_got_two, late_parts))
+        got_two, patch_got_two, got_rows, vector_term, grad_hi, got_out, late_grad = barrier(
+            (got_two, patch_got_two, got_rows, vector_term, grad_hi, got_out, late_grad)
+        )
         line = lines.line_of(terms, got, got_two)
         line_parts = lines.sum_line(line)
         patch_line = lines.line_of(patch, patch_got, patch_got_two)
         patch_got = lines.sum_low_first(patch_line)
-        late_grad = lines.line_total(late_line, late_parts)
+        vector_total = summed(vector_term, (1, 2))
+        block_piece = output(got_out)
+        got_hi = lax.ppermute(grad_hi, "section", [(0, 1)])
         tail_grad = lines.line_total(line, line_parts)
         patch_low = lines.sum_low_last(patch_line, patch_got)
         patch_high = lax.ppermute(patch_low, "section", [(1, 0)])
@@ -1394,8 +1445,10 @@
             is_stem & (dp_index < owners), jnp.concatenate([patch_low, patch_high]), 0.0
         )
     else:
-        vector_total = summed(vector_term, 1, dp)
-        got_rows = sent_rows()
+        vector_total = summed(vector_term, [1 << bit for bit in range(dp.bit_length() - 1)])
+        got_rows = send(to_cores(rows_low, rows_high).reshape(dp, room, D))
+        block_piece = output(got_out)
+        got_hi = lax.ppermute(grad_hi, "section", [(0, 1)])
         tail_grad, patch_grad = lines.scatter_plain(
             grad_w_lo, grad_w_hi, kv_w_lo, kv_w_hi, grad_patch_w
         )

time: 623 us -> 577 us (0.926)
  starting transfers between devices: 150 us -> 115 us
  loops' own time: 5.96 us -> 26.1 us
  waiting for transfers between devices: 170 us -> 153 us
  other arithmetic: 94.2 us -> 80.6 us
    ppermute x4, waiting for transfers between devices: 6.57 us -> 30.4 us  [summed(): lax.ppermute(vector, 'dp', [(i, i ^ step) for i in range(dp)])]
    ppermute x22 -> x19, waiting for transfers between devices: 47.6 us -> 26.5 us  [across(): return lax.ppermute(array, BOTH, pairs)]
    all_to_all x6, starting transfers between devices: 52.9 us -> 34.3 us  [send(): return lax.all_to_all(block, 'dp', split_axis=0, concat_axis=0, tiled=True)]
    ppermute x22 -> x19, starting transfers between devices: 37.7 us -> 28.1 us  [across(): return lax.ppermute(array, BOTH, pairs)]
    ppermute x9 -> x0, starting transfers between devices: 9.28 us -> none  [the longest x6 6.64 us: merged(): other = lax.ppermute(state, 'dp', [(i, i ^ step) for i in range(dp)])]
    ppermute x9 -> x0, waiting for transfers between devices: 9.2 us -> none  [the longest x6 9.2 us: merged(): other = lax.ppermute(state, 'dp', [(i, i ^ step) for i in range(dp)])]
    another operation x1, loops' own time: 0.43 us -> 8.78 us  [per_device(): lax.cond(is_stem, last_stem, last_text)]
    another operation x1, loops' own time: 0.47 us -> 7.72 us  [per_device(): lax.cond(is_stem, middle_stem, middle_text)]
  transfers between devices with their start and end apart: 61 -> 54, of which waited for: 25 -> 21; matrix products, arithmetic and copies ran while one was open for 18% -> 20% of each run, Pallas kernels for 20% -> 21%
where the time goes in v3:
time: 577 us; the launch traced here: 566 us
  waiting for transfers between devices  153 us (27%)
  Pallas kernels  118 us (20%)
  starting transfers between devices  115 us (20%)
  other arithmetic  80.6 us (14%)
  local copies, waits for them, and re-layouts  43.3 us (8%)
  loops' own time  26.1 us (5%)
  between operations  19.3 us (3%)
  matrix products  10.9 us (2%)
    ppermute x5, waiting for transfers between devices, to_cores(): lax.ppermute(block_a, 'section', [(1, 0)])  44.7 us
    all_to_all x6, waiting for transfers between devices, send(): return lax.all_to_all(block, 'dp', split_axis=0, concat_axis=0, tiled=True)  42.5 us
    all_to_all x6, starting transfers between devices, send(): return lax.all_to_all(block, 'dp', split_axis=0, concat_axis=0, tiled=True)  34.3 us
    ppermute x4, waiting for transfers between devices, summed(): lax.ppermute(vector, 'dp', [(i, i ^ step) for i in range(dp)])  30.4 us
    ppermute x19, starting transfers between devices, across(): return lax.ppermute(array, BOTH, pairs)  28.1 us
    ppermute x19, waiting for transfers between devices, across(): return lax.ppermute(array, BOTH, pairs)  26.5 us
    pallas_call x1, Pallas kernels, first_stem(): call(stem_forward, blocks, [rows_spec(CH), whole(bn), patch_spec, whole(p...  23.2 us
    pallas_call x1, Pallas kernels, stem_kv(): call(stem_backward_kv, blocks, kv_specs + [rows_spec(D)] * 3, [rows_spec(...  22.9 us
  transfers between devices with their start and end apart: 54, of which 21 were waited for; matrix products, arithmetic and copies ran while one was open for 20% of the time, Pallas kernels for 21%

profile of v3, /device:TPU:0, one launch (start us, length us, event | category | flops | bytes accessed | tf_op | source)
XLA Modules:
  0.0 565.7 jit_solution(6342680972035067583)
XLA Ops:
  9.4 5.0 collective-permute-start.4
  16.7 4.9 collective-permute-start.5
  41.0 5.3 all-to-all-start.4
  93.9 27.5 %all-to-all-done.6 = bf16[16,40,768]{2,1,0:T(8,128)(2,1)S(1)} async-done(((bf16[16,40,768]{2,1,0:T(8,128)(2,1)}), bf16[16,40,768]{2,1,0:T(8,128)(2,1)S(1)}, u32[]{:S(2)}, u32[]{:S(2)}) %all-to-all-start.6) | async-done | bytes 983072 | tf_op jit(solution)/shard_map/all_to_all | solution.py:891
  133.8 5.4 collective-permute-done.13
  144.4 7.7 %collective-permute-done.16.four = bf16[2,4,24,1408]{3,2,1,0:T(8,128)(2,1)} collective-permute-done((bf16[2,4,24,1408]{3,2,1,0:T(8,128)(2,1)S(1)}, bf16[2,4,24,1408]{3,2,1,0:T(8,128)(2,1)}, u32[]{:S(2)}, u32[]{:S(2)}) %collective-permute-start.16) | collective-permute-done | bytes 540704 | tf_op jit(solution)/shard_map/ppermute | solution.py:698
  177.3 29.3 %conditional.17 = (bf16[1024,2304]{1,0:T(8,128)(2,1)}, bf16[1024,768]{1,0:T(8,128)(2,1)}, f32[1024,768]{1,0:T(8,128)}, bf16[512,384]{1,0:T(8,128)(2,1)S(1)}, bf1...) conditional(s32[]{:T(128)} %convert_element_type.218, ...), branch_computations={%region_29.30_spmd, %region_30.31_spmd} | conditional | flops 23000000512 | bytes 12352 | solution.py:1140
  183.3 23.2 %branch_1_fun.9 = (bf16[3136,768]{1,0:T(8,128)(2,1)}, bf16[3136,768]{1,0:T(8,128)(2,1)}, bf16[3136,768]{1,0:T(8,128)(2,1)}) custom-call(bf16[3136,1024]{1,0:T(8,128)(2,1)} %get-tuple-element.507.features, f32[4,1024]{1,0:T(4,128)S(1)} %get-tuple-element.508.bn, bf16[1024,768]{1,0:T(8,128)(2,1)} %get-tuple-element.509.w_patch, f32[1,768]{1,0:T(1,128)} %reshape.880.patch_bias, ...), custom_call_target="tpu_custom_call" | custom-call | flops 23000000512 | tf_op jit(solution)/shard_map/cond/branch_1_fun/pallas_call | solution.py:1129
  216.0 8.5 %conditional.18 = (bf16[512,384]{1,0:T(8,128)(2,1)}) conditional(s32[]{:T(128)} %convert_element_type.218, (bf16[512,384]{1,0:T(8,128)(2,1)S(1)}, bf16[3136,768]{1,0:T(8,128)(2,1)}) %tuple.126, (bf16[512,384]{1,0:T(8,128)(2,1)S(1)}, bf16[3136,768]{1,0:T(8,128)(2,1)}) %tuple.127), branch_computations={%region_32.33_spmd, %region_33.34_spmd} | conditional | flops 8000000000 | bytes 8 | solution.py:1161
  216.0 8.5 %branch_1_fun.10 = bf16[512,384]{1,0:T(8,128)(2,1)} custom-call(bf16[512,384]{1,0:T(8,128)(2,1)S(1)} %get-tuple-element.517.queries, bf16[3136,768]{1,0:T(8,128)(2,1)} %get-tuple-element.518.kv), custom_call_target="tpu_custom_call" | custom-call | flops 8000000000 | tf_op jit(solution)/shard_map/cond/branch_1_fun/pallas_call | solution.py:1151
  228.2 6.3 %shard_map.340 = bf16[1024,768]{1,0:T(8,128)(2,1)} custom-call(s32[1,1024]{1,0:T(1,128)} %broadcast_in_dim_reshape.4.arrival, s32[1,512]{1,0:T(1,128)S(1)} %bitcast.266, bf16[1024,384]{1,0:T(8,128)(2,1)} %collective-permute-done.22.slots_a, bf16[1024,384]{1,0:T(8,128)(2,1)} %bitcast.232, f32[512,768]{1,0:T(8,128)} %rows.1), custom_call_target="tpu_custom_call" | custom-call | flops 4000000000 | tf_op jit(solution)/shard_map/pallas_call | solution.py:665
  237.3 13.9 %conditional.19 = (bf16[768,8192]{1,0:T(8,128)(2,1)}, bf16[1024,384]{1,0:T(8,128)(2,1)}, bf16[1024,384]{1,0:T(8,128)(2,1)}, bf16[512,384]{1,0:T(8,128)(2,1)}, bf...) conditional(s32[]{:T(128)} %convert_element_type.218, ...), branch_computations={%region_34.35_spmd.clone, %region_35.36_spmd.clone} | conditional | flops 28999999488 | bytes 12582994 | solution.py:1252
  245.0 6.1 %broadcast.517 = bf16[768,8192]{1,0:T(8,128)(2,1)} broadcast(bf16[]{:T(256)} %constant.317.clone.1), dimensions={} | broadcast | bytes 12582914 | tf_op jit(solution)/shard_map/broadcast.18
  253.8 41.9 %collective-permute-done.23 = bf16[512,384]{1,0:T(8,128)(2,1)S(1)} collective-permute-done((bf16[512,384]{1,0:T(8,128)(2,1)}, bf16[512,384]{1,0:T(8,128)(2,1)S(1)}, u32[]{:S(2)}, u32[]{:S(2)}) %collective-permute-start.23) | collective-permute-done | bytes 393248 | tf_op jit(solution)/shard_map/ppermute | solution.py:1147
  298.5 12.3 %all-to-all-start.8 = ((bf16[16,64,384]{2,1,0:T(8,128)(2,1)}), bf16[16,64,384]{2,1,0:T(8,128)(2,1)S(1)}, u32[]{:S(2)}, u32[]{:S(2)}) async-start(bf16[16,64,384]{2,1,0:T(8,128)(2,1)} %bitcast.54), calls=%async_computation.8 | async-start | bytes 1572864 | tf_op jit(solution)/shard_map/all_to_all | solution.py:891
  310.8 16.9 %conditional.20 = ((bf16[512,384]{1,0:T(8,128)(2,1)}, bf16[3136,768]{1,0:T(8,128)(2,1)})) conditional(s32[]{:T(128)} %convert_element_type.218, (bf16[512,384]{1,0:T(8,128)(2,1)S(1)}, bf16[512,384]{1,0:T(8,128)(2,1)S(1)}, bf16[3136,768]{1,0:T(8,128)(2,1)}) %tuple.131, (bf16[512,384]{1,0:T(8,128)(2,1)S(1)}, bf16[512,384]{1,0:T(8,128)(2,1)S(1)}, ...), branch_computations={%region_36.37_spmd, %region_37.38_spmd} | conditional | bytes 8 | solution.py:1280
  310.9 16.9 %branch_1_fun.11 = (bf16[512,384]{1,0:T(8,128)(2,1)}, bf16[3136,768]{1,0:T(8,128)(2,1)}) custom-call(bf16[512,384]{1,0:T(8,128)(2,1)S(1)} %get-tuple-element.554.queries, bf16[512,384]{1,0:T(8,128)(2,1)S(1)} %get-tuple-element.555.grads, bf16[3136,768]{1,0:T(8,128)(2,1)} %get-tuple-element.556.kv), custom_call_target="tpu_custom_call" | custom-call | tf_op jit(solution)/shard_map/cond/branch_1_fun/pallas_call | solution.py:1269
  332.2 5.2 collective-permute-start.25
  337.4 4.7 collective-permute-done.26
  342.2 22.9 %conditional.21 = ((bf16[3136,768]{1,0:T(8,128)(2,1)}, bf16[384,1536]{1,0:T(8,128)(2,1)}, bf16[384,1536]{1,0:T(8,128)(2,1)}, f32[1,768]{1,0:T(1,128)})) conditional(s32[]{:T(128)} %convert_element_type.218, () %tuple.134, (bf16[768,1536]{1,0:T(8,128)(2,1)}, bf16[3136,768]{1,0:T(8,128)(2,1)}, bf16[3136,768]{1,0:T(8,128)(2,1)}, ...), branch_computations={%region_38.39_spmd, %region_39.40_spmd} | conditional | flops 23000000512 | bytes 8 | solution.py:1305
  342.2 22.9 %branch_1_fun.12 = (bf16[3136,768]{1,0:T(8,128)(2,1)}, bf16[384,1536]{1,0:T(8,128)(2,1)}, bf16[384,1536]{1,0:T(8,128)(2,1)}, f32[1,768]{1,0:T(1,128)}) custom-call(bf16[768,1536]{1,0:T(8,128)(2,1)} %get-tuple-element.557.k_lo.k_hi.v_lo.v_hi, bf16[768,1536]{1,0:T(8,128)(2,1)} %get-tuple-element.557.k_lo.k_hi.v_lo.v_hi, ...), custom_call_target="tpu_custom_call" | custom-call | flops 23000000512 | tf_op jit(solution)/shard_map/cond/branch_1_fun/pallas_call | solution.py:1293
  365.2 30.5 %conditional.22 = (bf16[1024,768]{1,0:T(8,128)(2,1)}, bf16[640,768]{1,0:T(8,128)(2,1)}, bf16[640,768]{1,0:T(8,128)(2,1)}, bf16[384,3840]{1,0:T(8,128)(2,1)}, bf1...) conditional(s32[]{:T(128)} %convert_element_type.218, ...), branch_computations={%region_40.41_spmd, %region_41.42_spmd} | conditional | bytes 8272 | solution.py:1365
  373.9 21.7 %branch_1_fun.14 = (bf16[3136,512]{1,0:T(8,128)(2,1)}, bf16[3136,512]{1,0:T(8,128)(2,1)}, bf16[1024,768]{1,0:T(8,128)(2,1)}, f32[2,1024]{1,0:T(2,128)}) custom-call(bf16[3136,1024]{1,0:T(8,128)(2,1)} %get-tuple-element.590.features, f32[4,1024]{1,0:T(4,128)S(1)} %get-tuple-element.591.bn, bf16[1024,768]{1,0:T(8,128)(2,1)S(1)} %get-tuple-element.592.w_patch, ...), custom_call_target="tpu_custom_call" | custom-call | tf_op jit(solution)/shard_map/cond/branch_1_fun/pallas_call | solution.py:1351
  397.0 4.8 collective-permute-start.28
  425.2 5.0 all-to-all-start.9
  434.8 20.6 %collective-permute-done.33 = f32[11,1024]{1,0:T(8,128)S(1)} collective-permute-done((f32[11,1024]{1,0:T(8,128)S(1)}, f32[11,1024]{1,0:T(8,128)S(1)}, u32[]{:S(2)}, u32[]{:S(2)}) %collective-permute-start.33) | collective-permute-done | bytes 45088 | tf_op jit(solution)/shard_map/ppermute | solution.py:1389
  455.4 5.4 collective-permute-start.34
  460.8 6.1 %collective-permute-done.34 = f32[11,1024]{1,0:T(8,128)S(1)} collective-permute-done((f32[11,1024]{1,0:T(8,128)S(1)}, f32[11,1024]{1,0:T(8,128)S(1)}, u32[]{:S(2)}, u32[]{:S(2)}) %collective-permute-start.34) | collective-permute-done | bytes 45088 | tf_op jit(solution)/shard_map/ppermute | solution.py:1389
  482.7 6.4 %collective-permute-done.36 = bf16[2,64,768]{2,1,0:T(8,128)(2,1)} collective-permute-done((bf16[2,64,768]{2,1,0:T(8,128)(2,1)S(1)}, bf16[2,64,768]{2,1,0:T(8,128)(2,1)}, u32[]{:S(2)}, u32[]{:S(2)}) %collective-permute-start.36) | collective-permute-done | bytes 196640 | tf_op jit(solution)/shard_map/ppermute | solution.py:698
  511.0 13.0 %conditional.24 = (f32[1000,768]{1,0:T(8,128)S(1)}, f32[1000,768]{1,0:T(8,128)S(1)}, f32[1000,768]{1,0:T(8,128)S(1)}, f32[1000,768]{1,0:T(8,128)}, bf16[1000,768]{1,0:T(8,128)(2,1)}) conditional(s32[]{:T(128)} %convert_element_type.243, (s32[16,40]{1,0:T(8,128)S(1)}, bf16[16,40,768]{2,1,0:T(8,128)(2,1)}, f32[1000,768]{1,0:T(8,128)}, ...), branch_computations={%region_44.45_spmd, %region_45.51_spmd} | conditional | flops 3998031872 | bytes 100082256
  511.2 7.3 %fusion.52 = (bf16[1000,768]{1,0:T(8,128)(2,1)}, f32[1000,768]{1,0:T(8,128)}, f32[1000,768]{1,0:T(8,128)S(1)}, f32[1000,768]{1,0:T(8,128)S(1)}) fusion(f32[1000,768]{1,0:T(8,128)} %get-tuple-element.602, f32[1000,768]{1,0:T(8,128)} %get-tuple-element.600, bf16[640,768]{1,0:T(8,128)(2,1)} %bitcast.1, s32[640]{0:T(1024)S(1)} %eq.152), kind=kOutput, calls=%fused_computation.227 | convolution fusion | flops 989056000 | bytes 17881600 | tf_op jit(solution)/shard_map/cond/branch_0_fun/dot_general | solution.py:38
  553.2 5.4 subtract_multiply_fusion
  (457 shorter events, 234.1 us)
Async XLA Ops:
  9.4 53.4 %collective-permute-start.4 = (bf16[24,5376]{1,0:T(8,128)(2,1)}, bf16[24,5376]{1,0:T(8,128)(2,1)}, u32[]{:S(2)}, u32[]{:S(2)}) collective-permute-start(bf16[24,5376]{1,0:T(8,128)(2,1)} %get-tuple-element.1203), channel_id=1, source_target_pairs={{0,12},{1,13},{2,14},{3,15},{4,8},{5,9},{6,10},{7,11},{8,4},{9,5},... | collective-permute-start | bytes 774152 | tf_op jit(solution)/shard_map/ppermute | solution.py:698
  14.4 48.4 %collective-permute-start.3 = (bf16[24,5376]{1,0:T(8,128)(2,1)}, bf16[24,5376]{1,0:T(8,128)(2,1)}, u32[]{:S(2)}, u32[]{:S(2)}) collective-permute-start(bf16[24,5376]{1,0:T(8,128)(2,1)} %get-tuple-element.1203), channel_id=1, source_target_pairs={{0,8},{1,9},{2,10},{3,11},{4,12},{5,13},{6,14},{7,15},{8,0},{9,1},... | collective-permute-start | bytes 774152 | tf_op jit(solution)/shard_map/ppermute | solution.py:698
  14.4 48.4 %collective-permute-start.2 = (bf16[24,5376]{1,0:T(8,128)(2,1)}, bf16[24,5376]{1,0:T(8,128)(2,1)}, u32[]{:S(2)}, u32[]{:S(2)}) collective-permute-start(bf16[24,5376]{1,0:T(8,128)(2,1)} %get-tuple-element.1203), channel_id=1, source_target_pairs={{0,4},{1,5},{2,6},{3,7},{4,0},{5,1},{6,2},{7,3},{8,12},{9,13},{10,... | collective-permute-start | bytes 774152 | tf_op jit(solution)/shard_map/ppermute | solution.py:698
  16.7 40.3 %collective-permute-start.5 = (bf16[64,768]{1,0:T(8,128)(2,1)}, bf16[64,768]{1,0:T(8,128)(2,1)}, u32[]{:S(2)}, u32[]{:S(2)}) collective-permute-start(bf16[64,768]{1,0:T(8,128)(2,1)} %slice.201), channel_id=1, source_target_pairs={{0,8},{1,9},{2,10},{3,11},{4,12},{5,13},{6,14},{7,15}} | collective-permute-start | bytes 294920 | tf_op jit(solution)/shard_map/ppermute | solution.py:754
  64.2 14.7 %collective-permute-start.7 = (bf16[4,24,5376]{2,1,0:T(8,128)(2,1)S(1)}, bf16[4,24,5376]{2,1,0:T(8,128)(2,1)S(1)}, u32[]{:S(2)}, u32[]{:S(2)}) collective-permute-start(bf16[4,24,5376]{2,1,0:T(8,128)(2,1)S(1)} %pad_maximum_fusion.2), channel_id=1, source_target_pairs={{0,1},{1,0},{2,3},{3,2},{4,5},{5,4},{6,7},{7,6},{8,9},{9,8},{10,11... | collective-permute-start | bytes 3096584 | tf_op jit(solution)/shard_map/ppermute | solution.py:698
  84.9 57.6 %collective-permute-start.12 = (bf16[2,4,24,5376]{3,2,1,0:T(8,128)(2,1)}, bf16[2,4,24,5376]{3,2,1,0:T(8,128)(2,1)}, u32[]{:S(2)}, u32[]{:S(2)}) collective-permute-start(bf16[2,4,24,5376]{3,2,1,0:T(8,128)(2,1)} %pad_maximum_fusion.two), channel_id=1, source_target_pairs={{0,2},{1,3},{2,0},{3,1},{4,6},{5,7},{6,4},{7,5},{8,10},{9,11},{10,... | collective-permute-start | bytes 6193160 | tf_op jit(solution)/shard_map/ppermute | solution.py:698
  89.2 32.2 %all-to-all-start.6 = ((bf16[16,40,768]{2,1,0:T(8,128)(2,1)}), bf16[16,40,768]{2,1,0:T(8,128)(2,1)S(1)}, u32[]{:S(2)}, u32[]{:S(2)}) async-start(bf16[16,40,768]{2,1,0:T(8,128)(2,1)} %bitcast.23), calls=%async_computation.6 | async-start | bytes 1966080 | tf_op jit(solution)/shard_map/all_to_all | solution.py:891
  121.4 21.1 %all-to-all-start.7 = ((bf16[16,64,384]{2,1,0:T(8,128)(2,1)}), bf16[16,64,384]{2,1,0:T(8,128)(2,1)S(1)}, u32[]{:S(2)}, u32[]{:S(2)}) async-start(bf16[16,64,384]{2,1,0:T(8,128)(2,1)} %bitcast.31), calls=%async_computation.7 | async-start | bytes 1572864 | tf_op jit(solution)/shard_map/all_to_all | solution.py:891
  125.6 111.7 %all-gather.2.cloned.1.call-start = ((), (), s32[]{:S(2)}) async-start(), calls=%async_computation.11 | async-start | bytes 12976128 | tf_op jit(solution)/shard_map/all_gather | solution.py:1041
  125.6 16.9 %collective-permute-start.11 = (bf16[640,768]{1,0:T(8,128)(2,1)S(1)}, bf16[640,768]{1,0:T(8,128)(2,1)}, u32[]{:S(2)}, u32[]{:S(2)}) collective-permute-start(bf16[640,768]{1,0:T(8,128)(2,1)S(1)} %bitcast.227), channel_id=1, source_target_pairs={{0,16},{1,17},{2,18},{3,19},{4,20},{5,21},{6,22},{7,23},{8,24},{9,... | collective-permute-start | bytes 2949128 | tf_op jit(solution)/shard_map/ppermute | solution.py:1036
  142.5 346.6 %reduce-scatter.2.cloned.1.call-start = ((), (), s32[]{:S(2)}) async-start(), calls=%async_computation.12 | async-start | bytes 12976128 | tf_op jit(solution)/shard_map/reduce_scatter | solution.py:1254
  144.4 15.7 %collective-permute-start.17 = (bf16[2,4,24,1408]{3,2,1,0:T(8,128)(2,1)S(1)}, bf16[2,4,24,1408]{3,2,1,0:T(8,128)(2,1)}, u32[]{:S(2)}, u32[]{:S(2)}) collective-permute-start(bf16[2,4,24,1408]{3,2,1,0:T(8,128)(2,1)S(1)} %pad_maximum_fusion.4.two), channel_id=1, source_target_pairs={{0,16},{16,0},{1,17},{17,1},{2,18},{18,2},{3,19},{19,3},{4,20},{20... | collective-permute-start | bytes 1622024 | tf_op jit(solution)/shard_map/ppermute | solution.py:701
  154.2 17.2 %collective-permute-start.14 = (bf16[2,4,24,5376]{3,2,1,0:T(8,128)(2,1)}, bf16[2,4,24,5376]{3,2,1,0:T(8,128)(2,1)}, u32[]{:S(2)}, u32[]{:S(2)}) collective-permute-start(bf16[2,4,24,5376]{3,2,1,0:T(8,128)(2,1)} %pad_maximum_fusion.two), channel_id=1, source_target_pairs={{0,16},{16,0},{1,17},{17,1},{2,18},{18,2},{3,19},{19,3},{4,20},{20... | collective-permute-start | bytes 6193160 | tf_op jit(solution)/shard_map/ppermute | solution.py:701
  154.7 16.7 %collective-permute-start.15 = (bf16[2,4,24,5376]{3,2,1,0:T(8,128)(2,1)}, bf16[2,4,24,5376]{3,2,1,0:T(8,128)(2,1)}, u32[]{:S(2)}, u32[]{:S(2)}) collective-permute-start(bf16[2,4,24,5376]{3,2,1,0:T(8,128)(2,1)} %collective-permute-done.12.four), channel_id=1, source_target_pairs={{0,16},{16,0},{1,17},{17,1},{2,18},{18,2},{3,19},{19,3},{4,20},{20... | collective-permute-start | bytes 6193160 | tf_op jit(solution)/shard_map/ppermute | solution.py:701
  210.1 18.1 %collective-permute-start.22 = (bf16[1024,384]{1,0:T(8,128)(2,1)S(1)}, bf16[1024,384]{1,0:T(8,128)(2,1)}, u32[]{:S(2)}, u32[]{:S(2)}) collective-permute-start(bf16[1024,384]{1,0:T(8,128)(2,1)S(1)} %bitcast.233), channel_id=1, source_target_pairs={{0,16},{1,17},{2,18},{3,19},{4,20},{5,21},{6,22},{7,23},{8,24},{9,... | collective-permute-start | bytes 2359304 | tf_op jit(solution)/shard_map/ppermute | solution.py:1164
  251.2 46.3 %collective-permute-start.24 = (bf16[1024,384]{1,0:T(8,128)(2,1)}, bf16[1024,384]{1,0:T(8,128)(2,1)S(1)}, u32[]{:S(2)}, u32[]{:S(2)}) collective-permute-start(bf16[1024,384]{1,0:T(8,128)(2,1)} %get-tuple-element.786), channel_id=1, source_target_pairs={{16,0},{17,1},{18,2},{19,3},{20,4},{21,5},{22,6},{23,7},{24,8},{25... | collective-permute-start | bytes 2359304 | tf_op jit(solution)/shard_map/ppermute | solution.py:1147
  252.5 43.2 %collective-permute-start.23 = (bf16[512,384]{1,0:T(8,128)(2,1)}, bf16[512,384]{1,0:T(8,128)(2,1)S(1)}, u32[]{:S(2)}, u32[]{:S(2)}) collective-permute-start(bf16[512,384]{1,0:T(8,128)(2,1)} %get-tuple-element.784), channel_id=1, source_target_pairs={{16,0},{17,1},{18,2},{19,3},{20,4},{21,5},{22,6},{23,7},{24,8},{25... | collective-permute-start | bytes 1179656 | tf_op jit(solution)/shard_map/ppermute | solution.py:1147
  298.5 32.4 %all-to-all-start.8 = ((bf16[16,64,384]{2,1,0:T(8,128)(2,1)}), bf16[16,64,384]{2,1,0:T(8,128)(2,1)S(1)}, u32[]{:S(2)}, u32[]{:S(2)}) async-start(bf16[16,64,384]{2,1,0:T(8,128)(2,1)} %bitcast.54), calls=%async_computation.8 | async-start | bytes 1572864 | tf_op jit(solution)/shard_map/all_to_all | solution.py:891
  332.2 32.9 %collective-permute-start.25 = (bf16[512,384]{1,0:T(8,128)(2,1)}, bf16[512,384]{1,0:T(8,128)(2,1)S(1)}, u32[]{:S(2)}, u32[]{:S(2)}) collective-permute-start(bf16[512,384]{1,0:T(8,128)(2,1)} %get-tuple-element.792), channel_id=1, source_target_pairs={{0,16},{1,17},{2,18},{3,19},{4,20},{5,21},{6,22},{7,23},{8,24},{9,... | collective-permute-start | bytes 1179656 | tf_op jit(solution)/shard_map/ppermute | solution.py:1308
  395.7 16.7 %collective-permute-start.27 = (bf16[384,3840]{1,0:T(8,128)(2,1)}, bf16[384,3840]{1,0:T(8,128)(2,1)}, u32[]{:S(2)}, u32[]{:S(2)}) collective-permute-start(bf16[384,3840]{1,0:T(8,128)(2,1)} %get-tuple-element.805), channel_id=1, source_target_pairs={{16,0},{17,1},{18,2},{19,3},{20,4},{21,5},{22,6},{23,7},{24,8},{25... | collective-permute-start | bytes 8847368 | tf_op jit(solution)/shard_map/ppermute | solution.py:1410
  397.0 15.4 %collective-permute-start.28 = (bf16[384,1536]{1,0:T(8,128)(2,1)}, bf16[384,1536]{1,0:T(8,128)(2,1)S(1)}, u32[]{:S(2)}, u32[]{:S(2)}) collective-permute-start(bf16[384,1536]{1,0:T(8,128)(2,1)} %get-tuple-element.808), channel_id=1, source_target_pairs={{0,16},{1,17},{2,18},{3,19},{4,20},{5,21},{6,22},{7,23},{8,24},{9,... | collective-permute-start | bytes 3538952 | tf_op jit(solution)/shard_map/ppermute | solution.py:1411
  420.8 48.8 %collective-permute-start.30 = (bf16[4,2,24,5376]{3,2,0,1:T(8,128)(2,1)}, bf16[4,2,24,5376]{3,2,0,1:T(8,128)(2,1)}, u32[]{:S(2)}, u32[]{:S(2)}) collective-permute-start(bf16[4,2,24,5376]{3,2,0,1:T(8,128)(2,1)} %pad_maximum_fusion.1), channel_id=1, source_target_pairs={{0,2},{1,3},{2,0},{3,1},{4,6},{5,7},{6,4},{7,5},{8,10},{9,11},{10,... | collective-permute-start | bytes 6193160 | tf_op jit(solution)/shard_map/ppermute | solution.py:698
  425.2 44.3 %all-to-all-start.9 = ((bf16[16,40,768]{2,1,0:T(8,128)(2,1)}), bf16[16,40,768]{2,1,0:T(8,128)(2,1)}, u32[]{:S(2)}, u32[]{:S(2)}) async-start(bf16[16,40,768]{2,1,0:T(8,128)(2,1)} %bitcast.75), calls=%async_computation.9 | async-start | bytes 1966080 | tf_op jit(solution)/shard_map/all_to_all | solution.py:891
  431.4 38.2 %collective-permute-start.31 = (bf16[2,2,64,768]{3,2,1,0:T(8,128)(2,1)S(1)}, bf16[2,2,64,768]{3,2,1,0:T(8,128)(2,1)S(1)}, u32[]{:S(2)}, u32[]{:S(2)}) collective-permute-start(bf16[2,2,64,768]{3,2,1,0:T(8,128)(2,1)S(1)} %bitcast_select_fusion.4), channel_id=1, source_target_pairs={{0,2},{1,3},{2,0},{3,1},{4,6},{5,7},{6,4},{7,5},{8,10},{9,11},{10,... | collective-permute-start | bytes 1179656 | tf_op jit(solution)/shard_map/ppermute | solution.py:698
  433.3 22.1 %collective-permute-start.33 = (f32[11,1024]{1,0:T(8,128)S(1)}, f32[11,1024]{1,0:T(8,128)S(1)}, u32[]{:S(2)}, u32[]{:S(2)}) collective-permute-start(f32[11,1024]{1,0:T(8,128)S(1)} %copy-done.53), channel_id=1, source_target_pairs={{0,4},{1,5},{2,6},{3,7},{4,0},{5,1},{6,2},{7,3},{8,12},{9,13},{10,... | collective-permute-start | bytes 135176 | tf_op jit(solution)/shard_map/ppermute | solution.py:1389
  472.1 17.0 %collective-permute-start.35 = (bf16[4,24,5376]{2,1,0:T(8,128)(2,1)}, bf16[4,24,5376]{2,1,0:T(8,128)(2,1)}, u32[]{:S(2)}, u32[]{:S(2)}) collective-permute-start(bf16[4,24,5376]{2,1,0:T(8,128)(2,1)} %fusion.28), channel_id=1, source_target_pairs={{0,1},{1,0},{2,3},{3,2},{4,5},{5,4},{6,7},{7,6},{8,9},{9,8},{10,11... | collective-permute-start | bytes 3096584 | tf_op jit(solution)/shard_map/ppermute | solution.py:698
  489.2 13.7 %collective-permute-start.39 = (f32[11,1024]{1,0:T(8,128)}, f32[11,1024]{1,0:T(8,128)S(1)}, u32[]{:S(2)}, u32[]{:S(2)}) collective-permute-start(f32[11,1024]{1,0:T(8,128)} %add.445), channel_id=1, source_target_pairs={{0,1},{1,0},{2,3},{3,2},{4,5},{5,4},{6,7},{7,6},{8,9},{9,8},{10,11... | collective-permute-start | bytes 135176 | tf_op jit(solution)/shard_map/ppermute | solution.py:1389
  490.6 62.5 %collective-permute-start.38 = (bf16[3136,512]{1,0:T(8,128)(2,1)}, bf16[3136,512]{1,0:T(8,128)(2,1)}, u32[]{:S(2)}, u32[]{:S(2)}) collective-permute-start(bf16[3136,512]{1,0:T(8,128)(2,1)} %get-tuple-element.837), channel_id=1, source_target_pairs={{0,16},{1,17},{2,18},{3,19},{4,20},{5,21},{6,22},{7,23},{8,24},{9,... | collective-permute-start | bytes 9633800 | tf_op jit(solution)/shard_map/ppermute | solution.py:1438
  496.8 46.3 %collective-permute-start.44 = (bf16[24,5376]{1,0:T(8,128)(2,1)}, bf16[24,5376]{1,0:T(8,128)(2,1)}, u32[]{:S(2)}, u32[]{:S(2)}) collective-permute-start(bf16[24,5376]{1,0:T(8,128)(2,1)} %get-tuple-element.1200), channel_id=1, source_target_pairs={{0,12},{1,13},{2,14},{3,15},{4,8},{5,9},{6,10},{7,11},{8,4},{9,5},... | collective-permute-start | bytes 774152 | tf_op jit(solution)/shard_map/ppermute | solution.py:698
  507.9 21.2 %collective-permute-start.41 = (f32[11,1024]{1,0:T(8,128)}, f32[11,1024]{1,0:T(8,128)}, u32[]{:S(2)}, u32[]{:S(2)}) collective-permute-start(f32[11,1024]{1,0:T(8,128)} %add.450), channel_id=1, source_target_pairs={{0,16},{16,0},{1,17},{17,1},{2,18},{18,2},{3,19},{19,3},{4,20},{20... | collective-permute-start | bytes 135176 | tf_op jit(solution)/shard_map/ppermute | solution.py:1460
  511.0 32.1 %collective-permute-start.43 = (bf16[24,5376]{1,0:T(8,128)(2,1)}, bf16[24,5376]{1,0:T(8,128)(2,1)}, u32[]{:S(2)}, u32[]{:S(2)}) collective-permute-start(bf16[24,5376]{1,0:T(8,128)(2,1)} %get-tuple-element.1201), channel_id=1, source_target_pairs={{0,8},{1,9},{2,10},{3,11},{4,12},{5,13},{6,14},{7,15},{8,0},{9,1},... | collective-permute-start | bytes 774152 | tf_op jit(solution)/shard_map/ppermute | solution.py:698
  524.1 19.1 %collective-permute-start.42 = (bf16[24,5376]{1,0:T(8,128)(2,1)}, bf16[24,5376]{1,0:T(8,128)(2,1)}, u32[]{:S(2)}, u32[]{:S(2)}) collective-permute-start(bf16[24,5376]{1,0:T(8,128)(2,1)} %get-tuple-element.1199), channel_id=1, source_target_pairs={{0,4},{1,5},{2,6},{3,7},{4,0},{5,1},{6,2},{7,3},{8,12},{9,13},{10,... | collective-permute-start | bytes 774152 | tf_op jit(solution)/shard_map/ppermute | solution.py:698
  (114 other events, 1529.9 us)
Sparse Core Ops, SparseCore 0:
  142.6 94.6 all-gather.1
  253.9 225.1 reduce-scatter.1

commit v4 on v3

--- a/solution.py
+++ b/solution.py
@@ -125,26 +125,12 @@
     return jnp.concatenate([jnp.where(allowed, 1, 0)] * 4, axis=0) > 0
 
 
-def each_block(count, body):
+def chunks_of(count, size, body):
     def step(index, carry):
-        body(pl.multiple_of(index * BLOCK, BLOCK))
+        body(pl.multiple_of(index * size, size))
         return carry
 
     lax.fori_loop(0, count, step, 0)
-
-
-def each_pair(count, body):
-    pairs = count // 2
-
-    def step(index, carry):
-        body(pl.multiple_of(index * ROWS, ROWS), ROWS)
-        return carry
-
-    lax.fori_loop(0, pairs, step, 0)
-
-    @pl.when(count % 2 == 1)
-    def _():
-        body(pl.multiple_of(pairs * ROWS, ROWS), BLOCK)
 
 
 def text_first(
@@ -161,8 +147,8 @@
     masks = head_masks(bf16)
     masks_f = head_masks(f32)
 
-    def project(first, size):
-        rows = pl.ds(first, size)
+    def project(first):
+        rows = pl.ds(first, ROWS)
         unit, _ = normalise(embed[rows, :].astype(f32))
         normed = (unit * vecs[0:1, :] + vecs[1:2, :]).astype(bf16)
         for third in range(3):
@@ -181,17 +167,17 @@
             mixed = mm(shares.astype(bf16), qkv_rows[span, values])
             mix_rows[rows, lanes] = join_heads(mixed, masks_f).astype(bf16)
 
-    def finish(first, size):
-        rows = pl.ds(first, size)
+    def finish(first):
+        rows = pl.ds(first, ROWS)
         resid = embed[rows, :].astype(f32) + mm(mix_rows[rows, :], w_out[...])
         resid_one[rows, :] = resid
         unit, _ = normalise(resid)
         normed = (unit * vecs[2:3, :] + vecs[3:4, :]).astype(bf16)
         queries[rows, :] = mm(normed, w_cq[...]).astype(bf16)
 
-    each_pair(count, project)
-    each_block(count, attend)
-    each_pair(count, finish)
+    chunks_of(count, ROWS, project)
+    chunks_of(count * (ROWS // BLOCK), BLOCK, attend)
+    chunks_of(count, ROWS, finish)
     packed = mm(one_hot_cols(pack[...], queries.shape[0]), queries[...]).astype(bf16)
     slots_a[...] = packed[:, :HALF]
     slots_b[...] = packed[:, HALF:]
@@ -247,9 +233,9 @@
         block_out[...] = jnp.zeros_like(block_out)
         vec_grad[...] = jnp.zeros_like(vec_grad)
 
-        def begin(first, size):
-            rows = pl.ds(first, size)
-            places = lax.broadcasted_iota(i32, (size, take.shape[1]), 0) + first
+        def begin(first):
+            rows = pl.ds(first, ROWS)
+            places = lax.broadcasted_iota(i32, (ROWS, take.shape[1]), 0) + first
             hit = jnp.where(places == take[...], 1.0, 0.0).astype(bf16)
             mixed[rows, :HALF] = mm(hit, mix_a[...]).astype(bf16)
             mixed[rows, HALF:] = mm(hit, mix_b[...]).astype(bf16)
@@ -261,10 +247,10 @@
             normed[rows, :] = low
             normed_t[:, rows] = low.T
             total[rows, :] = resid_two + vecs[2:3, :]
-            back[rows, :] = jnp.zeros((size, D), f32)
+            back[rows, :] = jnp.zeros((ROWS, D), f32)
             grad_down_t[:, rows] = cotangent[rows, :].T
 
-        each_pair(count, begin)
+        chunks_of(count, ROWS, begin)
 
     @pl.when(step < last)
     def _():
@@ -284,8 +270,8 @@
         down_sum[...] = jnp.zeros_like(down_sum)
         up_bias_grad[...] = jnp.zeros_like(up_bias_grad)
 
-        def forward_back(first, size):
-            rows = pl.ds(first, size)
+        def forward_back(first):
+            rows = pl.ds(first, ROWS)
             act, slope = gelu_parts(mm(normed[rows, :], w_up[...]) + up_bias[...])
             act = act.astype(bf16)
             total[rows, :] += mm_rt(act, w_down_t[...])
@@ -295,7 +281,7 @@
             down_sum[...] += mm(grad_down_t[:, rows], act)
             back[rows, :] += mm_rt(grad_up, w_up[...])
 
-        each_pair(count, forward_back)
+        chunks_of(count, ROWS, forward_back)
         slot = step % 2
         up_buffer[slot] = up_sum[...].astype(bf16)
         if by_owner:
@@ -323,8 +309,8 @@
     def _():
         up_sum[:, :D] = jnp.zeros((D, D), f32)
 
-        def end(first, size):
-            rows = pl.ds(first, size)
+        def end(first):
+            rows = pl.ds(first, ROWS)
             block_out[rows, :] = total[rows, :].astype(bf16)
             incoming, unit = back[rows, :], grad_two[rows, :]
             vec_grad[0:1, :] += jnp.sum(incoming * unit, axis=0, keepdims=True)
@@ -336,7 +322,7 @@
             up_sum[:, :D] += mm_lt(mixed[rows, :], grad)
             normed[rows, :] = mm_rt(grad, w_cout[...]).astype(bf16)
 
-        each_pair(count, end)
+        chunks_of(count, ROWS, end)
         slot = step % 2
         up_buffer[slot, :, :D] = up_sum[:, :D].astype(bf16)
         up_buffer[slot, :, D:] = jnp.zeros((D, wide - D), bf16)
@@ -382,9 +368,9 @@
     sums[...] = jnp.zeros_like(sums)
     grad_embed[...] = jnp.zeros_like(grad_embed)
 
-    def begin(first, size):
-        rows = pl.ds(first, size)
-        places = lax.broadcasted_iota(i32, (size, take.shape[1]), 0) + first
+    def begin(first):
+        rows = pl.ds(first, ROWS)
+        places = lax.broadcasted_iota(i32, (ROWS, take.shape[1]), 0) + first
         hit = jnp.where(places == take[...], 1.0, 0.0).astype(bf16)
         grad_q = jnp.concatenate([mm(hit, grad_a[...]), mm(hit, grad_b[...])], axis=1).astype(bf16)
         unit, factor = normalise(resid_one[rows, :])
@@ -419,8 +405,8 @@
             total[span, lanes] += mm_lt(grad_scores, query) * SCALE
             total[span, later] += mm_lt(shares.astype(bf16), grad)
 
-    def end(first, size):
-        rows = pl.ds(first, size)
+    def end(first):
+        rows = pl.ds(first, ROWS)
         unit, factor = normalise(embed[rows, :].astype(f32))
         normed = (unit * vecs[0:1, :] + vecs[1:2, :]).astype(bf16)
         grad = jnp.concatenate([grad_queries[rows, :], total[rows, :].astype(bf16)], axis=1)
@@ -433,12 +419,12 @@
         grad = grad_one[rows, :] + norm_back(incoming, unit, factor, vecs[0:1, :])
         grad_embed[rows, :] = grad.astype(bf16)
 
-    each_pair(count, begin)
+    chunks_of(count, ROWS, begin)
     keep(4 * D, sums[:, :D])
     keep(3 * D, sums[:, D : 2 * D])
-    each_block(count, attend)
+    chunks_of(count * (ROWS // BLOCK), BLOCK, attend)
     sums[...] = jnp.zeros_like(sums)
-    each_pair(count, end)
+    chunks_of(count, ROWS, end)
     keep(0, sums[...])
     half = rows_a.shape[0]
     rows_a[...] = mm(one_hot_rows(place[...], half), grad_embed[...]).astype(bf16)
@@ -795,11 +781,13 @@
         return (kept + got_two.astype(f32)).astype(bf16)
 
     def sum_line(self, line):
-        parts = [self.pick(line, 0, self.z ^ k) for k in (1, 2, 3)]
-        return [self.across(p, 4 * k, 4 * k) for k, p in zip((1, 2, 3), parts)]
-
-    def line_total(self, line, parts):
-        return self.pick(line, 0, self.z).astype(f32) + sum(part.astype(f32) for part in parts)
+        groups = [[c + 4 * z for z in range(4)] for c in range(4)]
+        return lax.all_to_all(
+            line, "dp", split_axis=0, concat_axis=0, axis_index_groups=groups, tiled=True
+        )
+
+    def line_total(self, parts):
+        return jnp.sum(parts.astype(f32), axis=0)
 
     def sum_low_first(self, line):
         return self.across(line, 8, 8)
@@ -958,7 +946,7 @@
     row = jnp.sum((before & here[None, :]).astype(i32), axis=1)
     row = jnp.where(here, row, -1)
     row_count = jnp.sum(here.astype(i32))
-    row_blocks = jnp.maximum((row_count + BLOCK - 1) // BLOCK, 2).reshape(1)
+    row_blocks = ((row_count + ROWS - 1) // ROWS).reshape(1)
     depth = jnp.concatenate(
         [jnp.tile(within, IMG_DEV), places - token_start]
     )
@@ -1009,6 +997,7 @@
             4 * 10**9,
         )[0]
 
+    cot_sum = jnp.sum(cotangent, axis=0)
     arrival_shape = shape((slots * LONGEST, HALF), bf16)
     cot_sent = simple(
         pack_half,
@@ -1018,7 +1007,9 @@
         3 * 10**9,
     )[0]
     if lines.by_hand:
-        got_ids, early, later, cot_sent = barrier((got_ids, early, later, cot_sent))
+        got_ids, early, later, cot_sent, cot_sum = barrier(
+            (got_ids, early, later, cot_sent, cot_sum)
+        )
         early = lines.gather_first(early)
         later = lines.gather_line(later)
     place, asked = round_of(0)
@@ -1364,6 +1355,28 @@
         grad_lo, grad_hi, grad_patch_w, bn_sums,
     ) = lax.cond(is_stem, last_stem, last_text)
 
+    def row_sums(asked, rows):
+        hit = (jnp.arange(table_rows, dtype=i32)[:, None] == asked[None, :]).astype(bf16)
+        return mm(hit, rows.reshape(half_room, D))
+
+    def table_more(turn, total):
+        place, asked = round_of(turn)
+        slot = jnp.arange(group * room, dtype=i32)
+        rows = mm((slot[:, None] == place[None, :]).astype(bf16), grad_embed).astype(bf16)
+        moved = lax.ppermute(rows[:half_room], "section", [(1, 0)])
+        rows = jnp.where(is_stem, moved, rows[half_room:]).reshape(dp, room, D)
+        return total + row_sums(send(asked).reshape(half_room), send(rows))
+
+    def table_update(total):
+        return sgd_update(total, table_momentum, table_master, table_average, 0.05)
+
+    def table_updated(got_rows):
+        return lax.cond(
+            rounds > 1,
+            lambda: table_update(lax.fori_loop(1, rounds, table_more, row_sums(asked, got_rows))),
+            lambda: table_update(row_sums(asked, got_rows)),
+        )
+
     gone = jnp.zeros((), f32)
     vector_term = jnp.concatenate(
         [
@@ -1377,7 +1390,7 @@
                         grads_outer.reshape(-1),
                         grads_three.reshape(-1),
                         grad_up_bias.reshape(-1),
-                        jnp.sum(cotangent, axis=0),
+                        cot_sum,
                     ]
                 ),
             ),
@@ -1426,17 +1439,20 @@
         got, patch_got, got_rows, vector_term = barrier((got, patch_got, got_rows, vector_term))
         got_two = lines.sum_second(terms, got)
         patch_got_two = lines.sum_second(patch, patch_got)
-        got_two, patch_got_two, got_rows, vector_term, grad_hi, got_out, late_grad = barrier(
-            (got_two, patch_got_two, got_rows, vector_term, grad_hi, got_out, late_grad)
+        table_new = table_updated(got_rows)
+        got_two, patch_got_two, _, vector_term, grad_hi, got_out = barrier(
+            (got_two, patch_got_two, table_new[0][:8, :128], vector_term, grad_hi, got_out)
         )
         line = lines.line_of(terms, got, got_two)
-        line_parts = lines.sum_line(line)
         patch_line = lines.line_of(patch, patch_got, patch_got_two)
         patch_got = lines.sum_low_first(patch_line)
+        line, patch_got = barrier((line, patch_got))
+        line_parts = lines.sum_line(line)
         vector_total = summed(vector_term, (1, 2))
         block_piece = output(got_out)
         got_hi = lax.ppermute(grad_hi, "section", [(0, 1)])
-        tail_grad = lines.line_total(line, line_parts)
+        line_parts, late_grad = barrier((line_parts, late_grad))
+        tail_grad = lines.line_total(line_parts)
         patch_low = lines.sum_low_last(patch_line, patch_got)
         patch_high = lax.ppermute(patch_low, "section", [(1, 0)])
         down_grad = late_grad[:, CH + FF :].astype(f32).reshape(late_grad.shape[0], -1, 128)
@@ -1449,6 +1465,7 @@
         got_rows = send(to_cores(rows_low, rows_high).reshape(dp, room, D))
         block_piece = output(got_out)
         got_hi = lax.ppermute(grad_hi, "section", [(0, 1)])
+        table_new = table_updated(got_rows)
         tail_grad, patch_grad = lines.scatter_plain(
             grad_w_lo, grad_w_hi, kv_w_lo, kv_w_hi, grad_patch_w
         )
@@ -1476,28 +1493,7 @@
         - own_normed * (own_gain * own_half(vector_total[0]) / every_patch)
     )
 
-    def row_sums(asked, rows):
-        hit = (jnp.arange(table_rows, dtype=i32)[:, None] == asked[None, :]).astype(bf16)
-        return mm(hit, rows.reshape(half_room, D))
-
-    def table_more(turn, total):
-        place, asked = round_of(turn)
-        slot = jnp.arange(group * room, dtype=i32)
-        rows = mm((slot[:, None] == place[None, :]).astype(bf16), grad_embed).astype(bf16)
-        moved = lax.ppermute(rows[:half_room], "section", [(1, 0)])
-        rows = jnp.where(is_stem, moved, rows[half_room:]).reshape(dp, room, D)
-        return total + row_sums(send(asked).reshape(half_room), send(rows))
-
     root_tokens = math.sqrt(tokens * dp)
-
-    def table_update(total):
-        return sgd_update(total, table_momentum, table_master, table_average, 0.05)
-
-    table_new = lax.cond(
-        rounds > 1,
-        lambda: table_update(lax.fori_loop(1, rounds, table_more, row_sums(asked, got_rows))),
-        lambda: table_update(row_sums(asked, got_rows)),
-    )
     block_new = sgd_update(
         block_grad, block_momentum, block_master, block_average, 0.5 * D ** (-0.5) / root_tokens
     )

time: 577 us -> 578 us (level)
  waiting for transfers between devices: 153 us -> 179 us
  loops' own time: 26.1 us -> 11.2 us
  starting transfers between devices: 115 us -> 128 us
  local copies, waits for them, and re-layouts: 43.3 us -> 32.8 us
  other arithmetic: 80.6 us -> 72.8 us
    ppermute x19 -> x16, waiting for transfers between devices: 26.5 us -> 59.7 us  [across(): return lax.ppermute(array, BOTH, pairs)]
    ppermute x4, waiting for transfers between devices: 30.4 us -> 18.4 us  [summed(): lax.ppermute(vector, 'dp', [(i, i ^ step) for i in range(dp)])]
    another operation x1, loops' own time: 8.78 us -> 0.44 us  [per_device(): lax.cond(is_stem, last_stem, last_text)]
    another operation x1, loops' own time: 7.72 us -> 0.48 us  [per_device(): lax.cond(is_stem, middle_stem, middle_text)]
    ppermute x19 -> x16, starting transfers between devices: 28.1 us -> 31.8 us  [across(): return lax.ppermute(array, BOTH, pairs)]
  transfers between devices with their start and end apart: 54 -> 52, of which waited for: 21 -> 20; matrix products, arithmetic and copies ran while one was open for 20% -> 17% of each run, Pallas kernels for 21% -> 20%
where the time goes in v4:
time: 578 us; the launch traced here: 571 us
  waiting for transfers between devices  179 us (31%)
  starting transfers between devices  128 us (22%)
  Pallas kernels  117 us (20%)
  other arithmetic  72.8 us (13%)
  local copies, waits for them, and re-layouts  32.8 us (6%)
  between operations  19.5 us (3%)
  loops' own time  11.2 us (2%)
  matrix products  10.9 us (2%)
    ppermute x16, waiting for transfers between devices, across(): return lax.ppermute(array, BOTH, pairs)  59.7 us
    ppermute x5, waiting for transfers between devices, to_cores(): lax.ppermute(block_a, 'section', [(1, 0)])  49.7 us
    all_to_all x6, waiting for transfers between devices, send(): return lax.all_to_all(block, 'dp', split_axis=0, concat_axis=0, tiled=True)  38.7 us
    all_to_all x6, starting transfers between devices, send(): return lax.all_to_all(block, 'dp', split_axis=0, concat_axis=0, tiled=True)  38.2 us
    ppermute x16, starting transfers between devices, across(): return lax.ppermute(array, BOTH, pairs)  31.8 us
    pallas_call x1, Pallas kernels, first_stem(): call(stem_forward, blocks, [rows_spec(CH), whole(bn), patch_spec, whole(p...  23.3 us
    pallas_call x1, Pallas kernels, stem_kv(): call(stem_backward_kv, blocks, kv_specs + [rows_spec(D)] * 3, [rows_spec(...  23 us
    pallas_call x1, Pallas kernels, last_stem(): call(stem_backward, blocks, [rows_spec(CH), whole(bn), patch_spec, rows_s...  21.2 us
  transfers between devices with their start and end apart: 52, of which 20 were waited for; matrix products, arithmetic and copies ran while one was open for 17% of the time, Pallas kernels for 20%

profile of v4, /device:TPU:0, one launch (start us, length us, event | category | flops | bytes accessed | tf_op | source)
XLA Modules:
  0.0 571.0 jit_solution(3189041027817193986)
XLA Ops:
  38.7 5.3 all-to-all-start.4
  89.3 27.5 %all-to-all-done.6 = bf16[16,40,768]{2,1,0:T(8,128)(2,1)S(1)} async-done(((bf16[16,40,768]{2,1,0:T(8,128)(2,1)}), bf16[16,40,768]{2,1,0:T(8,128)(2,1)S(1)}, u32[]{:S(2)}, u32[]{:S(2)}) %all-to-all-start.6) | async-done | bytes 983072 | tf_op jit(solution)/shard_map/all_to_all | solution.py:879
  129.2 6.8 %collective-permute-done.13 = bf16[4,24,1408]{2,1,0:T(8,128)(2,1)S(1)} collective-permute-done((bf16[4,24,1408]{2,1,0:T(8,128)(2,1)S(1)}, bf16[4,24,1408]{2,1,0:T(8,128)(2,1)S(1)}, u32[]{:S(2)}, u32[]{:S(2)}) %collective-permute-start.13) | collective-permute-done | bytes 270368 | tf_op jit(solution)/shard_map/ppermute | solution.py:684
  138.9 7.8 %collective-permute-done.16.four = bf16[2,4,24,1408]{3,2,1,0:T(8,128)(2,1)} collective-permute-done((bf16[2,4,24,1408]{3,2,1,0:T(8,128)(2,1)S(1)}, bf16[2,4,24,1408]{3,2,1,0:T(8,128)(2,1)}, u32[]{:S(2)}, u32[]{:S(2)}) %collective-permute-start.16) | collective-permute-done | bytes 540704 | tf_op jit(solution)/shard_map/ppermute | solution.py:684
  171.8 29.0 %conditional.17 = (bf16[1024,2304]{1,0:T(8,128)(2,1)}, bf16[1024,768]{1,0:T(8,128)(2,1)}, f32[1024,768]{1,0:T(8,128)}, bf16[512,384]{1,0:T(8,128)(2,1)S(1)}, bf1...) conditional(s32[]{:T(128)} %convert_element_type.206, ...), branch_computations={%region_30.31_spmd, %region_31.32_spmd} | conditional | flops 23000000512 | bytes 12352 | solution.py:1131
  177.5 23.3 %branch_1_fun.9 = (bf16[3136,768]{1,0:T(8,128)(2,1)}, bf16[3136,768]{1,0:T(8,128)(2,1)}, bf16[3136,768]{1,0:T(8,128)(2,1)}) custom-call(bf16[3136,1024]{1,0:T(8,128)(2,1)} %get-tuple-element.507.features, f32[4,1024]{1,0:T(4,128)S(1)} %get-tuple-element.508.bn, bf16[1024,768]{1,0:T(8,128)(2,1)} %get-tuple-element.509.w_patch, f32[1,768]{1,0:T(1,128)} %reshape.878.patch_bias, ...), custom_call_target="tpu_custom_call" | custom-call | flops 23000000512 | tf_op jit(solution)/shard_map/cond/branch_1_fun/pallas_call | solution.py:1120
  210.3 7.8 %conditional.18 = (bf16[512,384]{1,0:T(8,128)(2,1)S(1)}) conditional(s32[]{:T(128)} %convert_element_type.206, (bf16[512,384]{1,0:T(8,128)(2,1)S(1)}, bf16[3136,768]{1,0:T(8,128)(2,1)}) %tuple.129, (bf16[512,384]{1,0:T(8,128)(2,1)S(1)}, bf16[3136,768]{1,0:T(8,128)(2,1)}) %tuple.130), branch_computations={%region_33.34_spmd, %region_34.35_spmd} | conditional | flops 8000000000 | bytes 8 | solution.py:1152
  210.3 7.7 %branch_1_fun.10 = bf16[512,384]{1,0:T(8,128)(2,1)S(1)} custom-call(bf16[512,384]{1,0:T(8,128)(2,1)S(1)} %get-tuple-element.517.queries, bf16[3136,768]{1,0:T(8,128)(2,1)} %get-tuple-element.518.kv), custom_call_target="tpu_custom_call" | custom-call | flops 8000000000 | tf_op jit(solution)/shard_map/cond/branch_1_fun/pallas_call | solution.py:1142
  221.8 6.2 %shard_map.340 = bf16[1024,768]{1,0:T(8,128)(2,1)} custom-call(s32[1,1024]{1,0:T(1,128)} %broadcast_in_dim_reshape.4.arrival, s32[1,512]{1,0:T(1,128)S(1)} %bitcast.269, bf16[1024,384]{1,0:T(8,128)(2,1)} %collective-permute-done.22.slots_a, bf16[1024,384]{1,0:T(8,128)(2,1)} %bitcast.233, f32[512,768]{1,0:T(8,128)} %rows.1), custom_call_target="tpu_custom_call" | custom-call | flops 4000000000 | tf_op jit(solution)/shard_map/pallas_call | solution.py:651
  232.1 6.6 %conditional.19 = (bf16[768,8192]{1,0:T(8,128)(2,1)}, bf16[1024,384]{1,0:T(8,128)(2,1)S(1)}, bf16[1024,384]{1,0:T(8,128)(2,1)S(1)}, bf16[512,384]{1,0:T(8,128)(2...) conditional(s32[]{:T(128)} %convert_element_type.206, ...), branch_computations={%region_35.36_spmd.clone, %region_36.37_spmd.clone} | conditional | flops 28999999488 | bytes 17301642 | solution.py:1243
  232.5 6.1 %broadcast.517 = bf16[768,8192]{1,0:T(8,128)(2,1)} broadcast(bf16[]{:T(256)} %constant.305.clone.1), dimensions={} | broadcast | bytes 12582914 | tf_op jit(solution)/shard_map/broadcast.18
  241.3 48.4 %collective-permute-done.23 = bf16[512,384]{1,0:T(8,128)(2,1)S(1)} collective-permute-done((bf16[512,384]{1,0:T(8,128)(2,1)S(1)}, bf16[512,384]{1,0:T(8,128)(2,1)S(1)}, u32[]{:S(2)}, u32[]{:S(2)}) %collective-permute-start.23) | collective-permute-done | bytes 393248 | tf_op jit(solution)/shard_map/ppermute | solution.py:1138
  290.7 14.9 %all-to-all-start.8 = ((bf16[16,64,384]{2,1,0:T(8,128)(2,1)}), bf16[16,64,384]{2,1,0:T(8,128)(2,1)S(1)}, u32[]{:S(2)}, u32[]{:S(2)}) async-start(bf16[16,64,384]{2,1,0:T(8,128)(2,1)} %bitcast.54), calls=%async_computation.8 | async-start | bytes 1572864 | tf_op jit(solution)/shard_map/all_to_all | solution.py:879
  305.6 16.8 %conditional.20 = ((bf16[512,384]{1,0:T(8,128)(2,1)}, bf16[3136,768]{1,0:T(8,128)(2,1)})) conditional(s32[]{:T(128)} %convert_element_type.206, (bf16[512,384]{1,0:T(8,128)(2,1)S(1)}, bf16[512,384]{1,0:T(8,128)(2,1)S(1)}, bf16[3136,768]{1,0:T(8,128)(2,1)}) %tuple.134, (bf16[512,384]{1,0:T(8,128)(2,1)S(1)}, bf16[512,384]{1,0:T(8,128)(2,1)S(1)}, ...), branch_computations={%region_37.38_spmd, %region_38.39_spmd} | conditional | bytes 8 | solution.py:1271
  305.8 16.6 %branch_1_fun.11 = (bf16[512,384]{1,0:T(8,128)(2,1)}, bf16[3136,768]{1,0:T(8,128)(2,1)}) custom-call(bf16[512,384]{1,0:T(8,128)(2,1)S(1)} %get-tuple-element.554.queries, bf16[512,384]{1,0:T(8,128)(2,1)S(1)} %get-tuple-element.555.grads, bf16[3136,768]{1,0:T(8,128)(2,1)} %get-tuple-element.556.kv), custom_call_target="tpu_custom_call" | custom-call | tf_op jit(solution)/shard_map/cond/branch_1_fun/pallas_call | solution.py:1260
  326.9 5.3 collective-permute-start.25
  335.9 23.0 %conditional.21 = ((bf16[3136,768]{1,0:T(8,128)(2,1)}, bf16[384,1536]{1,0:T(8,128)(2,1)}, bf16[384,1536]{1,0:T(8,128)(2,1)}, f32[1,768]{1,0:T(1,128)})) conditional(s32[]{:T(128)} %convert_element_type.206, () %tuple.137, (bf16[768,1536]{1,0:T(8,128)(2,1)}, bf16[3136,768]{1,0:T(8,128)(2,1)}, bf16[3136,768]{1,0:T(8,128)(2,1)}, ...), branch_computations={%region_39.40_spmd, %region_40.41_spmd} | conditional | flops 23000000512 | bytes 8 | solution.py:1296
  335.9 23.0 %branch_1_fun.12 = (bf16[3136,768]{1,0:T(8,128)(2,1)}, bf16[384,1536]{1,0:T(8,128)(2,1)}, bf16[384,1536]{1,0:T(8,128)(2,1)}, f32[1,768]{1,0:T(1,128)}) custom-call(bf16[768,1536]{1,0:T(8,128)(2,1)} %get-tuple-element.557.k_lo.k_hi.v_lo.v_hi, bf16[768,1536]{1,0:T(8,128)(2,1)} %get-tuple-element.557.k_lo.k_hi.v_lo.v_hi, ...), custom_call_target="tpu_custom_call" | custom-call | flops 23000000512 | tf_op jit(solution)/shard_map/cond/branch_1_fun/pallas_call | solution.py:1284
  358.9 21.7 %conditional.22 = (bf16[1024,768]{1,0:T(8,128)(2,1)}, bf16[640,768]{1,0:T(8,128)(2,1)}, bf16[640,768]{1,0:T(8,128)(2,1)}, bf16[384,3840]{1,0:T(8,128)(2,1)}, bf1...) conditional(s32[]{:T(128)} %convert_element_type.206, ...), branch_computations={%region_41.42_spmd, %region_42.43_spmd} | conditional | bytes 8272 | solution.py:1356
  359.3 21.2 %branch_1_fun.14 = (bf16[3136,512]{1,0:T(8,128)(2,1)}, bf16[3136,512]{1,0:T(8,128)(2,1)}, bf16[1024,768]{1,0:T(8,128)(2,1)S(1)}, f32[2,1024]{1,0:T(2,128)}) custom-call(bf16[3136,1024]{1,0:T(8,128)(2,1)} %get-tuple-element.590.features, f32[4,1024]{1,0:T(4,128)S(1)} %get-tuple-element.591.bn, bf16[1024,768]{1,0:T(8,128)(2,1)S(1)} %get-tuple-element.592.w_patch, ...), custom_call_target="tpu_custom_call" | custom-call | tf_op jit(solution)/shard_map/cond/branch_1_fun/pallas_call | solution.py:1342
  381.9 5.7 %collective-permute-start.28 = (bf16[384,1536]{1,0:T(8,128)(2,1)}, bf16[384,1536]{1,0:T(8,128)(2,1)S(1)}, u32[]{:S(2)}, u32[]{:S(2)}) collective-permute-start(bf16[384,1536]{1,0:T(8,128)(2,1)} %get-tuple-element.811), channel_id=1, source_target_pairs={{0,16},{1,17},{2,18},{3,19},{4,20},{5,21},{6,22},{7,23},{8,24},{9,... | collective-permute-start | bytes 3538952 | tf_op jit(solution)/shard_map/ppermute | solution.py:1424
  400.4 11.2 %collective-permute-start.30 = (bf16[4,2,24,5376]{3,2,0,1:T(8,128)(2,1)}, bf16[4,2,24,5376]{3,2,0,1:T(8,128)(2,1)}, u32[]{:S(2)}, u32[]{:S(2)}) collective-permute-start(bf16[4,2,24,5376]{3,2,0,1:T(8,128)(2,1)} %pad_maximum_fusion.1), channel_id=1, source_target_pairs={{0,2},{1,3},{2,0},{3,1},{4,6},{5,7},{6,4},{7,5},{8,10},{9,11},{10,... | collective-permute-start | bytes 6193160 | tf_op jit(solution)/shard_map/ppermute | solution.py:684
  412.7 5.7 %all-to-all-start.9 = ((bf16[16,40,768]{2,1,0:T(8,128)(2,1)}), bf16[16,40,768]{2,1,0:T(8,128)(2,1)S(1)}, u32[]{:S(2)}, u32[]{:S(2)}) async-start(bf16[16,40,768]{2,1,0:T(8,128)(2,1)} %bitcast.75), calls=%async_computation.9 | async-start | bytes 1966080 | tf_op jit(solution)/shard_map/all_to_all | solution.py:879
  424.3 12.2 %collective-permute-done.33 = f32[11,1024]{1,0:T(8,128)S(1)} collective-permute-done((f32[11,1024]{1,0:T(8,128)S(1)}, f32[11,1024]{1,0:T(8,128)S(1)}, u32[]{:S(2)}, u32[]{:S(2)}) %collective-permute-start.33) | collective-permute-done | bytes 45088 | tf_op jit(solution)/shard_map/ppermute | solution.py:1402
  436.6 5.3 collective-permute-start.34
  447.0 25.1 %collective-permute-done.31 = bf16[2,2,64,768]{3,2,1,0:T(8,128)(2,1)S(1)} collective-permute-done((bf16[2,2,64,768]{3,2,1,0:T(8,128)(2,1)S(1)}, bf16[2,2,64,768]{3,2,1,0:T(8,128)(2,1)S(1)}, u32[]{:S(2)}, u32[]{:S(2)}) %collective-permute-start.31) | collective-permute-done | bytes 393248 | tf_op jit(solution)/shard_map/ppermute | solution.py:684
  485.8 13.9 %conditional.24 = (f32[1000,768]{1,0:T(8,128)S(1)}, f32[1000,768]{1,0:T(8,128)S(1)}, f32[1000,768]{1,0:T(8,128)S(1)}, f32[1000,768]{1,0:T(8,128)}, bf16[1000,768]{1,0:T(8,128)(2,1)}) conditional(s32[]{:T(128)} %convert_element_type.231, (s32[16,40]{1,0:T(8,128)S(1)}, bf16[16,40,768]{2,1,0:T(8,128)(2,1)}, f32[1000,768]{1,0:T(8,128)}, ...), branch_computations={%region_43.44_spmd, %region_44.50_spmd} | conditional | flops 3998031872 | bytes 104014448
  485.9 7.3 %fusion.54 = (bf16[1000,768]{1,0:T(8,128)(2,1)}, f32[1000,768]{1,0:T(8,128)}, f32[1000,768]{1,0:T(8,128)S(1)}, f32[1000,768]{1,0:T(8,128)S(1)}) fusion(f32[1000,768]{1,0:T(8,128)} %get-tuple-element.602, f32[1000,768]{1,0:T(8,128)} %get-tuple-element.600, bf16[640,768]{1,0:T(8,128)(2,1)} %bitcast.214, s32[640]{0:T(1024)S(1)} %eq.152), kind=kOutput, calls=%fused_computation.232 | convolution fusion | flops 989056000 | bytes 17881600 | tf_op jit(solution)/shard_map/cond/branch_0_fun/dot_general | solution.py:38
  499.9 6.3 %collective-permute-start.38 = (bf16[3136,512]{1,0:T(8,128)(2,1)}, bf16[3136,512]{1,0:T(8,128)(2,1)}, u32[]{:S(2)}, u32[]{:S(2)}) collective-permute-start(bf16[3136,512]{1,0:T(8,128)(2,1)} %get-tuple-element.839), channel_id=1, source_target_pairs={{0,16},{1,17},{2,18},{3,19},{4,20},{5,21},{6,22},{7,23},{8,24},{9,... | collective-permute-start | bytes 9633800 | tf_op jit(solution)/shard_map/ppermute | solution.py:1453
  526.9 15.8 %collective-permute-done.43 = bf16[64,768]{1,0:T(8,128)(2,1)S(1)} collective-permute-done((bf16[64,768]{1,0:T(8,128)(2,1)S(1)}, bf16[64,768]{1,0:T(8,128)(2,1)S(1)}, u32[]{:S(2)}, u32[]{:S(2)}) %collective-permute-start.43) | collective-permute-done | bytes 98336 | tf_op jit(solution)/shard_map/ppermute | solution.py:684
  544.1 5.1 all-to-all-done.10
  558.5 5.4 subtract_multiply_fusion
  (455 shorter events, 215.7 us)
Async XLA Ops:
  8.6 49.1 %collective-permute-start.4 = (bf16[24,5376]{1,0:T(8,128)(2,1)S(1)}, bf16[24,5376]{1,0:T(8,128)(2,1)S(1)}, u32[]{:S(2)}, u32[]{:S(2)}) collective-permute-start(bf16[24,5376]{1,0:T(8,128)(2,1)S(1)} %get-tuple-element.1206), channel_id=1, source_target_pairs={{0,12},{1,13},{2,14},{3,15},{4,8},{5,9},{6,10},{7,11},{8,4},{9,5},... | collective-permute-start | bytes 774152 | tf_op jit(solution)/shard_map/ppermute | solution.py:684
  13.7 44.0 %collective-permute-start.3 = (bf16[24,5376]{1,0:T(8,128)(2,1)S(1)}, bf16[24,5376]{1,0:T(8,128)(2,1)S(1)}, u32[]{:S(2)}, u32[]{:S(2)}) collective-permute-start(bf16[24,5376]{1,0:T(8,128)(2,1)S(1)} %get-tuple-element.1206), channel_id=1, source_target_pairs={{0,8},{1,9},{2,10},{3,11},{4,12},{5,13},{6,14},{7,15},{8,0},{9,1},... | collective-permute-start | bytes 774152 | tf_op jit(solution)/shard_map/ppermute | solution.py:684
  13.7 44.0 %collective-permute-start.2 = (bf16[24,5376]{1,0:T(8,128)(2,1)S(1)}, bf16[24,5376]{1,0:T(8,128)(2,1)}, u32[]{:S(2)}, u32[]{:S(2)}) collective-permute-start(bf16[24,5376]{1,0:T(8,128)(2,1)S(1)} %get-tuple-element.1206), channel_id=1, source_target_pairs={{0,4},{1,5},{2,6},{3,7},{4,0},{5,1},{6,2},{7,3},{8,12},{9,13},{10,... | collective-permute-start | bytes 774152 | tf_op jit(solution)/shard_map/ppermute | solution.py:684
  16.0 37.4 %collective-permute-start.5 = (bf16[64,768]{1,0:T(8,128)(2,1)}, bf16[64,768]{1,0:T(8,128)(2,1)}, u32[]{:S(2)}, u32[]{:S(2)}) collective-permute-start(bf16[64,768]{1,0:T(8,128)(2,1)} %slice.202), channel_id=1, source_target_pairs={{0,8},{1,9},{2,10},{3,11},{4,12},{5,13},{6,14},{7,15}} | collective-permute-start | bytes 294920 | tf_op jit(solution)/shard_map/ppermute | solution.py:740
  38.7 12.5 %all-to-all-start.4 = ((s32[16,1,64]{2,1,0:T(1,128)}), s32[16,1,64]{2,1,0:T(1,128)S(1)}, u32[]{:S(2)}, u32[]{:S(2)}) async-start(s32[16,1,64]{2,1,0:T(1,128)} %all_to_all.59), calls=%async_computation.4 | async-start | bytes 16384 | tf_op jit(solution)/shard_map/all_to_all | solution.py:879
  58.8 14.8 %collective-permute-start.7 = (bf16[4,24,5376]{2,1,0:T(8,128)(2,1)S(1)}, bf16[4,24,5376]{2,1,0:T(8,128)(2,1)}, u32[]{:S(2)}, u32[]{:S(2)}) collective-permute-start(bf16[4,24,5376]{2,1,0:T(8,128)(2,1)S(1)} %pad_maximum_fusion.2), channel_id=1, source_target_pairs={{0,1},{1,0},{2,3},{3,2},{4,5},{5,4},{6,7},{7,6},{8,9},{9,8},{10,11... | collective-permute-start | bytes 3096584 | tf_op jit(solution)/shard_map/ppermute | solution.py:684
  68.5 11.7 %all-to-all-start.5 = ((s32[16,1,41]{2,1,0:T(1,128)}), s32[16,1,41]{2,1,0:T(1,128)S(1)}, u32[]{:S(2)}, u32[]{:S(2)}) async-start(s32[16,1,41]{2,1,0:T(1,128)} %bitcast.8), calls=%async_computation.5 | async-start | bytes 16384 | tf_op jit(solution)/shard_map/all_to_all | solution.py:879
  80.3 56.8 %collective-permute-start.12 = (bf16[2,4,24,5376]{3,2,1,0:T(8,128)(2,1)}, bf16[2,4,24,5376]{3,2,1,0:T(8,128)(2,1)}, u32[]{:S(2)}, u32[]{:S(2)}) collective-permute-start(bf16[2,4,24,5376]{3,2,1,0:T(8,128)(2,1)} %pad_maximum_fusion.two), channel_id=1, source_target_pairs={{0,2},{1,3},{2,0},{3,1},{4,6},{5,7},{6,4},{7,5},{8,10},{9,11},{10,... | collective-permute-start | bytes 6193160 | tf_op jit(solution)/shard_map/ppermute | solution.py:684
  84.6 32.2 %all-to-all-start.6 = ((bf16[16,40,768]{2,1,0:T(8,128)(2,1)}), bf16[16,40,768]{2,1,0:T(8,128)(2,1)S(1)}, u32[]{:S(2)}, u32[]{:S(2)}) async-start(bf16[16,40,768]{2,1,0:T(8,128)(2,1)} %bitcast.23), calls=%async_computation.6 | async-start | bytes 1966080 | tf_op jit(solution)/shard_map/all_to_all | solution.py:879
  116.8 20.3 %all-to-all-start.7 = ((bf16[16,64,384]{2,1,0:T(8,128)(2,1)}), bf16[16,64,384]{2,1,0:T(8,128)(2,1)S(1)}, u32[]{:S(2)}, u32[]{:S(2)}) async-start(bf16[16,64,384]{2,1,0:T(8,128)(2,1)} %bitcast.31), calls=%async_computation.7 | async-start | bytes 1572864 | tf_op jit(solution)/shard_map/all_to_all | solution.py:879
  121.0 111.1 %all-gather.2.cloned.1.call-start = ((), (), s32[]{:S(2)}) async-start(), calls=%async_computation.12 | async-start | bytes 12976128 | tf_op jit(solution)/shard_map/all_gather | solution.py:1032
  121.0 16.1 %collective-permute-start.11 = (bf16[640,768]{1,0:T(8,128)(2,1)S(1)}, bf16[640,768]{1,0:T(8,128)(2,1)}, u32[]{:S(2)}, u32[]{:S(2)}) collective-permute-start(bf16[640,768]{1,0:T(8,128)(2,1)S(1)} %bitcast.228), channel_id=1, source_target_pairs={{0,16},{1,17},{2,18},{3,19},{4,20},{5,21},{6,22},{7,23},{8,24},{9,... | collective-permute-start | bytes 2949128 | tf_op jit(solution)/shard_map/ppermute | solution.py:1027
  138.9 15.7 %collective-permute-start.17 = (bf16[2,4,24,1408]{3,2,1,0:T(8,128)(2,1)S(1)}, bf16[2,4,24,1408]{3,2,1,0:T(8,128)(2,1)}, u32[]{:S(2)}, u32[]{:S(2)}) collective-permute-start(bf16[2,4,24,1408]{3,2,1,0:T(8,128)(2,1)S(1)} %pad_maximum_fusion.4.two), channel_id=1, source_target_pairs={{0,16},{16,0},{1,17},{17,1},{2,18},{18,2},{3,19},{19,3},{4,20},{20... | collective-permute-start | bytes 1622024 | tf_op jit(solution)/shard_map/ppermute | solution.py:687
  148.8 17.2 %collective-permute-start.14 = (bf16[2,4,24,5376]{3,2,1,0:T(8,128)(2,1)}, bf16[2,4,24,5376]{3,2,1,0:T(8,128)(2,1)}, u32[]{:S(2)}, u32[]{:S(2)}) collective-permute-start(bf16[2,4,24,5376]{3,2,1,0:T(8,128)(2,1)} %pad_maximum_fusion.two), channel_id=1, source_target_pairs={{0,16},{16,0},{1,17},{17,1},{2,18},{18,2},{3,19},{19,3},{4,20},{20... | collective-permute-start | bytes 6193160 | tf_op jit(solution)/shard_map/ppermute | solution.py:687
  149.3 16.7 %collective-permute-start.15 = (bf16[2,4,24,5376]{3,2,1,0:T(8,128)(2,1)}, bf16[2,4,24,5376]{3,2,1,0:T(8,128)(2,1)}, u32[]{:S(2)}, u32[]{:S(2)}) collective-permute-start(bf16[2,4,24,5376]{3,2,1,0:T(8,128)(2,1)} %collective-permute-done.12.four), channel_id=1, source_target_pairs={{0,16},{16,0},{1,17},{17,1},{2,18},{18,2},{3,19},{19,3},{4,20},{20... | collective-permute-start | bytes 6193160 | tf_op jit(solution)/shard_map/ppermute | solution.py:687
  204.4 17.4 %collective-permute-start.22 = (bf16[1024,384]{1,0:T(8,128)(2,1)S(1)}, bf16[1024,384]{1,0:T(8,128)(2,1)}, u32[]{:S(2)}, u32[]{:S(2)}) collective-permute-start(bf16[1024,384]{1,0:T(8,128)(2,1)S(1)} %bitcast.234), channel_id=1, source_target_pairs={{0,16},{1,17},{2,18},{3,19},{4,20},{5,21},{6,22},{7,23},{8,24},{9,... | collective-permute-start | bytes 2359304 | tf_op jit(solution)/shard_map/ppermute | solution.py:1155
  238.7 51.0 %collective-permute-start.24 = (bf16[1024,384]{1,0:T(8,128)(2,1)S(1)}, bf16[1024,384]{1,0:T(8,128)(2,1)S(1)}, u32[]{:S(2)}, u32[]{:S(2)}) collective-permute-start(bf16[1024,384]{1,0:T(8,128)(2,1)S(1)} %get-tuple-element.789), channel_id=1, source_target_pairs={{16,0},{17,1},{18,2},{19,3},{20,4},{21,5},{22,6},{23,7},{24,8},{25... | collective-permute-start | bytes 2359304 | tf_op jit(solution)/shard_map/ppermute | solution.py:1138
  240.0 49.7 %collective-permute-start.23 = (bf16[512,384]{1,0:T(8,128)(2,1)S(1)}, bf16[512,384]{1,0:T(8,128)(2,1)S(1)}, u32[]{:S(2)}, u32[]{:S(2)}) collective-permute-start(bf16[512,384]{1,0:T(8,128)(2,1)S(1)} %get-tuple-element.787), channel_id=1, source_target_pairs={{16,0},{17,1},{18,2},{19,3},{20,4},{21,5},{22,6},{23,7},{24,8},{25... | collective-permute-start | bytes 1179656 | tf_op jit(solution)/shard_map/ppermute | solution.py:1138
  290.7 34.9 %all-to-all-start.8 = ((bf16[16,64,384]{2,1,0:T(8,128)(2,1)}), bf16[16,64,384]{2,1,0:T(8,128)(2,1)S(1)}, u32[]{:S(2)}, u32[]{:S(2)}) async-start(bf16[16,64,384]{2,1,0:T(8,128)(2,1)} %bitcast.54), calls=%async_computation.8 | async-start | bytes 1572864 | tf_op jit(solution)/shard_map/all_to_all | solution.py:879
  305.6 243.7 %reduce-scatter.2.cloned.1.call-start = ((), (), s32[]{:S(2)}) async-start(), calls=%async_computation.13 | async-start | bytes 12976128 | tf_op jit(solution)/shard_map/reduce_scatter | solution.py:1245
  326.9 32.0 %collective-permute-start.25 = (bf16[512,384]{1,0:T(8,128)(2,1)}, bf16[512,384]{1,0:T(8,128)(2,1)S(1)}, u32[]{:S(2)}, u32[]{:S(2)}) collective-permute-start(bf16[512,384]{1,0:T(8,128)(2,1)} %get-tuple-element.795), channel_id=1, source_target_pairs={{0,16},{1,17},{2,18},{3,19},{4,20},{5,21},{6,22},{7,23},{8,24},{9,... | collective-permute-start | bytes 1179656 | tf_op jit(solution)/shard_map/ppermute | solution.py:1299
  380.6 12.8 %collective-permute-start.27 = (bf16[384,3840]{1,0:T(8,128)(2,1)}, bf16[384,3840]{1,0:T(8,128)(2,1)}, u32[]{:S(2)}, u32[]{:S(2)}) collective-permute-start(bf16[384,3840]{1,0:T(8,128)(2,1)} %get-tuple-element.808), channel_id=1, source_target_pairs={{16,0},{17,1},{18,2},{19,3},{20,4},{21,5},{22,6},{23,7},{24,8},{25... | collective-permute-start | bytes 8847368 | tf_op jit(solution)/shard_map/ppermute | solution.py:1423
  399.0 12.6 %collective-permute-start.32 = (bf16[640,768]{1,0:T(8,128)(2,1)}, bf16[640,768]{1,0:T(8,128)(2,1)S(1)}, u32[]{:S(2)}, u32[]{:S(2)}) collective-permute-start(bf16[640,768]{1,0:T(8,128)(2,1)} %get-tuple-element.827), channel_id=1, source_target_pairs={{16,0},{17,1},{18,2},{19,3},{20,4},{21,5},{22,6},{23,7},{24,8},{25... | collective-permute-start | bytes 2949128 | tf_op jit(solution)/shard_map/ppermute | solution.py:1138
  400.4 71.7 %collective-permute-start.30 = (bf16[4,2,24,5376]{3,2,0,1:T(8,128)(2,1)}, bf16[4,2,24,5376]{3,2,0,1:T(8,128)(2,1)}, u32[]{:S(2)}, u32[]{:S(2)}) collective-permute-start(bf16[4,2,24,5376]{3,2,0,1:T(8,128)(2,1)} %pad_maximum_fusion.1), channel_id=1, source_target_pairs={{0,2},{1,3},{2,0},{3,1},{4,6},{5,7},{6,4},{7,5},{8,10},{9,11},{10,... | collective-permute-start | bytes 6193160 | tf_op jit(solution)/shard_map/ppermute | solution.py:684
  412.7 59.5 %all-to-all-start.9 = ((bf16[16,40,768]{2,1,0:T(8,128)(2,1)}), bf16[16,40,768]{2,1,0:T(8,128)(2,1)S(1)}, u32[]{:S(2)}, u32[]{:S(2)}) async-start(bf16[16,40,768]{2,1,0:T(8,128)(2,1)} %bitcast.75), calls=%async_computation.9 | async-start | bytes 1966080 | tf_op jit(solution)/shard_map/all_to_all | solution.py:879
  419.6 52.5 %collective-permute-start.31 = (bf16[2,2,64,768]{3,2,1,0:T(8,128)(2,1)S(1)}, bf16[2,2,64,768]{3,2,1,0:T(8,128)(2,1)S(1)}, u32[]{:S(2)}, u32[]{:S(2)}) collective-permute-start(bf16[2,2,64,768]{3,2,1,0:T(8,128)(2,1)S(1)} %bitcast_select_fusion.1), channel_id=1, source_target_pairs={{0,2},{1,3},{2,0},{3,1},{4,6},{5,7},{6,4},{7,5},{8,10},{9,11},{10,... | collective-permute-start | bytes 1179656 | tf_op jit(solution)/shard_map/ppermute | solution.py:684
  421.6 14.9 %collective-permute-start.33 = (f32[11,1024]{1,0:T(8,128)S(1)}, f32[11,1024]{1,0:T(8,128)S(1)}, u32[]{:S(2)}, u32[]{:S(2)}) collective-permute-start(f32[11,1024]{1,0:T(8,128)S(1)} %reshape.947), channel_id=1, source_target_pairs={{0,4},{1,5},{2,6},{3,7},{4,0},{5,1},{6,2},{7,3},{8,12},{9,13},{10,... | collective-permute-start | bytes 135176 | tf_op jit(solution)/shard_map/ppermute | solution.py:1402
  475.2 24.5 %collective-permute-start.35 = (bf16[4,24,5376]{2,1,0:T(8,128)(2,1)}, bf16[4,24,5376]{2,1,0:T(8,128)(2,1)}, u32[]{:S(2)}, u32[]{:S(2)}) collective-permute-start(bf16[4,24,5376]{2,1,0:T(8,128)(2,1)} %fusion.29), channel_id=1, source_target_pairs={{0,1},{1,0},{2,3},{3,2},{4,5},{5,4},{6,7},{7,6},{8,9},{9,8},{10,11... | collective-permute-start | bytes 3096584 | tf_op jit(solution)/shard_map/ppermute | solution.py:684
  481.9 17.8 %collective-permute-start.36 = (bf16[2,64,768]{2,1,0:T(8,128)(2,1)}, bf16[2,64,768]{2,1,0:T(8,128)(2,1)}, u32[]{:S(2)}, u32[]{:S(2)}) collective-permute-start(bf16[2,64,768]{2,1,0:T(8,128)(2,1)} %fusion.37), channel_id=1, source_target_pairs={{0,1},{1,0},{2,3},{3,2},{4,5},{5,4},{6,7},{7,6},{8,9},{9,8},{10,11... | collective-permute-start | bytes 589832 | tf_op jit(solution)/shard_map/ppermute | solution.py:684
  499.9 58.6 %collective-permute-start.38 = (bf16[3136,512]{1,0:T(8,128)(2,1)}, bf16[3136,512]{1,0:T(8,128)(2,1)}, u32[]{:S(2)}, u32[]{:S(2)}) collective-permute-start(bf16[3136,512]{1,0:T(8,128)(2,1)} %get-tuple-element.839), channel_id=1, source_target_pairs={{0,16},{1,17},{2,18},{3,19},{4,20},{5,21},{6,22},{7,23},{8,24},{9,... | collective-permute-start | bytes 9633800 | tf_op jit(solution)/shard_map/ppermute | solution.py:1453
  520.0 29.3 %all-to-all-start.10 = ((bf16[4,24,5376]{2,1,0:T(8,128)(2,1)}), bf16[4,24,5376]{2,1,0:T(8,128)(2,1)S(1)}, u32[]{:S(2)}, u32[]{:S(2)}) async-start(bf16[4,24,5376]{2,1,0:T(8,128)(2,1)} %fusion.25), calls=%async_computation.10 | async-start | bytes 2064384 | tf_op jit(solution)/shard_map/all_to_all | solution.py:785
  524.3 18.4 %collective-permute-start.43 = (bf16[64,768]{1,0:T(8,128)(2,1)S(1)}, bf16[64,768]{1,0:T(8,128)(2,1)S(1)}, u32[]{:S(2)}, u32[]{:S(2)}) collective-permute-start(bf16[64,768]{1,0:T(8,128)(2,1)S(1)} %dynamic-slice_bitcast_fusion.8), channel_id=1, source_target_pairs={{0,4},{1,5},{2,6},{3,7},{4,0},{5,1},{6,2},{7,3},{8,12},{9,13},{10,... | collective-permute-start | bytes 294920 | tf_op jit(solution)/shard_map/ppermute | solution.py:684
  (112 other events, 1544.7 us)
Sparse Core Ops, SparseCore 0:
  137.3 94.6 all-gather.1
  327.0 178.2 reduce-scatter.1
